TPU v7x, 32 devices: a whole 2x2x4 slice. The times are simulated.
32 devices in a mesh: dp: 8 (over z, x), rep: 4 (over y, core).
Axes of the slice: x: 2, y: 2, z: 4, core: 2. Of those that a mesh axis runs over, the one named last changes fastest.
Arguments:
- deter_states: bfloat16 [64, 64, 1024], P(('dp', 'rep')), may hold values from -6 to 6
- embed: bfloat16 [64, 64, 1536], P(('dp', 'rep')), may hold values from -6 to 6
- lengths: int32 [64], P(('dp', 'rep')), may hold values from 8 to 64, as said below
- resets: int32 [64, 64], P(('dp', 'rep')), may hold values 0 or 1
- terminal: int32 [64, 64], P(('dp', 'rep')), may hold values 0 or 1
- rewards: float32 [64, 64], P(('dp', 'rep')), may hold values from -6 to 6
- prev_stoch: int32 [64, 64, 32], P(('dp', 'rep')), may hold values from 0 to 31
- prev_action: int32 [64, 64], P(('dp', 'rep')), may hold values from 0 to 16
- regroup: int32 [32, 128], P(('dp', 'rep')), may hold values from 0 to 127, each once within a row
- goal_codes: int32 [4096, 8], P(('dp', 'rep')), may hold values from 0 to 7
- samples: int32 [4096, 16, 32], P(('dp', 'rep')), may hold values from 0 to 31
- actions: int32 [4096, 16], P(('dp', 'rep')), may hold values from 0 to 16
- obs_gain: bfloat16 [1024], P('rep'), may hold values from 0.5 to 1.5
- manager_in: bfloat16 [1024, 512], P('rep'), may hold values from -0.1875 to 0.1875
- manager_gain: bfloat16 [512], P('rep'), may hold values from 0.5 to 1.5
- manager_out: bfloat16 [512], P('rep'), may hold values from -0.25 to 0.25
- goal_in: bfloat16 [64, 512], P('rep'), may hold values from -2 to 2
- goal_gain: bfloat16 [512], P('rep'), may hold values from 0.5 to 1.5
- goal_out: bfloat16 [512, 1024], P('rep'), may hold values from -0.25 to 0.25
- actor_in: bfloat16 [3072, 512], P('rep'), may hold values from -0.125 to 0.125
- actor_gain: bfloat16 [512], P('rep'), may hold values from 0.5 to 1.5
- actor_out: bfloat16 [512, 17], P('rep'), may hold values from -0.25 to 0.25
- critic_in: bfloat16 [3072, 512], P('rep'), may hold values from -0.125 to 0.125
- critic_gain: bfloat16 [512], P('rep'), may hold values from 0.5 to 1.5
- critic_out: bfloat16 [512], P('rep'), may hold values from -0.25 to 0.25
- img_stoch: bfloat16 [1024, 1024], P('rep'), may hold values from -1 to 1
- img_action: bfloat16 [17, 1024], P(None, 'rep'), may hold values from -6 to 6
- img_gain: bfloat16 [1024], P('rep'), may hold values from 0.5 to 1.5
- gru_weight: bfloat16 [2048, 3072], P('rep'), may hold values from -0.125 to 0.125
- gru_gain: bfloat16 [3072], P('rep'), may hold values from 0.5 to 1.5
- post_in: bfloat16 [2560, 1024], P('rep'), may hold values from -0.125 to 0.125
- post_gain: bfloat16 [1024], P('rep'), may hold values from 0.5 to 1.5
- post_out: bfloat16 [1024, 1024], P('rep'), may hold values from -0.1875 to 0.1875
- prior_in: bfloat16 [1024, 1024], P('rep'), may hold values from -0.1875 to 0.1875
- prior_gain: bfloat16 [1024], P('rep'), may hold values from 0.5 to 1.5
- prior_out: bfloat16 [1024, 1024], P('rep'), may hold values from -0.1875 to 0.1875
- enc_in: bfloat16 [1024, 512], P('rep'), may hold values from -0.1875 to 0.1875
- enc_gain: bfloat16 [512], P('rep'), may hold values from 0.5 to 1.5
- enc_out: bfloat16 [512, 64], P('rep'), may hold values from -0.25 to 0.25
Outputs:
- total_loss: float32 [], replicated
- deter_grad: float32 [64, 64, 1024], P(('dp', 'rep'))
- embed_grad: float32 [64, 64, 1536], P(('dp', 'rep'))
- obs_gain_grad: float32 [1024], P('rep')
- manager_in_grad: float32 [1024, 512], P('rep', 'dp')
- manager_gain_grad: float32 [512], P('rep')
- manager_out_grad: float32 [512], P('rep')
- goal_in_grad: float32 [64, 512], P('rep', 'dp')
- goal_gain_grad: float32 [512], P('rep')
- goal_out_grad: float32 [512, 1024], P('rep', 'dp')
- actor_in_grad: float32 [3072, 512], P('rep', 'dp')
- actor_gain_grad: float32 [512], P('rep')
- actor_out_grad: float32 [512, 17], P('rep')
- critic_in_grad: float32 [3072, 512], P('rep', 'dp')
- critic_gain_grad: float32 [512], P('rep')
- critic_out_grad: float32 [512], P('rep')
- img_stoch_grad: float32 [1024, 1024], P('rep', 'dp')
- img_action_grad: float32 [17, 1024], P(None, 'rep')
- img_gain_grad: float32 [1024], P('rep')
- gru_weight_grad: float32 [2048, 3072], P('rep', 'dp')
- gru_gain_grad: float32 [3072], P('rep')
- post_in_grad: float32 [2560, 1024], P('rep', 'dp')
- post_gain_grad: float32 [1024], P('rep')
- post_out_grad: float32 [1024, 1024], P('rep', 'dp')
- prior_in_grad: float32 [1024, 1024], P('rep', 'dp')
- prior_gain_grad: float32 [1024], P('rep')
- prior_out_grad: float32 [1024, 1024], P('rep', 'dp')
- enc_in_grad: float32 [1024, 512], P('rep', 'dp')
- enc_gain_grad: float32 [512], P('rep')
- enc_out_grad: float32 [512, 64], P('rep')
Inputs may be any that keep to these rules, and one draw needn't show every extreme that they name: `lengths`: in the 2 sequences of every device one has exactly 64 frames. `regroup`: each row is a permutation of 0 to 127.
All inputs are finite; a program needn't handle non-finite values. Where the computation divides by a largest or mean magnitude, that divisor is 1e-20 or more. No bound on the sum of `resets` or of `terminal` on one device may be relied on, other than what follows from the above.
Results may differ from a plain program's by a relative error of at most 0.01.
The roundings to bfloat16 on the way count: a program that leaves them out, or rounds other values in their place, can miss the bound.
Values may be sent and summed in bfloat16 or wider, within the bound.
A program may use at most 320 MiB of HBM per device.

v0:
```python
import math

import jax
import jax.numpy as jnp
from jax import lax
from jax.sharding import PartitionSpec as P

H = 1024
ZG = 32
ZK = 32
U = 512
GC = 8
GK = 8
NA = 17
E = 1536
LEN = 64
HOR = 16
SEQ_DEV = 2
Z = 1024
GCODE = 64
ROWS = 128


discount = 0.99
return_mix = 0.95
epsilon = 1e-05
small_floor = 1e-06
highest = lax.Precision.HIGHEST


def product(left, right):
    return jnp.dot(left, right, preferred_element_type=jnp.float32)


def normalize(values_in):
    row_mean = jnp.mean(values_in, -1, keepdims=True)
    centred = values_in - row_mean
    inverse = lax.rsqrt(jnp.mean(centred * centred, -1, keepdims=True) + epsilon)
    return (centred * inverse, inverse)


def normalize_back(grad_normed, normed, inverse):
    return inverse * (
        grad_normed
        - jnp.mean(grad_normed, -1, keepdims=True)
        - normed * jnp.mean(grad_normed * normed, -1, keepdims=True)
    )


def hidden_forward(pre_act, scaling):
    normed, inverse = normalize(pre_act)
    scaled = normed * scaling
    return ((normed, inverse, scaled), jax.nn.elu(scaled).astype(jnp.bfloat16))


def hidden_backward(grad_hidden, cache, scaling):
    normed, inverse, scaled = cache
    grad_scaled = grad_hidden * jnp.where(scaled > 0, 1.0, jnp.exp(jnp.minimum(scaled, 0.0)))
    grad_gain = jnp.sum(grad_scaled * normed, tuple(range(scaled.ndim - 1)))
    return (normalize_back(grad_scaled * scaling, normed, inverse).astype(jnp.bfloat16), grad_gain)


def input_backward(grad_pre, input_low, weight):
    grad_weight = jnp.einsum("nk,nu->ku", input_low, grad_pre, preferred_element_type=jnp.float32)
    to_input = jnp.einsum("nu,ku->nk", grad_pre, weight, preferred_element_type=jnp.float32)
    return (grad_weight, to_input)


def head_backward(grad_head, hidden_low, head, cache, scaling):
    grad_weight = jnp.einsum("nu,nk->uk", hidden_low, grad_head, preferred_element_type=jnp.float32)
    grad_hidden = jnp.einsum("nk,uk->nu", grad_head, head, preferred_element_type=jnp.float32)
    grad_pre, grad_gain = hidden_backward(grad_hidden, cache, scaling)
    return (grad_weight, grad_pre, grad_gain)


def group_softmax(flat_logits, groups):
    log_part = jax.nn.log_softmax(flat_logits.reshape(flat_logits.shape[0], groups, -1), axis=-1)
    return (log_part, jnp.exp(log_part))


def chain_returns(values_now, rewards_now, linked, carried):

    def back_step(carry_pair, inputs):
        later_return, later_value = carry_pair
        current, reward_now, link_now, carry_now = inputs
        blended = (1.0 - return_mix) * later_value + return_mix * later_return
        result = jnp.where(link_now, reward_now + discount * carry_now * blended, current)
        return ((result, current), result)

    zero_start = jnp.zeros(values_now.shape[:1], jnp.float32)
    _, stacked = lax.scan(
        back_step,
        (zero_start, zero_start),
        (values_now.T, rewards_now.T, linked.T, carried.T),
        reverse=True,
    )
    return stacked.T


def worker_forward(start_state, goal_low, stoch_hot, first_layer, scaling):
    slot_part = product(start_state, first_layer[:H]) + product(goal_low, first_layer[H + Z :])
    varying = product(stoch_hot, first_layer[H : H + Z]).reshape(start_state.shape[0], HOR, U)
    return hidden_forward(slot_part[:, None, :] + varying, scaling)


def worker_backward(grad_pre, start_state, goal_low, stoch_hot, first_layer):
    slot_count = grad_pre.shape[0]
    grad_stoch = jnp.einsum(
        "nz,nu->zu",
        stoch_hot,
        grad_pre.reshape(slot_count * HOR, U),
        preferred_element_type=jnp.float32,
    )
    summed = jnp.sum(grad_pre, 1, dtype=jnp.float32).astype(jnp.bfloat16)
    grad_state_rows, to_state = input_backward(summed, start_state, first_layer[:H])
    grad_goal_rows, to_goal = input_backward(summed, goal_low, first_layer[H + Z :])
    return (jnp.concatenate([grad_state_rows, grad_stoch, grad_goal_rows], 0), to_state, to_goal)


def per_device(
    deter_states,
    embed,
    lengths,
    resets,
    terminal,
    rewards,
    prev_stoch,
    prev_action,
    regroup,
    goal_codes,
    samples,
    actions,
    obs_gain,
    manager_in,
    manager_gain,
    manager_out,
    goal_in,
    goal_gain,
    goal_out,
    actor_in,
    actor_gain,
    actor_out,
    critic_in,
    critic_gain,
    critic_out,
    img_stoch,
    img_action,
    img_gain,
    gru_weight,
    gru_gain,
    post_in,
    post_gain,
    post_out,
    prior_in,
    prior_gain,
    prior_out,
    enc_in,
    enc_gain,
    enc_out,
):
    (
        obs_gain,
        manager_in,
        manager_gain,
        manager_out,
        goal_in,
        goal_gain,
        goal_out,
        actor_in,
        actor_gain,
        actor_out,
        critic_in,
        critic_gain,
        critic_out,
        img_stoch,
        img_action,
        img_gain,
        gru_weight,
        gru_gain,
        post_in,
        post_gain,
        post_out,
        prior_in,
        prior_gain,
        prior_out,
        enc_in,
        enc_gain,
        enc_out,
    ) = (
        lax.all_gather(obs_gain, "rep", axis=0, tiled=True),
        lax.all_gather(manager_in, "rep", axis=0, tiled=True),
        lax.all_gather(manager_gain, "rep", axis=0, tiled=True),
        lax.all_gather(manager_out, "rep", axis=0, tiled=True),
        lax.all_gather(goal_in, "rep", axis=0, tiled=True),
        lax.all_gather(goal_gain, "rep", axis=0, tiled=True),
        lax.all_gather(goal_out, "rep", axis=0, tiled=True),
        lax.all_gather(actor_in, "rep", axis=0, tiled=True),
        lax.all_gather(actor_gain, "rep", axis=0, tiled=True),
        lax.all_gather(actor_out, "rep", axis=0, tiled=True),
        lax.all_gather(critic_in, "rep", axis=0, tiled=True),
        lax.all_gather(critic_gain, "rep", axis=0, tiled=True),
        lax.all_gather(critic_out, "rep", axis=0, tiled=True),
        lax.all_gather(img_stoch, "rep", axis=0, tiled=True),
        lax.all_gather(img_action, "rep", axis=1, tiled=True),
        lax.all_gather(img_gain, "rep", axis=0, tiled=True),
        lax.all_gather(gru_weight, "rep", axis=0, tiled=True),
        lax.all_gather(gru_gain, "rep", axis=0, tiled=True),
        lax.all_gather(post_in, "rep", axis=0, tiled=True),
        lax.all_gather(post_gain, "rep", axis=0, tiled=True),
        lax.all_gather(post_out, "rep", axis=0, tiled=True),
        lax.all_gather(prior_in, "rep", axis=0, tiled=True),
        lax.all_gather(prior_gain, "rep", axis=0, tiled=True),
        lax.all_gather(prior_out, "rep", axis=0, tiled=True),
        lax.all_gather(enc_in, "rep", axis=0, tiled=True),
        lax.all_gather(enc_gain, "rep", axis=0, tiled=True),
        lax.all_gather(enc_out, "rep", axis=0, tiled=True),
    )
    prev_low = deter_states.reshape(ROWS, H)
    prev_float = prev_low.astype(jnp.float32)
    embed_low = embed.reshape(ROWS, E)
    positions = lax.broadcasted_iota(jnp.int32, (SEQ_DEV, LEN), 1)
    is_valid = positions < lengths[:, None]
    next_valid = jnp.concatenate([is_valid[:, 1:], jnp.zeros((SEQ_DEV, 1), jnp.bool_)], 1)
    next_reset = jnp.concatenate([resets[:, 1:], jnp.ones((SEQ_DEV, 1), jnp.int32)], 1)
    linked = next_valid & (next_reset == 0)
    carried = 1.0 - terminal.astype(jnp.float32)
    valid_rows = is_valid.astype(jnp.float32).reshape(ROWS)
    frame_scale = valid_rows / ROWS
    stoch_prev_hot = (
        (prev_stoch[..., None] == lax.broadcasted_iota(jnp.int32, (1, 1, 1, ZK), 3))
        .astype(jnp.bfloat16)
        .reshape(ROWS, Z)
    )
    action_prev_hot = (
        prev_action.reshape(ROWS)[:, None] == lax.broadcasted_iota(jnp.int32, (1, NA), 1)
    ).astype(jnp.bfloat16)
    img_cache, img_hidden = hidden_forward(
        product(stoch_prev_hot, img_stoch) + product(action_prev_hot, img_action), img_gain
    )
    gru_input = jnp.concatenate([img_hidden, prev_low], 1)
    gru_normed, gru_inverse = normalize(product(gru_input, gru_weight))
    gru_parts = gru_normed * gru_gain
    reset_gate = jax.nn.sigmoid(gru_parts[:, :H])
    candidate_in = gru_parts[:, H : 2 * H]
    candidate = jnp.tanh(reset_gate * candidate_in)
    update_gate = jax.nn.sigmoid(gru_parts[:, 2 * H :] - 1.0)
    deter_state = update_gate * candidate + (1.0 - update_gate) * prev_float
    deter_low = deter_state.astype(jnp.bfloat16)
    obs_normed, obs_inverse = normalize(deter_state)
    feature = (obs_normed * obs_gain).astype(jnp.bfloat16)
    man_cache, man_hidden = hidden_forward(product(feature, manager_in), manager_gain)
    manager_value = product(man_hidden, manager_out).reshape(SEQ_DEV, LEN)
    manager_return = chain_returns(manager_value, rewards, linked, carried)
    manager_misfit = (manager_value - manager_return).reshape(ROWS)
    post_input = jnp.concatenate([deter_low, embed_low], 1)
    post_cache, post_hidden = hidden_forward(product(post_input, post_in), post_gain)
    post_log, post_prob = group_softmax(product(post_hidden, post_out), ZG)
    prior_cache, prior_hidden = hidden_forward(product(deter_low, prior_in), prior_gain)
    prior_log, prior_prob = group_softmax(product(prior_hidden, prior_out), ZG)
    log_gap = post_log - prior_log
    group_kl = jnp.sum(post_prob * log_gap, -1, keepdims=True)
    enc_cache, enc_hidden = hidden_forward(product(deter_low, enc_in), enc_gain)
    code_log, code_prob = group_softmax(product(enc_hidden, enc_out), GC)
    code_kl = jnp.sum(code_prob * (code_log + math.log(GK)), (1, 2))
    code_spread = jnp.sum(code_prob * code_log, -1, keepdims=True)
    soft_code = code_prob.reshape(ROWS, GCODE).astype(jnp.bfloat16)
    dec_cache, dec_hidden = hidden_forward(product(soft_code, goal_in), goal_gain)
    recon_err = product(dec_hidden, goal_out) - deter_state
    frame_terms = (
        jnp.sum(post_prob * log_gap, (1, 2)) + code_kl + 0.5 * jnp.mean(recon_err * recon_err, -1)
    )
    frame_loss = jnp.sum(valid_rows * (0.5 * manager_misfit * manager_misfit + frame_terms)) / ROWS
    send_order = regroup[0]
    start_state, slot_flag = (
        lax.all_to_all(deter_low[send_order], "dp", split_axis=0, concat_axis=0, tiled=True),
        lax.all_to_all(
            valid_rows[send_order].astype(jnp.bfloat16),
            "dp",
            split_axis=0,
            concat_axis=0,
            tiled=True,
        ),
    )
    slot_weight = slot_flag.astype(jnp.float32)
    code_hot = (
        (goal_codes[:, :, None] == lax.broadcasted_iota(jnp.int32, (1, 1, GK), 2))
        .astype(jnp.bfloat16)
        .reshape(ROWS, GCODE)
    )
    goal_cache, goal_hidden = hidden_forward(product(code_hot, goal_in), goal_gain)
    goal_vector = product(goal_hidden, goal_out)
    goal_low = goal_vector.astype(jnp.bfloat16)
    state_float = start_state.astype(jnp.float32)
    alignment = jnp.sum(goal_vector * state_float, -1)
    largest_square = (
        jnp.maximum(jnp.sum(goal_vector * goal_vector, -1), jnp.sum(state_float * state_float, -1))
        + small_floor
    )
    reward_slot = alignment / largest_square
    stoch_hot = (
        (samples[..., None] == lax.broadcasted_iota(jnp.int32, (1, 1, 1, ZK), 3))
        .astype(jnp.bfloat16)
        .reshape(ROWS * HOR, Z)
    )
    action_hot = (actions[..., None] == lax.broadcasted_iota(jnp.int32, (1, 1, NA), 2)).astype(
        jnp.float32
    )
    actor_cache, actor_hidden = worker_forward(
        start_state, goal_low, stoch_hot, actor_in, actor_gain
    )
    logits = jnp.einsum("rku,ua->rka", actor_hidden, actor_out, preferred_element_type=jnp.float32)
    log_chance = jax.nn.log_softmax(logits, axis=-1)
    chosen = jnp.sum(log_chance * action_hot, -1)
    critic_cache, critic_hidden = worker_forward(
        start_state, goal_low, stoch_hot, critic_in, critic_gain
    )
    worker_value = jnp.einsum(
        "rku,u->rk", critic_hidden, critic_out, preferred_element_type=jnp.float32
    )
    step_link = lax.broadcasted_iota(jnp.int32, (ROWS, HOR), 1) < HOR - 1
    worker_return = chain_returns(
        worker_value,
        jnp.broadcast_to(reward_slot[:, None], (ROWS, HOR)),
        step_link,
        jnp.ones((ROWS, HOR), jnp.float32),
    )
    advantage = worker_return - worker_value
    local_top = jnp.max(slot_weight[:, None] * jnp.abs(advantage))
    return_scale = lax.pmax(local_top, ("dp", "rep")) + small_floor
    step_total = ROWS * HOR
    value_misfit = worker_value - worker_return
    critic_part = 0.5 * jnp.sum(slot_weight[:, None] * value_misfit * value_misfit)
    actor_part = jnp.sum(slot_weight[:, None] * chosen * advantage) / return_scale
    local_loss = frame_loss + (critic_part - actor_part) / step_total
    grad_value = slot_weight[:, None] * value_misfit / step_total
    grad_chosen = -slot_weight[:, None] * advantage / return_scale / step_total
    grad_logits = (grad_chosen[..., None] * (action_hot - jnp.exp(log_chance))).astype(jnp.bfloat16)
    grad_actor_out = jnp.einsum(
        "rku,rka->ua", actor_hidden, grad_logits, preferred_element_type=jnp.float32
    )
    grad_actor_hidden = jnp.einsum(
        "rka,ua->rku", grad_logits, actor_out, preferred_element_type=jnp.float32
    )
    actor_pre, grad_actor_gain = hidden_backward(grad_actor_hidden, actor_cache, actor_gain)
    grad_critic_out = jnp.einsum("rku,rk->u", critic_hidden, grad_value, precision=highest)
    critic_pre, grad_critic_gain = hidden_backward(
        grad_value[..., None] * critic_out, critic_cache, critic_gain
    )
    grad_actor_in, actor_to_state, actor_to_goal = worker_backward(
        actor_pre, start_state, goal_low, stoch_hot, actor_in
    )
    grad_critic_in, critic_to_state, critic_to_goal = worker_backward(
        critic_pre, start_state, goal_low, stoch_hot, critic_in
    )
    grad_goal_low = (actor_to_goal + critic_to_goal).astype(jnp.bfloat16)
    worker_goal_out, goal_pre, worker_goal_gain = head_backward(
        grad_goal_low, goal_hidden, goal_out, goal_cache, goal_gain
    )
    worker_goal_in = jnp.einsum("ng,nu->gu", code_hot, goal_pre, preferred_element_type=jnp.float32)
    returned = lax.all_to_all(
        (actor_to_state + critic_to_state).astype(jnp.bfloat16),
        "dp",
        split_axis=0,
        concat_axis=0,
        tiled=True,
    )
    grad_manager_value = frame_scale * manager_misfit
    grad_manager_out = jnp.dot(grad_manager_value, man_hidden, precision=highest)
    manager_pre, grad_manager_gain = hidden_backward(
        grad_manager_value[:, None] * manager_out, man_cache, manager_gain
    )
    grad_manager_in, grad_feature = input_backward(manager_pre, feature, manager_in)
    grad_obs_gain = jnp.sum(grad_feature * obs_normed, 0)
    obs_back = normalize_back(grad_feature * obs_gain, obs_normed, obs_inverse)
    weight_cube = frame_scale[:, None, None]
    post_grad_logits = (
        (weight_cube * post_prob * (log_gap - group_kl)).reshape(ROWS, Z).astype(jnp.bfloat16)
    )
    prior_grad_logits = (
        (weight_cube * (prior_prob - post_prob)).reshape(ROWS, Z).astype(jnp.bfloat16)
    )
    grad_post_out, post_pre, grad_post_gain = head_backward(
        post_grad_logits, post_hidden, post_out, post_cache, post_gain
    )
    grad_post_in, post_back = input_backward(post_pre, post_input, post_in)
    grad_prior_out, prior_pre, grad_prior_gain = head_backward(
        prior_grad_logits, prior_hidden, prior_out, prior_cache, prior_gain
    )
    grad_prior_in, prior_back = input_backward(prior_pre, deter_low, prior_in)
    recon_grad = frame_scale[:, None] * recon_err / H
    dec_goal_out, dec_pre, dec_goal_gain = head_backward(
        recon_grad.astype(jnp.bfloat16), dec_hidden, goal_out, dec_cache, goal_gain
    )
    dec_goal_in, grad_code = input_backward(dec_pre, soft_code, goal_in)
    grad_code = grad_code.reshape(ROWS, GC, GK)
    code_grad_logits = code_prob * (
        grad_code - jnp.sum(code_prob * grad_code, -1, keepdims=True)
    ) + weight_cube * code_prob * (code_log - code_spread)
    grad_enc_out, enc_pre, grad_enc_gain = head_backward(
        code_grad_logits.reshape(ROWS, GCODE).astype(jnp.bfloat16),
        enc_hidden,
        enc_out,
        enc_cache,
        enc_gain,
    )
    grad_enc_in, enc_back = input_backward(enc_pre, deter_low, enc_in)
    grad_goal_out = worker_goal_out + dec_goal_out
    grad_goal_in = worker_goal_in + dec_goal_in
    grad_goal_gain = worker_goal_gain + dec_goal_gain
    scattered = jnp.zeros((ROWS, H), jnp.float32).at[send_order].add(returned.astype(jnp.float32))
    grad_deter = obs_back + post_back[:, :H] + prior_back + enc_back + scattered - recon_grad
    grad_inner = grad_deter * update_gate * (1.0 - candidate * candidate)
    grad_parts = jnp.concatenate(
        [
            grad_inner * candidate_in * reset_gate * (1.0 - reset_gate),
            grad_inner * reset_gate,
            grad_deter * (candidate - prev_float) * update_gate * (1.0 - update_gate),
        ],
        1,
    )
    grad_gru_gain = jnp.sum(grad_parts * gru_normed, 0)
    gru_pre = normalize_back(grad_parts * gru_gain, gru_normed, gru_inverse).astype(jnp.bfloat16)
    grad_gru_weight, gru_back = input_backward(gru_pre, gru_input, gru_weight)
    img_pre, grad_img_gain = hidden_backward(gru_back[:, :H], img_cache, img_gain)
    grad_img_stoch = jnp.einsum(
        "nz,nh->zh", stoch_prev_hot, img_pre, preferred_element_type=jnp.float32
    )
    grad_img_action = jnp.einsum(
        "na,nh->ah", action_prev_hot, img_pre, preferred_element_type=jnp.float32
    )
    grad_prev = grad_deter * (1.0 - update_gate) + gru_back[:, H:]
    embed_grad = post_back[:, H:]
    rep_count = lax.axis_size("rep")
    (
        loss_vector,
        grad_obs_gain,
        grad_manager_in,
        grad_manager_gain,
        grad_manager_out,
        grad_goal_in,
        grad_goal_gain,
        grad_goal_out,
        grad_actor_in,
        grad_actor_gain,
        grad_actor_out,
        grad_critic_in,
        grad_critic_gain,
        grad_critic_out,
        grad_img_stoch,
        grad_img_action,
        grad_img_gain,
        grad_gru_weight,
        grad_gru_gain,
        grad_post_in,
        grad_post_gain,
        grad_post_out,
        grad_prior_in,
        grad_prior_gain,
        grad_prior_out,
        grad_enc_in,
        grad_enc_gain,
        grad_enc_out,
    ) = (
        lax.psum_scatter(
            jnp.full((rep_count,), local_loss), "rep", scatter_dimension=0, tiled=True
        ),
        lax.psum_scatter(grad_obs_gain, "rep", scatter_dimension=0, tiled=True),
        lax.psum_scatter(grad_manager_in, "rep", scatter_dimension=0, tiled=True),
        lax.psum_scatter(grad_manager_gain, "rep", scatter_dimension=0, tiled=True),
        lax.psum_scatter(grad_manager_out, "rep", scatter_dimension=0, tiled=True),
        lax.psum_scatter(grad_goal_in, "rep", scatter_dimension=0, tiled=True),
        lax.psum_scatter(grad_goal_gain, "rep", scatter_dimension=0, tiled=True),
        lax.psum_scatter(grad_goal_out, "rep", scatter_dimension=0, tiled=True),
        lax.psum_scatter(grad_actor_in, "rep", scatter_dimension=0, tiled=True),
        lax.psum_scatter(grad_actor_gain, "rep", scatter_dimension=0, tiled=True),
        lax.psum_scatter(grad_actor_out, "rep", scatter_dimension=0, tiled=True),
        lax.psum_scatter(grad_critic_in, "rep", scatter_dimension=0, tiled=True),
        lax.psum_scatter(grad_critic_gain, "rep", scatter_dimension=0, tiled=True),
        lax.psum_scatter(grad_critic_out, "rep", scatter_dimension=0, tiled=True),
        lax.psum_scatter(grad_img_stoch, "rep", scatter_dimension=0, tiled=True),
        lax.psum_scatter(grad_img_action, "rep", scatter_dimension=1, tiled=True),
        lax.psum_scatter(grad_img_gain, "rep", scatter_dimension=0, tiled=True),
        lax.psum_scatter(grad_gru_weight, "rep", scatter_dimension=0, tiled=True),
        lax.psum_scatter(grad_gru_gain, "rep", scatter_dimension=0, tiled=True),
        lax.psum_scatter(grad_post_in, "rep", scatter_dimension=0, tiled=True),
        lax.psum_scatter(grad_post_gain, "rep", scatter_dimension=0, tiled=True),
        lax.psum_scatter(grad_post_out, "rep", scatter_dimension=0, tiled=True),
        lax.psum_scatter(grad_prior_in, "rep", scatter_dimension=0, tiled=True),
        lax.psum_scatter(grad_prior_gain, "rep", scatter_dimension=0, tiled=True),
        lax.psum_scatter(grad_prior_out, "rep", scatter_dimension=0, tiled=True),
        lax.psum_scatter(grad_enc_in, "rep", scatter_dimension=0, tiled=True),
        lax.psum_scatter(grad_enc_gain, "rep", scatter_dimension=0, tiled=True),
        lax.psum_scatter(grad_enc_out, "rep", scatter_dimension=0, tiled=True),
    )
    (
        grad_manager_in,
        grad_goal_in,
        grad_goal_out,
        grad_actor_in,
        grad_critic_in,
        grad_img_stoch,
        grad_gru_weight,
        grad_post_in,
        grad_post_out,
        grad_prior_in,
        grad_prior_out,
        grad_enc_in,
    ) = (
        lax.psum_scatter(grad_manager_in, "dp", scatter_dimension=1, tiled=True),
        lax.psum_scatter(grad_goal_in, "dp", scatter_dimension=1, tiled=True),
        lax.psum_scatter(grad_goal_out, "dp", scatter_dimension=1, tiled=True),
        lax.psum_scatter(grad_actor_in, "dp", scatter_dimension=1, tiled=True),
        lax.psum_scatter(grad_critic_in, "dp", scatter_dimension=1, tiled=True),
        lax.psum_scatter(grad_img_stoch, "dp", scatter_dimension=1, tiled=True),
        lax.psum_scatter(grad_gru_weight, "dp", scatter_dimension=1, tiled=True),
        lax.psum_scatter(grad_post_in, "dp", scatter_dimension=1, tiled=True),
        lax.psum_scatter(grad_post_out, "dp", scatter_dimension=1, tiled=True),
        lax.psum_scatter(grad_prior_in, "dp", scatter_dimension=1, tiled=True),
        lax.psum_scatter(grad_prior_out, "dp", scatter_dimension=1, tiled=True),
        lax.psum_scatter(grad_enc_in, "dp", scatter_dimension=1, tiled=True),
    )
    (
        loss_vector,
        grad_obs_gain,
        grad_manager_gain,
        grad_manager_out,
        grad_goal_gain,
        grad_actor_gain,
        grad_actor_out,
        grad_critic_gain,
        grad_critic_out,
        grad_img_action,
        grad_img_gain,
        grad_gru_gain,
        grad_post_gain,
        grad_prior_gain,
        grad_enc_gain,
        grad_enc_out,
    ) = lax.psum(
        (
            loss_vector,
            grad_obs_gain,
            grad_manager_gain,
            grad_manager_out,
            grad_goal_gain,
            grad_actor_gain,
            grad_actor_out,
            grad_critic_gain,
            grad_critic_out,
            grad_img_action,
            grad_img_gain,
            grad_gru_gain,
            grad_post_gain,
            grad_prior_gain,
            grad_enc_gain,
            grad_enc_out,
        ),
        "dp",
    )
    total_loss = loss_vector[0]
    return (
        total_loss,
        grad_prev.reshape(SEQ_DEV, LEN, H),
        embed_grad.reshape(SEQ_DEV, LEN, E),
        grad_obs_gain,
        grad_manager_in,
        grad_manager_gain,
        grad_manager_out,
        grad_goal_in,
        grad_goal_gain,
        grad_goal_out,
        grad_actor_in,
        grad_actor_gain,
        grad_actor_out,
        grad_critic_in,
        grad_critic_gain,
        grad_critic_out,
        grad_img_stoch,
        grad_img_action,
        grad_img_gain,
        grad_gru_weight,
        grad_gru_gain,
        grad_post_in,
        grad_post_gain,
        grad_post_out,
        grad_prior_in,
        grad_prior_gain,
        grad_prior_out,
        grad_enc_in,
        grad_enc_gain,
        grad_enc_out,
    )


def solution(mesh):
    in_specs = (
        P(("dp", "rep"), None, None),
        P(("dp", "rep"), None, None),
        P(("dp", "rep")),
        P(("dp", "rep"), None),
        P(("dp", "rep"), None),
        P(("dp", "rep"), None),
        P(("dp", "rep"), None, None),
        P(("dp", "rep"), None),
        P(("dp", "rep"), None),
        P(("dp", "rep"), None),
        P(("dp", "rep"), None, None),
        P(("dp", "rep"), None),
        P("rep"),
        P("rep", None),
        P("rep"),
        P("rep"),
        P("rep", None),
        P("rep"),
        P("rep", None),
        P("rep", None),
        P("rep"),
        P("rep", None),
        P("rep", None),
        P("rep"),
        P("rep"),
        P("rep", None),
        P(None, "rep"),
        P("rep"),
        P("rep", None),
        P("rep"),
        P("rep", None),
        P("rep"),
        P("rep", None),
        P("rep", None),
        P("rep"),
        P("rep", None),
        P("rep", None),
        P("rep"),
        P("rep", None),
    )
    out_specs = (
        P(),
        P(("dp", "rep"), None, None),
        P(("dp", "rep"), None, None),
        P("rep"),
        P("rep", "dp"),
        P("rep"),
        P("rep"),
        P("rep", "dp"),
        P("rep"),
        P("rep", "dp"),
        P("rep", "dp"),
        P("rep"),
        P("rep", None),
        P("rep", "dp"),
        P("rep"),
        P("rep"),
        P("rep", "dp"),
        P(None, "rep"),
        P("rep"),
        P("rep", "dp"),
        P("rep"),
        P("rep", "dp"),
        P("rep"),
        P("rep", "dp"),
        P("rep", "dp"),
        P("rep"),
        P("rep", "dp"),
        P("rep", "dp"),
        P("rep"),
        P("rep", None),
    )
    return jax.shard_map(
        per_device, mesh=mesh, in_specs=in_specs, out_specs=out_specs, check_vma=False
    )
```

profile of v0, /device:TPU:0, one launch (start us, length us, event | category | flops | bytes accessed | tf_op | source)
XLA Modules:
  0.0 2262.3 jit_solution(12048722476929971649)
XLA Ops:
  164.0 325.2 %while.38 = (s32[]{:T(128)}, f32[2]{0:T(128)}, f32[2]{0:T(128)}, f32[64,2]{1,0:T(8,128)}, pred[64,2]{0,1:T(4,128)(4,1)}, /*index=5*/f32[64,2]{1,0:T(8,128)}, f32...) while((s32[]{:T(128)}, f32[2]{0:T(128)}, f32[2]{0:T(128)}, ...), condition=%wide.region_9.10_spmd.clone, body=%wide.region_8.9_spmd.clone.sunk | while | flops 20 | bytes 233 | solution.py:91
  559.0 40.6 %pmax.7 = f32[]{:T(128)} all-reduce(f32[]{:T(128)} %get-tuple-element.572), channel_id=1, replica_groups=mesh['dp'=8,'rep'=4] {'dp','rep'}, use_global_device_ids=true, to_apply=%region_43.45 | all-reduce | flops 1 | bytes 8 | tf_op jit(solution)/shard_map/pmax | solution.py:329
  717.4 30.1 %copy.130 = pred[128,16,32,32]{3,2,1,0:T(32,128)(4,1)} copy(pred[128,16,32,32]{0,3,2,1:T(32,128)(4,1)S(1)} %iota_compare_fusion) | data formatting | bytes 4194304 | tf_op jit(solution)/shard_map/eq | solution.py:301
  843.1 46.8 %reduce-scatter.66.cloned.1.call-done = f32[256,1024]{1,0:T(8,128)} async-done(((f32[1024,1024]{1,0:T(8,128)}), f32[256,1024]{1,0:T(8,128)}) %reduce-scatter.66.cloned.1.call-update) | async-done | bytes 1048592 | tf_op jit(solution)/shard_map/reduce_scatter | solution.py:487
  890.1 47.1 %reduce-scatter.52.cloned.1.call-done = f32[256,1024]{1,0:T(8,128)} async-done(((f32[1024,1024]{1,0:T(8,128)}), f32[256,1024]{1,0:T(8,128)}) %reduce-scatter.52.cloned.1.call-update) | async-done | bytes 1048592 | tf_op jit(solution)/shard_map/reduce_scatter | solution.py:480
  937.3 60.7 %reduce-scatter.50.cloned.1.call-done = f32[768,512]{1,0:T(8,128)} async-done(((f32[3072,512]{1,0:T(8,128)}), f32[768,512]{1,0:T(8,128)}) %reduce-scatter.50.cloned.1.call-update) | async-done | bytes 1572880 | tf_op jit(solution)/shard_map/reduce_scatter | solution.py:477
  1001.1 58.0 %reduce-scatter.46.cloned.1.call-done = f32[768,512]{1,0:T(8,128)} async-done(((f32[3072,512]{1,0:T(8,128)}), f32[768,512]{1,0:T(8,128)}) %reduce-scatter.46.cloned.1.call-update) | async-done | bytes 1572880 | tf_op jit(solution)/shard_map/reduce_scatter | solution.py:474
  1062.2 84.8 %reduce-scatter.62.cloned.1.call-done = f32[640,1024]{1,0:T(8,128)} async-done(((f32[2560,1024]{1,0:T(8,128)}), f32[640,1024]{1,0:T(8,128)}) %reduce-scatter.62.cloned.1.call-update) | async-done | bytes 2621456 | tf_op jit(solution)/shard_map/reduce_scatter | solution.py:485
  1147.1 183.0 %reduce-scatter.58.cloned.1.call-done = f32[512,3072]{1,0:T(8,128)} async-done(((f32[2048,3072]{1,0:T(8,128)}), f32[512,3072]{1,0:T(8,128)}) %reduce-scatter.58.cloned.1.call-update) | async-done | bytes 6291472 | tf_op jit(solution)/shard_map/reduce_scatter | solution.py:483
  1338.9 56.0 %reduce-scatter.84.cloned.1.call-done = f32[64,16]{1,0:T(8,128)} async-done(((f32[512,16]{1,0:T(8,128)}), f32[64,16]{1,0:T(8,128)}) %reduce-scatter.84.cloned.1.call-update) | async-done | bytes 4112
  1415.9 21.9 reduce-scatter.80.cloned.1.call-done
  1437.8 22.0 reduce-scatter.56.cloned.1.call-done
  1459.7 39.7 %all-reduce.18 = (f32[]{:T(128)}, f32[256]{0:T(256)}, f32[128]{0:T(128)}, f32[128]{0:T(128)}, f32[128]{0:T(128)}, /*index=5*/f32[128]{0:T(128)}, f32[128,17]{0,1...) all-reduce(f32[]{:T(128)} %bitcast.42, ...), channel_id=1, replica_groups=mesh['dp'=8,'rep'=4] {'dp'}, use_global_device_ids=true, to_apply=%region_45.47 | all-reduce | flops 17409 | bytes 139272 | tf_op jit(solution)/shard_map/psum | solution.py:539
  1499.4 26.7 %reduce-scatter.82.cloned.1.call-done = f32[64,256]{1,0:T(8,128)} async-done(((f32[512,256]{1,0:T(8,128)}), f32[64,256]{1,0:T(8,128)}) %reduce-scatter.82.cloned.1.call-update) | async-done | bytes 65552
  1526.1 64.9 %reduce-scatter.90.cloned.1.call-done = f32[64,256]{1,0:T(8,128)} async-done(((f32[512,256]{1,0:T(8,128)}), f32[64,256]{1,0:T(8,128)}) %reduce-scatter.90.cloned.1.call-update) | async-done | bytes 65552
  1591.0 65.6 %reduce-scatter.44.cloned.1.call-done = f32[128,128]{1,0:T(8,128)} async-done(((f32[128,1024]{1,0:T(8,128)}), f32[128,128]{1,0:T(8,128)}) %reduce-scatter.44.cloned.1.call-update) | async-done | bytes 65552 | tf_op jit(solution)/shard_map/reduce_scatter | solution.py:511
  1656.5 67.0 %reduce-scatter.72.cloned.1.call-done = f32[256,128]{1,0:T(8,128)} async-done(((f32[256,1024]{1,0:T(8,128)}), f32[256,128]{1,0:T(8,128)}) %reduce-scatter.72.cloned.1.call-update) | async-done | bytes 131088 | tf_op jit(solution)/shard_map/reduce_scatter | solution.py:518
  1723.5 67.4 %reduce-scatter.76.cloned.1.call-done = f32[256,128]{1,0:T(8,128)} async-done(((f32[256,1024]{1,0:T(8,128)}), f32[256,128]{1,0:T(8,128)}) %reduce-scatter.76.cloned.1.call-update) | async-done | bytes 131088 | tf_op jit(solution)/shard_map/reduce_scatter | solution.py:519
  1790.9 66.7 %reduce-scatter.68.cloned.1.call-done = f32[256,128]{1,0:T(8,128)} async-done(((f32[256,1024]{1,0:T(8,128)}), f32[256,128]{1,0:T(8,128)}) %reduce-scatter.68.cloned.1.call-update) | async-done | bytes 131088 | tf_op jit(solution)/shard_map/reduce_scatter | solution.py:517
  1857.6 67.3 %reduce-scatter.54.cloned.1.call-done = f32[256,128]{1,0:T(8,128)} async-done(((f32[256,1024]{1,0:T(8,128)}), f32[256,128]{1,0:T(8,128)}) %reduce-scatter.54.cloned.1.call-update) | async-done | bytes 131088 | tf_op jit(solution)/shard_map/reduce_scatter | solution.py:514
  1924.9 67.9 %reduce-scatter.88.cloned.1.call-done = f32[64,768]{1,0:T(8,128)} async-done(((f32[512,768]{1,0:T(8,128)}), f32[64,768]{1,0:T(8,128)}) %reduce-scatter.88.cloned.1.call-update) | async-done | bytes 196624
  1992.8 67.9 %reduce-scatter.86.cloned.1.call-done = f32[64,768]{1,0:T(8,128)} async-done(((f32[512,768]{1,0:T(8,128)}), f32[64,768]{1,0:T(8,128)}) %reduce-scatter.86.cloned.1.call-update) | async-done | bytes 196624
  2060.7 73.8 %reduce-scatter.64.cloned.1.call-done = f32[640,128]{1,0:T(8,128)} async-done(((f32[640,1024]{1,0:T(8,128)}), f32[640,128]{1,0:T(8,128)}) %reduce-scatter.64.cloned.1.call-update) | async-done | bytes 327696 | tf_op jit(solution)/shard_map/reduce_scatter | solution.py:516
  2134.5 121.0 %reduce-scatter.60.cloned.1.call-done = f32[512,384]{1,0:T(8,128)} async-done(((f32[512,3072]{1,0:T(8,128)}), f32[512,384]{1,0:T(8,128)}) %reduce-scatter.60.cloned.1.call-update) | async-done | bytes 786448 | tf_op jit(solution)/shard_map/reduce_scatter | solution.py:515
  (1078 shorter events, 794.2 us)
Async XLA Ops:
  10.0 484.3 %all-gather.34.cloned.1.call-start = ((), (), s32[]{:S(2)}) async-start(), calls=%async_computation.35 | async-start | bytes 2621440 | tf_op jit(solution)/shard_map/all_gather | solution.py:211
  10.6 486.9 %all-gather.36.cloned.1.call-start = ((), (), s32[]{:S(2)}) async-start(), calls=%async_computation.36 | async-start | bytes 2621440 | tf_op jit(solution)/shard_map/all_gather | solution.py:213
  11.4 489.8 %all-gather.30.cloned.1.call-start = ((), (), s32[]{:S(2)}) async-start(), calls=%async_computation.33 | async-start | bytes 6553600 | tf_op jit(solution)/shard_map/all_gather | solution.py:208
  12.2 493.9 %all-gather.32.cloned.1.call-start = ((), (), s32[]{:S(2)}) async-start(), calls=%async_computation.34 | async-start | bytes 2621440 | tf_op jit(solution)/shard_map/all_gather | solution.py:210
  12.9 501.3 %all-gather.40.cloned.1.call-start = ((), (), s32[]{:S(2)}) async-start(), calls=%async_computation.38 | async-start | bytes 1310720 | tf_op jit(solution)/shard_map/all_gather | solution.py:196
  13.7 510.4 %all-gather.44.cloned.1.call-start = ((), (), s32[]{:S(2)}) async-start(), calls=%async_computation.40 | async-start | bytes 3932160 | tf_op jit(solution)/shard_map/all_gather | solution.py:197
  24.1 509.6 %all-gather.42.cloned.1.call-start = ((), (), s32[]{:S(2)}) async-start(), calls=%async_computation.39 | async-start | bytes 3932160 | tf_op jit(solution)/shard_map/all_gather | solution.py:200
  143.7 666.9 %reduce-scatter.40.cloned.1.call-start = ((), (), s32[]{:S(2)}) async-start(), calls=%async_computation.42 | async-start | bytes 163840 | tf_op jit(solution)/shard_map/reduce_scatter | solution.py:471
  796.0 534.1 %reduce-scatter.58.cloned.1.call-start = ((), (), s32[]{:S(2)}) async-start(), calls=%async_computation.51 | async-start | bytes 31457280 | tf_op jit(solution)/shard_map/reduce_scatter | solution.py:483
  810.6 584.3 %reduce-scatter.84.cloned.1.call-start = ((), (), s32[]{:S(2)}) async-start(), calls=%async_computation.64 | async-start | bytes 294912
  812.4 603.5 %reduce-scatter.48.cloned.1.call-start = ((), (), s32[]{:S(2)}) async-start(), calls=%async_computation.46 | async-start | bytes 61440 | tf_op jit(solution)/shard_map/reduce_scatter | solution.py:476
  814.5 623.2 %reduce-scatter.80.cloned.1.call-start = ((), (), s32[]{:S(2)}) async-start(), calls=%async_computation.62 | async-start | bytes 163840 | tf_op jit(solution)/shard_map/reduce_scatter | solution.py:493
  815.5 644.2 %reduce-scatter.56.cloned.1.call-start = ((), (), s32[]{:S(2)}) async-start(), calls=%async_computation.50 | async-start | bytes 122880 | tf_op jit(solution)/shard_map/reduce_scatter | solution.py:481
  816.5 709.6 %reduce-scatter.82.cloned.1.call-start = ((), (), s32[]{:S(2)}) async-start(), calls=%async_computation.63 | async-start | bytes 589824
  818.8 772.2 %reduce-scatter.90.cloned.1.call-start = ((), (), s32[]{:S(2)}) async-start(), calls=%async_computation.67 | async-start | bytes 589824
  820.9 835.6 %reduce-scatter.44.cloned.1.call-start = ((), (), s32[]{:S(2)}) async-start(), calls=%async_computation.44 | async-start | bytes 589824 | tf_op jit(solution)/shard_map/reduce_scatter | solution.py:511
  821.5 902.0 %reduce-scatter.72.cloned.1.call-start = ((), (), s32[]{:S(2)}) async-start(), calls=%async_computation.58 | async-start | bytes 1179648 | tf_op jit(solution)/shard_map/reduce_scatter | solution.py:518
  822.3 968.6 %reduce-scatter.76.cloned.1.call-start = ((), (), s32[]{:S(2)}) async-start(), calls=%async_computation.60 | async-start | bytes 1179648 | tf_op jit(solution)/shard_map/reduce_scatter | solution.py:519
  843.1 1014.5 %reduce-scatter.68.cloned.1.call-start = ((), (), s32[]{:S(2)}) async-start(), calls=%async_computation.56 | async-start | bytes 1179648 | tf_op jit(solution)/shard_map/reduce_scatter | solution.py:517
  890.0 1034.9 %reduce-scatter.54.cloned.1.call-start = ((), (), s32[]{:S(2)}) async-start(), calls=%async_computation.49 | async-start | bytes 1179648 | tf_op jit(solution)/shard_map/reduce_scatter | solution.py:514
  937.2 1055.5 %reduce-scatter.88.cloned.1.call-start = ((), (), s32[]{:S(2)}) async-start(), calls=%async_computation.66 | async-start | bytes 1769472
  1001.1 1059.6 %reduce-scatter.86.cloned.1.call-start = ((), (), s32[]{:S(2)}) async-start(), calls=%async_computation.65 | async-start | bytes 1769472
  1062.1 1072.4 %reduce-scatter.64.cloned.1.call-start = ((), (), s32[]{:S(2)}) async-start(), calls=%async_computation.54 | async-start | bytes 2949120 | tf_op jit(solution)/shard_map/reduce_scatter | solution.py:516
  1147.0 1108.5 %reduce-scatter.60.cloned.1.call-start = ((), (), s32[]{:S(2)}) async-start(), calls=%async_computation.52 | async-start | bytes 7077888 | tf_op jit(solution)/shard_map/reduce_scatter | solution.py:515
  (236 other events, 6903.5 us)
Sparse Core Ops, SparseCore 0:
  36.5 83.3 all-gather.25
  206.0 40.4 all-gather.29
  649.7 31.4 reduce-scatter.37
  683.6 31.4 reduce-scatter.77
  751.5 44.4 reduce-scatter.69
  798.5 44.4 reduce-scatter.73
  845.5 44.4 reduce-scatter.65
  892.7 44.4 reduce-scatter.51
  939.6 58.3 reduce-scatter.49
  1000.7 58.3 reduce-scatter.45
  1061.7 85.2 reduce-scatter.61
  1149.6 180.4 reduce-scatter.57
  1333.6 61.1 reduce-scatter.83
  1464.0 62.0 reduce-scatter.81
  1530.0 60.9 reduce-scatter.89
  1595.1 61.3 reduce-scatter.43
  1660.5 62.9 reduce-scatter.71
  1727.9 62.9 reduce-scatter.75
  1794.7 62.8 reduce-scatter.67
  1861.9 62.8 reduce-scatter.53
  1928.9 63.8 reduce-scatter.87
  1997.0 63.6 reduce-scatter.85
  2064.7 69.8 reduce-scatter.63
  2138.7 116.8 reduce-scatter.59
  (14 shorter events, 308.0 us)
where the time goes:
time: 2270 us; the launch traced here: 2260 us
  waiting for transfers between devices  1380 us (61%)
  local copies, waits for them, and re-layouts  345 us (15%)
  blocking collectives  174 us (8%)
  matrix products  156 us (7%)
  other arithmetic  155 us (7%)
  starting transfers between devices  32.9 us (1%)
    unnamed x43, waiting for transfers between devices  292 us
    reduce_scatter x1, waiting for transfers between devices, per_device(): lax.psum_scatter(grad_gru_weight, 'rep', scatter_dimension=0, tiled=True)  183 us
    dynamic_slice x128, local copies, waits for them, and re-layouts, chain_returns(): lax.scan(back_step, (zero_start, zero_start), (values_now.T, rewards_now....  160 us
    reduce_scatter x1, waiting for transfers between devices, per_device(): lax.psum_scatter(grad_gru_weight, 'dp', scatter_dimension=1, tiled=True)  121 us
    reduce_scatter x1, waiting for transfers between devices, per_device(): lax.psum_scatter(grad_post_in, 'rep', scatter_dimension=0, tiled=True)  84.8 us
    dynamic_update_slice x80, local copies, waits for them, and re-layouts, chain_returns(): lax.scan(back_step, (zero_start, zero_start), (values_now.T, rewards_now....  83.2 us
    select_n x80, other arithmetic, back_step(): jnp.where(link_now, reward_now + discount * carry_now * blended, current)  82.9 us
    reduce_scatter x1, waiting for transfers between devices, per_device(): lax.psum_scatter(grad_post_in, 'dp', scatter_dimension=1, tiled=True)  73.8 us
  transfers between devices with their start and end apart: 41, of which 23 were waited for; matrix products, arithmetic and copies ran while one was open for 26% of the time, Pallas kernels for 0%

commit v1 on v0

v1 whole, which is shorter than its diff:
```python
import math
from typing import Any, NamedTuple

import jax
import jax.numpy as jnp
from jax import lax
from jax.experimental import pallas as pl
from jax.experimental.pallas import tpu as pltpu
from jax.sharding import PartitionSpec as P

H = 1024
ZG = 32
ZK = 32
U = 512
GC = 8
GK = 8
NA = 17
E = 1536
LEN = 64
HOR = 16
SEQ_DEV = 2
Z = 1024
GCODE = 64
ROWS = 128


discount = 0.99
return_mix = 0.95
epsilon = 1e-05
small_floor = 1e-06
highest = lax.Precision.HIGHEST


MESH = pl.DeviceIdType.MESH
BF = jnp.bfloat16
F32 = jnp.float32
LANES = 128
VMEM_BYTES = 62 * 2**20


class Arg(NamedTuple):
    kind: Any
    shape: Any
    dtype: Any
    here: bool = True


TAKEN, GIVEN, KEPT, SIGNAL = range(4)


def taken(*shape, dtype=BF, here=True):
    return Arg(TAKEN, shape, dtype, here)


def given(*shape, dtype=BF, here=True):
    return Arg(GIVEN, shape, dtype, here)


def kept(*shape, dtype=BF):
    return Arg(KEPT, shape, dtype)


def signal(*shape):
    return Arg(SIGNAL, shape, None)


def run_kernel(body, layout, inputs, name, collective=None):
    def kernel(*refs):
        body(type(layout)(*refs))

    def place(arg):
        return pl.BlockSpec(memory_space=pltpu.VMEM if arg.here else pl.ANY)

    outs = [a for a in layout if a.kind == GIVEN]
    more = {} if collective is None else dict(collective_id=collective, has_side_effects=True)
    results = pl.pallas_call(
        kernel,
        out_shape=[jax.ShapeDtypeStruct(a.shape, a.dtype) for a in outs],
        in_specs=[place(a) for a in layout if a.kind == TAKEN],
        out_specs=[place(a) for a in outs],
        scratch_shapes=[
            pltpu.VMEM(a.shape, a.dtype) if a.kind == KEPT else pltpu.SemaphoreType.DMA(a.shape)
            for a in layout
            if a.kind >= KEPT
        ],
        compiler_params=pltpu.CompilerParams(vmem_limit_bytes=VMEM_BYTES, **more),
        name=name,
    )(*inputs)
    results = iter(results)
    return type(layout)(*[next(results) if a.kind == GIVEN else None for a in layout])


def product(left, right):
    return jnp.dot(left, right, preferred_element_type=jnp.float32)


def normalize(values_in):
    row_mean = jnp.mean(values_in, -1, keepdims=True)
    centred = values_in - row_mean
    inverse = lax.rsqrt(jnp.mean(centred * centred, -1, keepdims=True) + epsilon)
    return (centred * inverse, inverse)


def normalize_back(grad_normed, normed, inverse):
    return inverse * (
        grad_normed
        - jnp.mean(grad_normed, -1, keepdims=True)
        - normed * jnp.mean(grad_normed * normed, -1, keepdims=True)
    )


def matmul_into(out_ref, left, weight_ref, turned=False, tile=256, low=0, extra=None):
    total = out_ref.shape[-1]

    def one(j, carry):
        start = pl.multiple_of(j * tile, tile)
        if turned:
            value = lax.dot_general(
                left,
                weight_ref[pl.ds(pl.multiple_of(low + j * tile, tile), tile), :],
                (((1,), (1,)), ((), ())),
                preferred_element_type=F32,
            )
        else:
            value = product(left, weight_ref[:, pl.ds(start, tile)])
        if extra is not None:
            value = value + extra(start, tile)
        out_ref[:, pl.ds(start, tile)] = value
        return carry

    lax.fori_loop(0, total // tile, one, 0)


def by_rows(count, size, body, carry=0):
    def one(i, carry):
        return body(pl.ds(pl.multiple_of(i * size, size), size), carry)

    return lax.fori_loop(0, count // size, one, carry)


def elu_of(value):
    return jnp.where(value > 0, value, jnp.exp(jnp.minimum(value, 0.0)) - 1.0)


def normalize_rows(ref, inverse_ref, size):
    def one(rows, carry):
        normed, inverse = normalize(ref[rows, :])
        ref[rows, :] = normed
        inverse_ref[rows, :] = inverse
        return carry

    by_rows(ref.shape[0], size, one)


def hidden_rows(ref, inverse_ref, gain, hidden_ref, size=32):
    def one(rows, carry):
        normed, inverse = normalize(ref[rows, :])
        ref[rows, :] = normed
        inverse_ref[rows, :] = inverse
        hidden_ref[rows, :] = elu_of(normed * gain).astype(BF)
        return carry

    by_rows(ref.shape[0], size, one)


def hidden_rows_back(grad_of, ref, inverse_ref, gain, pre_ref, size=32):
    def one(rows, total):
        normed = ref[rows, :]
        scaled = normed * gain
        grad_scaled = grad_of(rows) * jnp.where(
            scaled > 0, 1.0, jnp.exp(jnp.minimum(scaled, 0.0))
        )
        total = total + jnp.sum(grad_scaled * normed, 0, keepdims=True)
        back = normalize_back(grad_scaled * gain, normed, inverse_ref[rows, :])
        pre_ref[rows, :] = back.astype(pre_ref.dtype)
        return total

    return by_rows(ref.shape[0], size, one, jnp.zeros((1, ref.shape[1]), F32))


def turn_into(out_ref, value_ref, low=0):
    for j in range(value_ref.shape[1] // LANES):
        tile = value_ref[:, j * LANES : (j + 1) * LANES].astype(F32).T
        out_ref[low + j * LANES : low + (j + 1) * LANES, :] = tile.astype(out_ref.dtype)


def class_spread(groups, classes, rows, width):
    group = lax.broadcasted_iota(jnp.int32, (rows, width), 0)
    lane = lax.broadcasted_iota(jnp.int32, (rows, width), 1)
    inside = (lane >= group * classes) & (lane < group * classes + classes) & (group < groups)
    return jnp.where(inside, 1.0, 0.0).astype(BF)


def hot_rows(ids, classes, groups, width):
    here = product(ids.astype(BF), class_spread(groups, classes, ids.shape[1], width))
    lane = lax.broadcasted_iota(jnp.int32, (1, width), 1)
    same = here == jnp.bitwise_and(lane, classes - 1).astype(F32)
    return jnp.where(same & (lane < groups * classes), 1.0, 0.0)


def vector_of(packed, low, tiles):
    return jnp.concatenate(
        [packed[r, low + i : low + i + 1, :] for r in range(4) for i in range(tiles)], 1
    )


def put_vector(small_ref, low, value):
    tiles = value.shape[1] // (4 * LANES)
    for r in range(4):
        for i in range(tiles):
            start = (r * tiles + i) * LANES
            small_ref[r % 2, r // 2, low + i : low + i + 1, :] = value[:, start : start + LANES]


def put_table(small_ref, low, value, rows):
    for r in range(4):
        small_ref[r % 2, r // 2, low : low + rows, :] = value[
            0:rows, r * LANES : (r + 1) * LANES
        ]


OBS, MAN_G, MAN_O, GOAL_G, ACT_G, CRI_G, CRI_O, IMG_G, GRU_G, POST_G, PRIOR_G, ENC_G, LOSS = (
    0, 2, 3, 4, 5, 6, 7, 8, 10, 16, 18, 20, 21,
)
ACT_T, ENC_T, IMG_T, SMALL_TILES = (24, 48, 112, 160)
TAB_ACT, TAB_ENC, TAB_IMG, TAB_GOAL, TABLES = (0, 32, 96, 160, 224)
VECTOR_TILES = 24


def spread_lanes(low_ref, out_ref, first_row, which):
    lane = lax.broadcasted_iota(jnp.int32, (ROWS, LANES), 1)
    keep = (lane < 64) if which == 0 else (lane >= 64)
    for j in range(4):
        tile = low_ref[:, j * LANES : (j + 1) * LANES].astype(F32)
        turned = pltpu.roll(tile, 64, 1)
        for x in range(2):
            source = tile if x == which else turned
            lanes = slice((2 * j + x) * LANES, (2 * j + x + 1) * LANES)
            out_ref[first_row : first_row + ROWS, lanes] = jnp.where(keep, source, 0.0).astype(BF)


def column(meta, k):
    return meta[:, k : k + 1]


class Frames(NamedTuple):
    meta: Any = taken(ROWS, LANES, dtype=F32)
    prev: Any = taken(ROWS, H)
    embed: Any = taken(ROWS, E)
    vector_share: Any = taken(VECTOR_TILES, LANES, dtype=F32)
    table_share: Any = taken(TABLES, LANES)
    img_stoch_share: Any = taken(Z // 4, H, here=False)
    gru_weight_share: Any = taken(H // 2, 3 * H, here=False)
    manager_in_share: Any = taken(H // 4, U, here=False)
    enc_in_share: Any = taken(H // 4, U, here=False)
    goal_out_share: Any = taken(U // 4, H, here=False)
    prior_in_share: Any = taken(H // 4, H, here=False)
    post_in_share: Any = taken((H + E) // 4, H, here=False)
    prior_out_share: Any = taken(H // 4, Z, here=False)
    post_out_share: Any = taken(H // 4, Z, here=False)
    actor_in_share: Any = taken(768, U, here=False)
    critic_in_share: Any = taken(768, U, here=False)
    gru_weight_out: Any = given(2 * H, 3 * H, here=False)
    goal_out_out: Any = given(U, H, here=False)
    actor_in_out: Any = given(3 * H, U, here=False)
    critic_in_out: Any = given(3 * H, U, here=False)
    vectors: Any = given(4, VECTOR_TILES, LANES, dtype=F32)
    tables: Any = given(4, TABLES, LANES)
    start_state: Any = given(ROWS, H + LANES)
    gru_left: Any = given(2 * H, ROWS)
    post_left: Any = given(H + E, ROWS)
    post_out_left: Any = given(H, ROWS)
    prior_out_left: Any = given(H, ROWS)
    img_left: Any = given(Z, ROWS)
    me_left: Any = given(H, 2 * ROWS)
    dec_left: Any = given(U, ROWS)
    soft_turned: Any = given(GCODE, ROWS)
    post_right: Any = given(ROWS, H)
    prior_right: Any = given(ROWS, H)
    post_out_right: Any = given(ROWS, Z)
    prior_out_right: Any = given(ROWS, Z)
    me_right: Any = given(2 * ROWS, 2 * U)
    recon_low: Any = given(ROWS, H)
    dec_pair: Any = given(ROWS, 2 * U)
    gru_normed: Any = given(ROWS, 3 * H, dtype=F32)
    gru_inverse: Any = given(ROWS, 1, dtype=F32)
    img_normed: Any = given(ROWS, H, dtype=F32)
    img_inverse: Any = given(ROWS, 1, dtype=F32)
    grad_deter: Any = given(ROWS, H, dtype=F32)
    embed_grad: Any = given(ROWS, E, dtype=F32)
    small: Any = given(2, 2, SMALL_TILES, LANES, dtype=F32)
    img_stoch: Any = kept(Z, H)
    gru_weight: Any = kept(2 * H, 3 * H)
    manager_in: Any = kept(H, U)
    enc_in: Any = kept(H, U)
    goal_out: Any = kept(U, H)
    prior_in: Any = kept(H, H)
    post_in: Any = kept(H + E, H)
    prior_out: Any = kept(H, Z)
    post_out: Any = kept(H, Z)
    actor_in: Any = kept(3 * H, U)
    critic_in: Any = kept(3 * H, U)
    img_action: Any = kept(32, H)
    enc_out: Any = kept(GCODE, U)
    goal_in: Any = kept(GCODE, U)
    hot: Any = kept(ROWS, Z)
    meta_turned: Any = kept(LANES, ROWS, dtype=F32)
    img_hidden: Any = kept(ROWS, H)
    deter: Any = kept(ROWS, H, dtype=F32)
    deter_low: Any = kept(ROWS, H)
    feature: Any = kept(ROWS, H)
    obs_normed: Any = kept(ROWS, H, dtype=F32)
    obs_inverse: Any = kept(ROWS, 1, dtype=F32)
    outgoing: Any = kept(ROWS, H + LANES)
    incoming: Any = kept(ROWS, H + LANES)
    pre_512: Any = kept(ROWS, U, dtype=F32)
    hid_512: Any = kept(ROWS, U)
    back_512: Any = kept(ROWS, U)
    wide_512: Any = kept(ROWS, U, dtype=F32)
    inverse: Any = kept(ROWS, 1, dtype=F32)
    grad_value: Any = kept(ROWS, 1, dtype=F32)
    dec_normed: Any = kept(ROWS, U, dtype=F32)
    dec_inverse: Any = kept(ROWS, 1, dtype=F32)
    dec_hidden: Any = kept(ROWS, U)
    dec_pre: Any = kept(ROWS, U)
    wide: Any = kept(ROWS, H, dtype=F32)
    prior_normed: Any = kept(ROWS, H, dtype=F32)
    prior_inverse: Any = kept(ROWS, 1, dtype=F32)
    prior_hidden: Any = kept(ROWS, H)
    post_normed: Any = kept(ROWS, H, dtype=F32)
    post_inverse: Any = kept(ROWS, 1, dtype=F32)
    post_hidden: Any = kept(ROWS, H)
    post_turned: Any = kept(Z, ROWS, dtype=F32)
    prior_turned: Any = kept(Z, ROWS, dtype=F32)
    loss: Any = kept(1, 1, dtype=F32)
    piece_send: Any = signal(14, 8)
    piece_recv: Any = signal(14, 8)
    load_done: Any = signal(14)
    save_done: Any = signal(4)
    small_send: Any = signal(2, 3)
    small_recv: Any = signal(2, 3)
    state_send: Any = signal(8)
    state_recv: Any = signal(8)

    def start(self):
        meta = self.meta[...]
        hot = hot_rows(meta[:, 0:ZG], ZK, ZG, Z)
        self.hot[...] = hot.astype(BF)
        turn_into(self.img_left, self.hot)
        turn_into(self.gru_left, self.prev, H)
        turn_into(self.post_left, self.embed, H)
        self.meta_turned[...] = meta.T
        self.small[...] = jnp.zeros(self.small.shape, F32)

    def unpack(self):
        for r in range(4):
            for i in range(2):
                self.img_action[:, (2 * r + i) * LANES : (2 * r + i + 1) * LANES] = self.tables[
                    r, TAB_IMG + 32 * i : TAB_IMG + 32 * (i + 1), :
                ]
            self.enc_out[:, r * LANES : (r + 1) * LANES] = self.tables[
                r, TAB_ENC : TAB_ENC + 64, :
            ]
            for i in range(4):
                self.goal_in[16 * r : 16 * (r + 1), i * LANES : (i + 1) * LANES] = self.tables[
                    r, TAB_GOAL + 16 * i : TAB_GOAL + 16 * (i + 1), :
                ]

    def gain(self, low, size):
        return vector_of(self.vectors, low, size // (4 * LANES))

    def img(self):
        meta = self.meta[...]
        lane = lax.broadcasted_iota(jnp.int32, (ROWS, 32), 1).astype(F32)
        action = jnp.where(column(meta, 32) == lane, 1.0, 0.0).astype(BF)
        matmul_into(
            self.img_normed, self.hot[...], self.img_stoch,
            extra=lambda start, tile: product(action, self.img_action[:, pl.ds(start, tile)]),
        )
        hidden_rows(self.img_normed, self.img_inverse, self.gain(IMG_G, H), self.img_hidden)
        turn_into(self.gru_left, self.img_hidden)

    def gru(self, third):
        low = third * H
        out = self.gru_normed.at[:, low : low + H]

        def one(j, carry):
            start = pl.multiple_of(low + j * 256, 256)
            value = product(self.img_hidden[...], self.gru_weight[0:H, pl.ds(start, 256)])
            value = value + product(
                self.prev[...], self.gru_weight[H : 2 * H, pl.ds(start, 256)]
            )
            self.gru_normed[:, pl.ds(start, 256)] = value
            return carry

        lax.fori_loop(0, 4, one, 0)

    def state(self):
        gain = self.gain(GRU_G, 3 * H)
        obs_gain = self.gain(OBS, H)

        def one(rows, carry):
            normed, inverse = normalize(self.gru_normed[rows, :])
            self.gru_normed[rows, :] = normed
            self.gru_inverse[rows, :] = inverse
            parts = normed * gain
            reset = 1.0 / (1.0 + jnp.exp(-parts[:, :H]))
            candidate = jnp.tanh(reset * parts[:, H : 2 * H])
            update = 1.0 / (1.0 + jnp.exp(1.0 - parts[:, 2 * H :]))
            state = update * candidate + (1.0 - update) * self.prev[rows, :].astype(F32)
            self.deter[rows, :] = state
            self.deter_low[rows, :] = state.astype(BF)
            obs, obs_inverse = normalize(state)
            self.obs_normed[rows, :] = obs
            self.obs_inverse[rows, :] = obs_inverse
            self.feature[rows, :] = (obs * obs_gain).astype(BF)
            return carry

        by_rows(ROWS, 16, one)
        turn_into(self.post_left, self.deter_low)

    def picked(self):
        meta = self.meta[...]
        lane = lax.broadcasted_iota(jnp.int32, (ROWS, ROWS), 1).astype(F32)
        pick = jnp.where(column(meta, 37) == lane, 1.0, 0.0).astype(BF)

        def one(j, carry):
            lanes = pl.ds(pl.multiple_of(j * 256, 256), 256)
            self.outgoing[:, lanes] = product(pick, self.deter_low[:, lanes]).astype(BF)
            return carry

        lax.fori_loop(0, H // 256, one, 0)
        valid = jnp.broadcast_to(column(meta, 33), (ROWS, LANES)).astype(BF)
        self.outgoing[:, H:] = product(pick, valid).astype(BF)

    def manager(self):
        meta = self.meta[...]
        gain, head = (self.gain(MAN_G, U), self.gain(MAN_O, U))
        for j in range(H // LANES):
            lanes = slice(j * LANES, (j + 1) * LANES)
            self.me_left[lanes, 0:ROWS] = self.feature[:, lanes].astype(F32).T.astype(BF)
            self.me_left[lanes, ROWS:] = self.deter_low[:, lanes].astype(F32).T.astype(BF)
        matmul_into(self.pre_512, self.feature[...], self.manager_in)
        hidden_rows(self.pre_512, self.inverse, gain, self.hid_512)
        value = jnp.sum(self.hid_512[...].astype(F32) * head, -1, keepdims=True)
        valid, linked, carried, rewards = (column(meta, 33 + i) for i in range(4))
        later = pltpu.roll(jnp.broadcast_to(value, (ROWS, LANES)), ROWS - 1, 0)
        base = jnp.where(
            linked > 0, rewards + discount * carried * ((1.0 - return_mix) * later), value
        )
        slope = jnp.broadcast_to(linked * (discount * return_mix) * carried, (ROWS, LANES))
        step = 1
        while step < LEN:
            base = base + slope * pltpu.roll(base, ROWS - step, 0)
            slope = slope * pltpu.roll(slope, ROWS - step, 0)
            step *= 2
        misfit = value - base[:, 0:1]
        scale = valid * (1.0 / ROWS)
        self.loss[...] = 0.5 * jnp.sum(scale * misfit * misfit, 0, keepdims=True)
        grad_value = scale * misfit
        put_vector(
            self.small, MAN_O,
            jnp.sum(self.hid_512[...].astype(F32) * grad_value, 0, keepdims=True),
        )
        self.grad_value[...] = grad_value
        total = hidden_rows_back(
            lambda rows: self.grad_value[rows, :] * head,
            self.pre_512, self.inverse, gain, self.back_512,
        )
        put_vector(self.small, MAN_G, total)
        spread_lanes(self.back_512, self.me_right, 0, 0)
        self.feature_back()

    def feature_back(self):
        obs_gain = self.gain(OBS, H)
        matmul_into(self.wide, self.back_512[...], self.manager_in, turned=True)

        def one(rows, total):
            grad = self.wide[rows, :]
            normed = self.obs_normed[rows, :]
            total = total + jnp.sum(grad * normed, 0, keepdims=True)
            self.grad_deter[rows, :] = normalize_back(
                grad * obs_gain, normed, self.obs_inverse[rows, :]
            )
            return total

        put_vector(self.small, OBS, by_rows(ROWS, 32, one, jnp.zeros((1, H), F32)))

    def add_back(self, left_ref, weight_ref):
        def one(j, carry):
            lanes = pl.ds(pl.multiple_of(j * 256, 256), 256)
            self.grad_deter[:, lanes] += lax.dot_general(
                left_ref[...], weight_ref[lanes, :], (((1,), (1,)), ((), ())),
                preferred_element_type=F32,
            )
            return carry

        lax.fori_loop(0, H // 256, one, 0)

    def encoder(self):
        gain, goal_gain = (self.gain(ENC_G, U), self.gain(GOAL_G, U))
        valid_row = self.meta_turned[33:34, :]
        scale_row = valid_row * (1.0 / ROWS)
        scale = column(self.meta[...], 33) * (1.0 / ROWS)
        matmul_into(self.pre_512, self.deter_low[...], self.enc_in)
        hidden_rows(self.pre_512, self.inverse, gain, self.hid_512)
        logits = lax.dot_general(
            self.enc_out[...], self.hid_512[...], (((1,), (1,)), ((), ())),
            preferred_element_type=F32,
        ).reshape(GC, GK, ROWS)
        shifted = logits - jnp.max(logits, 1, keepdims=True)
        code_log = shifted - jnp.log(jnp.sum(jnp.exp(shifted), 1, keepdims=True))
        code = jnp.exp(code_log)
        spread = jnp.sum(code * code_log, 1, keepdims=True)
        code_kl = jnp.sum(jnp.sum(code * (code_log + math.log(GK)), 1), 0, keepdims=True)
        flat = jnp.concatenate(
            [code.reshape(GCODE, ROWS), jnp.zeros((ROWS - GCODE, ROWS), F32)], 0
        )
        self.soft_turned[...] = flat[0:GCODE].astype(BF)
        soft = flat.T[:, 0:GCODE].astype(BF)
        matmul_into(self.dec_normed, soft, self.goal_in)
        hidden_rows(self.dec_normed, self.dec_inverse, goal_gain, self.dec_hidden)
        turn_into(self.dec_left, self.dec_hidden)

        def one(j, total):
            lanes = pl.ds(pl.multiple_of(j * 256, 256), 256)
            err = product(self.dec_hidden[...], self.goal_out[:, lanes]) - self.deter[:, lanes]
            grad = scale * err * (1.0 / H)
            self.grad_deter[:, lanes] -= grad
            self.recon_low[:, lanes] = grad.astype(BF)
            return total + jnp.sum(err * err, -1, keepdims=True)

        squares = lax.fori_loop(0, H // 256, one, jnp.zeros((ROWS, 1), F32))
        self.loss[...] += jnp.sum(scale * (0.5 / H) * squares, 0, keepdims=True) + jnp.sum(
            scale_row * code_kl, 1, keepdims=True
        )
        matmul_into(self.wide_512, self.recon_low[...], self.goal_out, turned=True)
        total = hidden_rows_back(
            lambda rows: self.wide_512[rows, :],
            self.dec_normed, self.dec_inverse, goal_gain, self.dec_pre,
        )
        put_vector(self.small, GOAL_G, total)
        spread_lanes(self.dec_pre, self.dec_pair, 0, 0)
        grad_code = lax.dot_general(
            self.goal_in[...], self.dec_pre[...], (((1,), (1,)), ((), ())),
            preferred_element_type=F32,
        ).reshape(GC, GK, ROWS)
        grad_logits = code * (grad_code - jnp.sum(code * grad_code, 1, keepdims=True))
        grad_logits = grad_logits + scale_row[None] * code * (code_log - spread)
        grad_turned = grad_logits.reshape(GCODE, ROWS)
        grad_low = jnp.concatenate(
            [grad_turned, jnp.zeros((ROWS - GCODE, ROWS), F32)], 0
        ).T[:, 0:GCODE].astype(BF)
        put_table(
            self.small, ENC_T, product(grad_turned.astype(BF), self.hid_512[...]), GCODE
        )
        matmul_into(self.wide_512, grad_low, self.enc_out)
        total = hidden_rows_back(
            lambda rows: self.wide_512[rows, :],
            self.pre_512, self.inverse, gain, self.back_512,
        )
        put_vector(self.small, ENC_G, total)
        spread_lanes(self.back_512, self.me_right, ROWS, 1)
        self.add_back(self.back_512, self.enc_in)

    def prior(self):
        matmul_into(self.prior_normed, self.deter_low[...], self.prior_in)
        hidden_rows(
            self.prior_normed, self.prior_inverse, self.gain(PRIOR_G, H), self.prior_hidden
        )
        turn_into(self.prior_out_left, self.prior_hidden)

    def post(self):
        def one(j, carry):
            lanes = pl.ds(pl.multiple_of(j * 256, 256), 256)
            value = product(self.deter_low[...], self.post_in[0:H, lanes])
            self.post_normed[:, lanes] = value + product(
                self.embed[...], self.post_in[H : H + E, lanes]
            )
            return carry

        lax.fori_loop(0, H // 256, one, 0)
        hidden_rows(self.post_normed, self.post_inverse, self.gain(POST_G, H), self.post_hidden)
        turn_into(self.post_out_left, self.post_hidden)

    def logits(self, hidden_ref, weight_ref, turned_ref):
        matmul_into(self.wide, hidden_ref[...], weight_ref)
        turn_into(turned_ref, self.wide)

    def state_kl(self):
        scale_row = self.meta_turned[33:34, :] * (1.0 / ROWS)

        def log_part(value):
            shifted = value - jnp.max(value, 0, keepdims=True)
            return shifted - jnp.log(jnp.sum(jnp.exp(shifted), 0, keepdims=True))

        def one(rows, total):
            post_log = log_part(self.post_turned[rows, :])
            prior_log = log_part(self.prior_turned[rows, :])
            post = jnp.exp(post_log)
            gap = post_log - prior_log
            kl = jnp.sum(post * gap, 0, keepdims=True)
            self.post_turned[rows, :] = scale_row * post * (gap - kl)
            self.prior_turned[rows, :] = scale_row * (jnp.exp(prior_log) - post)
            return total + kl

        total = by_rows(Z, ZK, one, jnp.zeros((1, ROWS), F32))
        self.loss[...] += jnp.sum(scale_row * total, 1, keepdims=True)
        for turned, low in (
            (self.post_turned, self.post_out_right), (self.prior_turned, self.prior_out_right),
        ):
            for j in range(Z // LANES):
                lanes = slice(j * LANES, (j + 1) * LANES)
                low[:, lanes] = turned[lanes, :].T.astype(BF)

    def prior_back(self):
        matmul_into(self.wide, self.prior_out_right[...], self.prior_out, turned=True)
        total = hidden_rows_back(
            lambda rows: self.wide[rows, :],
            self.prior_normed, self.prior_inverse, self.gain(PRIOR_G, H), self.prior_right,
        )
        put_vector(self.small, PRIOR_G, total)
        self.add_back(self.prior_right, self.prior_in)

    def post_back(self):
        matmul_into(self.wide, self.post_out_right[...], self.post_out, turned=True)
        total = hidden_rows_back(
            lambda rows: self.wide[rows, :],
            self.post_normed, self.post_inverse, self.gain(POST_G, H), self.post_right,
        )
        put_vector(self.small, POST_G, total)
        self.add_back(self.post_right, self.post_in)
        matmul_into(self.embed_grad, self.post_right[...], self.post_in, turned=True, low=H)
        for y in range(2):
            for c in range(2):
                self.small[c, y, LOSS : LOSS + 1, :] = jnp.broadcast_to(
                    self.loss[...], (1, LANES)
                )


class Places:
    def __init__(self):
        dp, rep = (lax.axis_index("dp"), lax.axis_index("rep"))
        self.dp, self.rep = (dp, rep)
        self.x, self.z, self.w = (lax.rem(dp, 2), lax.rem(dp // 2, 2), dp // 4)
        self.y, self.c = (rep // 2, lax.rem(rep, 2))
        self.to_x = (dp + 1 - 2 * self.x, rep)
        self.to_z = (dp + 2 - 4 * self.z, rep)
        self.to_w = (dp + 4 - 8 * self.w, rep)
        self.to_y = (dp, rep + 2 - 4 * self.y)
        self.to_c = (dp, rep + 1 - 2 * self.c)
        self.to_d = (dp, 3 - rep)

    def around(self, offset):
        return lax.rem(self.dp + offset, 8)


def greet(devices):
    barrier = pltpu.get_barrier_semaphore()
    for device in devices:
        pl.semaphore_signal(barrier, inc=1, device_id=device, device_id_type=MESH)
    pl.semaphore_wait(barrier, len(devices))


def send_to(source, target, send_sem, recv_sem, device):
    return pltpu.make_async_remote_copy(
        src_ref=source,
        dst_ref=target,
        send_sem=send_sem,
        recv_sem=recv_sem,
        device_id=device,
        device_id_type=MESH,
    )


def regroup_start(places, outgoing, incoming, send_sem, recv_sem):
    count = ROWS // 8
    mine = pl.ds(pl.multiple_of(places.dp * count, 16), count)
    copies = []
    for offset in range(1, 8):
        there = places.around(offset)
        copy = send_to(
            outgoing.at[pl.ds(pl.multiple_of(there * count, 16), count)],
            incoming.at[mine],
            send_sem.at[offset],
            recv_sem.at[offset],
            (there, places.rep),
        )
        copy.start()
        copies.append(copy)
    incoming[mine, :] = outgoing[mine, :]
    return copies


def diagonal_split(quarter):
    over_y = quarter // 3 // 16 * 16
    over_x = (quarter - over_y) // 2 // 16 * 16
    over_z = quarter - over_y - over_x
    return (over_z, over_x, over_y) if over_y < over_z else (over_y, over_x, over_z)


OWN, Y_A, Y_B, X_A, Z_A, X_B, Z_B, RELAY = range(8)


class Gather:
    def __init__(self, places, units, send_sem, recv_sem, load_sem):
        self.places, self.units = (places, units)
        self.send_sem, self.recv_sem, self.load_sem = (send_sem, recv_sem, load_sem)
        self.far = places.rep + 2 - 4 * places.y
        self.mine = places.x * 2 + places.z
        self.across = 3 - self.mine
        self.from_x = (1 - places.x) * 2 + places.z
        self.from_z = places.x * 2 + 1 - places.z
        self.copies = {}
        self.loads = {}

    def remote(self, u, kind, source, target, device):
        copy = send_to(
            source, target, self.send_sem.at[u, kind], self.recv_sem.at[u, kind], device
        )
        copy.start()
        self.copies[u, kind] = copy

    def rows(self, u, share, piece, low, number):
        extent = self.units[u][0].shape[0]
        start = share * extent + piece * (extent // 4) + low
        return pl.ds(pl.multiple_of(start, 16), number)

    def part(self, u, rows, whole=True):
        share, all_rows, low, count = self.units[u]
        return (all_rows if whole else share).at[rows, pl.ds(low, count)]

    def extent(self, u):
        return self.units[u][0].shape[0]

    def load(self, u):
        everything = self.rows(u, 0, 0, 0, self.extent(u))
        copy = pltpu.make_async_copy(
            self.part(u, everything, False),
            self.part(u, self.rows(u, self.places.rep, 0, 0, self.extent(u))),
            self.load_sem.at[u],
        )
        copy.start()
        self.loads[u] = copy

    def over_y(self, u):
        if u >= len(self.units):
            return
        rep, quarter = (self.places.rep, self.extent(u) // 4)
        first = diagonal_split(quarter)[0]
        self.remote(
            u, Y_A,
            self.part(u, self.rows(u, 0, self.mine, 0, quarter), False),
            self.part(u, self.rows(u, rep, self.mine, 0, quarter)),
            self.places.to_y,
        )
        if first:
            self.remote(
                u, Y_B,
                self.part(u, self.rows(u, 0, self.across, 0, first), False),
                self.part(u, self.rows(u, rep, self.across, 0, first)),
                self.places.to_y,
            )
        everything = self.rows(u, 0, 0, 0, self.extent(u))
        self.remote(
            u, OWN,
            self.part(u, everything, False),
            self.part(u, self.rows(u, rep, 0, 0, self.extent(u))),
            self.places.to_c,
        )

    def stage_1(self, u):
        self.copies[u, Y_A].wait_recv()
        piece = self.part(u, self.rows(u, self.far, self.mine, 0, self.extent(u) // 4))
        self.remote(u, X_A, piece, piece, self.places.to_x)
        self.remote(u, Z_A, piece, piece, self.places.to_z)

    def stage_2(self, u):
        first, second, third = diagonal_split(self.extent(u) // 4)
        self.copies[u, Z_A].wait_recv()
        if second:
            piece = self.part(u, self.rows(u, self.far, self.from_z, first, second))
            self.remote(u, X_B, piece, piece, self.places.to_x)
        self.copies[u, X_A].wait_recv()
        if third:
            piece = self.part(u, self.rows(u, self.far, self.from_x, first + second, third))
            self.remote(u, Z_B, piece, piece, self.places.to_z)

    def stage_3(self, u):
        for kind in (Y_B, X_B, Z_B):
            if (u, kind) in self.copies:
                self.copies[u, kind].wait_recv()
        share = self.part(u, self.rows(u, self.far, 0, 0, self.extent(u)))
        self.remote(u, RELAY, share, share, self.places.to_c)

    def pump(self, t, ahead):
        count = len(self.units)
        if t < count:
            self.stage_1(t)
            self.over_y(t + ahead)
        if 0 <= t - 1 < count:
            self.stage_2(t - 1)
        if 0 <= t - 2 < count:
            self.stage_3(t - 2)

    def complete(self, u):
        self.loads[u].wait()
        self.copies[u, OWN].wait_recv()
        self.copies[u, RELAY].wait_recv()

    def drain(self):
        for copy in self.copies.values():
            copy.wait_send()


AHEAD = 3


def frames_kernel(f):
    places = Places()
    units = [(f.img_stoch_share, f.img_stoch, 0, H)]
    units += [(f.gru_weight_share, f.gru_weight, i * H, H) for i in range(3)]
    units += [
        (f.manager_in_share, f.manager_in, 0, U),
        (f.enc_in_share, f.enc_in, 0, U),
        (f.goal_out_share, f.goal_out, 0, H),
        (f.prior_in_share, f.prior_in, 0, H),
        (f.post_in_share, f.post_in, 0, U),
        (f.post_in_share, f.post_in, U, U),
        (f.prior_out_share, f.prior_out, 0, Z),
        (f.post_out_share, f.post_out, 0, Z),
        (f.actor_in_share, f.actor_in, 0, U),
        (f.critic_in_share, f.critic_in, 0, U),
    ]
    gather = Gather(places, units, f.piece_send, f.piece_recv, f.load_done)
    for u in range(len(units)):
        gather.load(u)
    greet(
        [(places.around(o), places.rep) for o in range(1, 8)]
        + [places.to_c, places.to_y, places.to_d]
    )
    packs = []
    for i, (share, whole) in enumerate(((f.vector_share, f.vectors), (f.table_share, f.tables))):
        for k, device in enumerate((places.to_c, places.to_y, places.to_d)):
            copy = send_to(
                share, whole.at[places.rep], f.small_send.at[i, k], f.small_recv.at[i, k], device
            )
            copy.start()
            packs.append(copy)
    for u in range(AHEAD):
        gather.over_y(u)
    f.vectors[places.rep] = f.vector_share[...]
    f.tables[places.rep] = f.table_share[...]
    f.start()
    saves = []

    def save(k, source, target):
        copy = pltpu.make_async_copy(source, target, f.save_done.at[k])
        copy.start()
        saves.append(copy)

    def pump(t):
        gather.pump(t, AHEAD)

    pump(0)
    pump(1)
    pump(2)
    for copy in packs:
        copy.wait()
    f.unpack()
    gather.complete(0)
    f.img()
    for third in range(3):
        pump(3 + third)
        gather.complete(1 + third)
        f.gru(third)
    save(0, f.gru_weight, f.gru_weight_out)
    f.state()
    f.picked()
    states = regroup_start(places, f.outgoing, f.incoming, f.state_send, f.state_recv)
    pump(6)
    gather.complete(4)
    f.manager()
    pump(7)
    gather.complete(5)
    pump(8)
    gather.complete(6)
    save(1, f.goal_out, f.goal_out_out)
    f.encoder()
    pump(9)
    gather.complete(7)
    f.prior()
    pump(10)
    pump(11)
    gather.complete(8)
    gather.complete(9)
    f.post()
    pump(12)
    gather.complete(10)
    f.logits(f.prior_hidden, f.prior_out, f.prior_turned)
    pump(13)
    gather.complete(11)
    f.logits(f.post_hidden, f.post_out, f.post_turned)
    pump(14)
    f.state_kl()
    pump(15)
    f.prior_back()
    for copy in states:
        copy.wait()
    f.start_state[...] = f.incoming[...]
    gather.complete(12)
    save(2, f.actor_in, f.actor_in_out)
    gather.complete(13)
    save(3, f.critic_in, f.critic_in_out)
    f.post_back()
    for copy in saves:
        copy.wait()
    gather.drain()


class Worker(NamedTuple):
    meta: Any = taken(ROWS, LANES, dtype=F32)
    samples: Any = taken(HOR, ROWS, ZG, dtype=F32)
    vectors: Any = taken(4, VECTOR_TILES, LANES, dtype=F32)
    tables: Any = taken(4, TABLES, LANES)
    start_state: Any = taken(ROWS, H + LANES)
    goal_out: Any = taken(U, H)
    actor_in: Any = taken(3 * H, U)
    critic_in: Any = taken(3 * H, U)
    worker_left: Any = given(3 * H, 2 * U)
    returned: Any = given(ROWS, H)
    goal_left: Any = given(U, ROWS)
    code_turned: Any = given(GCODE, ROWS)
    goal_right: Any = given(ROWS, H)
    goal_pair: Any = given(ROWS, 2 * U)
    small: Any = given(2, 2, SMALL_TILES, LANES, dtype=F32)
    act_out: Any = kept(32, U)
    goal_in: Any = kept(GCODE, U)
    goal_normed: Any = kept(ROWS, U, dtype=F32)
    goal_inverse: Any = kept(ROWS, 1, dtype=F32)
    goal_hidden: Any = kept(ROWS, U)
    goal_pre: Any = kept(ROWS, U)
    goal_low: Any = kept(ROWS, H)
    turned: Any = kept(2 * H, ROWS)
    slot_part: Any = kept(2, ROWS, U, dtype=F32)
    normed: Any = kept(2, HOR * ROWS, U, dtype=F32)
    inverse: Any = kept(2, HOR * ROWS, 1, dtype=F32)
    hidden: Any = kept(2, HOR * ROWS, U)
    hot_turned: Any = kept(Z, HOR * ROWS)
    log_chance: Any = kept(HOR * ROWS, 32, dtype=F32)
    chosen: Any = kept(HOR, ROWS, 1, dtype=F32)
    value: Any = kept(HOR, ROWS, 1, dtype=F32)
    returns: Any = kept(HOR, ROWS, 1, dtype=F32)
    pre: Any = kept(HOR * ROWS, U, dtype=F32)
    pre_pair: Any = kept(HOR * ROWS, 2 * U)
    summed: Any = kept(2, ROWS, U, dtype=F32)
    sum_low: Any = kept(2, ROWS, U)
    sum_pair: Any = kept(ROWS, 2 * U)
    to_state: Any = kept(ROWS, H)
    incoming: Any = kept(ROWS, H)
    wide: Any = kept(ROWS, H, dtype=F32)
    wide_512: Any = kept(ROWS, U, dtype=F32)
    top: Any = kept(8, LANES, dtype=F32)
    top_in: Any = kept(5, 8, LANES, dtype=F32)
    top_send: Any = signal(5)
    top_recv: Any = signal(5)
    state_send: Any = signal(8)
    state_recv: Any = signal(8)

    def gain(self, low, size):
        return vector_of(self.vectors, low, size // (4 * LANES))

    def goal(self):
        self.small[...] = jnp.zeros(self.small.shape, F32)
        for r in range(4):
            self.act_out[:, r * LANES : (r + 1) * LANES] = self.tables[
                r, TAB_ACT : TAB_ACT + 32, :
            ]
            for i in range(4):
                self.goal_in[16 * r : 16 * (r + 1), i * LANES : (i + 1) * LANES] = self.tables[
                    r, TAB_GOAL + 16 * i : TAB_GOAL + 16 * (i + 1), :
                ]
        hot = hot_rows(self.meta[:, 0:32], GK, GC, LANES)
        self.code_turned[...] = hot.T[0:GCODE].astype(BF)
        matmul_into(self.goal_normed, hot[:, 0:GCODE].astype(BF), self.goal_in)
        hidden_rows(
            self.goal_normed, self.goal_inverse, self.gain(GOAL_G, U), self.goal_hidden
        )
        turn_into(self.goal_left, self.goal_hidden)

        def one(j, totals):
            lanes = pl.ds(pl.multiple_of(j * 256, 256), 256)
            goal = product(self.goal_hidden[...], self.goal_out[:, lanes])
            state = self.start_state[:, lanes].astype(F32)
            self.goal_low[:, lanes] = goal.astype(BF)
            terms = (goal * state, goal * goal, state * state)
            return tuple(
                t + jnp.sum(term, -1, keepdims=True) for t, term in zip(totals, terms)
            )

        zero = jnp.zeros((ROWS, 1), F32)
        aligned, goal_square, state_square = lax.fori_loop(0, H // 256, one, (zero,) * 3)
        turn_into(self.turned, self.start_state.at[:, 0:H])
        turn_into(self.turned, self.goal_low, H)
        return aligned / (jnp.maximum(goal_square, state_square) + small_floor)

    def slots(self):
        for which, weight in enumerate((self.actor_in, self.critic_in)):
            def one(j, carry):
                lanes = pl.ds(pl.multiple_of(j * 256, 256), 256)
                self.slot_part[which, :, lanes] = product(
                    self.start_state[:, 0:H], weight[0:H, lanes]
                ) + product(self.goal_low[...], weight[2 * H : 3 * H, lanes])
                return carry

            lax.fori_loop(0, U // 256, one, 0)

    def forward(self):
        gains = (self.gain(ACT_G, U), self.gain(CRI_G, U))
        head = self.gain(CRI_O, U)
        spread = class_spread(ZG, ZK, ZG, Z)
        lane = lax.broadcasted_iota(jnp.int32, (1, Z), 1)
        lane_class = jnp.bitwise_and(lane, ZK - 1).astype(F32)
        group = lax.broadcasted_iota(jnp.int32, (Z, LANES), 1)
        place = lax.broadcasted_iota(jnp.int32, (Z, LANES), 0)
        inside = (place >= group * ZK) & (place < group * ZK + ZK) & (group < ZG)
        spread_turned = jnp.where(inside, 1.0, 0.0).astype(BF)
        place_class = jnp.bitwise_and(
            lax.broadcasted_iota(jnp.int32, (Z, 1), 0), ZK - 1
        ).astype(F32)
        act_lane = lax.broadcasted_iota(jnp.int32, (1, 32), 1)

        def step(k, carry):
            rows = pl.ds(pl.multiple_of(k * ROWS, ROWS), ROWS)
            ids = self.samples[k]
            hot = jnp.where(product(ids.astype(BF), spread) == lane_class, 1.0, 0.0).astype(BF)
            ids_turned = jnp.concatenate(
                [ids, jnp.zeros((ROWS, LANES - ZG), F32)], 1
            ).T.astype(BF)
            self.hot_turned[:, rows] = jnp.where(
                product(spread_turned, ids_turned) == place_class, 1.0, 0.0
            ).astype(BF)
            for which, weight in enumerate((self.actor_in, self.critic_in)):
                pre = product(hot, weight[H : 2 * H, :]) + self.slot_part[which]
                normed, inverse = normalize(pre)
                self.normed[which, rows, :] = normed
                self.inverse[which, rows, :] = inverse
                hidden = elu_of(normed * gains[which]).astype(BF)
                self.hidden[which, rows, :] = hidden
                if which == 0:
                    logits = lax.dot_general(
                        hidden, self.act_out[...], (((1,), (1,)), ((), ())),
                        preferred_element_type=F32,
                    )
                    logits = jnp.where(act_lane < NA, logits, -1e30)
                    shifted = logits - jnp.max(logits, -1, keepdims=True)
                    total = jnp.sum(jnp.exp(shifted), -1, keepdims=True)
                    log_chance = shifted - jnp.log(total)
                    self.log_chance[rows, :] = log_chance
                    self.chosen[k] = jnp.sum(
                        jnp.where(self.action_here(k), log_chance, 0.0), -1, keepdims=True
                    )
                else:
                    self.value[k] = jnp.sum(hidden.astype(F32) * head, -1, keepdims=True)
            return carry

        lax.fori_loop(0, HOR, step, 0)

    def action_here(self, k):
        meta = self.meta[...]
        lane = lax.broadcasted_iota(jnp.int32, (ROWS, LANES), 1)
        action = jnp.sum(jnp.where(lane == 32 + k, meta, 0.0), -1, keepdims=True)
        return action == lax.broadcasted_iota(jnp.int32, (1, 32), 1).astype(F32)

    def targets(self, reward):
        weight = self.start_state[:, H : H + 1].astype(F32)
        later = self.value[HOR - 1]
        self.returns[HOR - 1] = later
        result = later
        top = jnp.zeros((ROWS, 1), F32)
        for k in range(HOR - 2, -1, -1):
            blended = (1.0 - return_mix) * later + return_mix * result
            result = reward + discount * blended
            self.returns[k] = result
            later = self.value[k]
            top = jnp.maximum(top, weight * jnp.abs(result - later))
        self.top[...] = jnp.broadcast_to(jnp.max(top, 0, keepdims=True), (8, LANES))

    def critic_back(self, first, last, total):
        gain, head = (self.gain(CRI_G, U), self.gain(CRI_O, U))
        weight = self.start_state[:, H : H + 1].astype(F32)

        def step(k, totals):
            rows = pl.ds(pl.multiple_of(k * ROWS, ROWS), ROWS)
            grad = weight * (self.value[k] - self.returns[k]) * (1.0 / (ROWS * HOR))
            self.wide_512[...] = grad * head
            head_total = totals[1] + jnp.sum(
                self.hidden[1, rows, :].astype(F32) * grad, 0, keepdims=True
            )
            gain_total = totals[0] + hidden_rows_back(
                lambda r: self.wide_512[r, :],
                self.normed.at[1, rows], self.inverse.at[1, rows], gain, self.pre.at[rows],
                64,
            )
            low = self.pre[rows, :].astype(BF).astype(F32)
            self.pre[rows, :] = low
            self.summed[1] += low
            return (gain_total, head_total)

        return lax.fori_loop(first, last, step, total)

    def pair(self, first, second, out_ref, rows):
        lane = lax.broadcasted_iota(jnp.int32, (ROWS, LANES), 1)
        for j in range(4):
            lanes = slice(j * LANES, (j + 1) * LANES)
            a, b = (first[:, lanes], second[:, lanes])
            out_ref[rows, 2 * j * LANES : (2 * j + 1) * LANES] = jnp.where(
                lane < 64, a, pltpu.roll(b, 64, 1)
            ).astype(BF)
            out_ref[rows, (2 * j + 1) * LANES : (2 * j + 2) * LANES] = jnp.where(
                lane < 64, pltpu.roll(a, 64, 1), b
            ).astype(BF)

    def actor_back(self):
        gain = self.gain(ACT_G, U)
        weight = self.start_state[:, H : H + 1].astype(F32)
        scale = self.top[0:1, 0:1] + small_floor

        def step(k, totals):
            rows = pl.ds(pl.multiple_of(k * ROWS, ROWS), ROWS)
            advantage = self.returns[k] - self.value[k]
            chosen_grad = -weight * advantage / scale * (1.0 / (ROWS * HOR))
            hot = jnp.where(self.action_here(k), 1.0, 0.0)
            grad = chosen_grad * (hot - jnp.exp(self.log_chance[rows, :]))
            grad_low = grad.astype(BF)
            grad_turned = jnp.concatenate(
                [grad, jnp.zeros((ROWS, LANES - 32), F32)], 1
            ).T[0:32].astype(BF)
            out_total = totals[1] + product(grad_turned, self.hidden[0, rows, :])
            self.wide_512[...] = product(grad_low, self.act_out[...])
            gain_total = totals[0] + hidden_rows_back(
                lambda r: self.wide_512[r, :],
                self.normed.at[0, rows], self.inverse.at[0, rows], gain,
                self.normed.at[0, rows], 64,
            )
            low = self.normed[0, rows, :].astype(BF).astype(F32)
            self.summed[0] += low
            self.pair(low, self.pre[rows, :], self.pre_pair, rows)
            loss = totals[2] + jnp.sum(
                weight * self.chosen[k] * advantage / scale, 0, keepdims=True
            )
            return (gain_total, out_total, loss)

        start = (jnp.zeros((1, U), F32), jnp.zeros((32, U), F32), jnp.zeros((1, 1), F32))
        return lax.fori_loop(0, HOR, step, start)

    def inputs_back(self, low, out_ref):
        def one(j, carry):
            rows = pl.ds(pl.multiple_of(low + j * 256, 256), 256)
            total = 0.0
            for which, weight in enumerate((self.actor_in, self.critic_in)):
                total = total + lax.dot_general(
                    self.sum_low[which], weight[rows, :], (((1,), (1,)), ((), ())),
                    preferred_element_type=F32,
                )
            out_ref[:, pl.ds(pl.multiple_of(j * 256, 256), 256)] = total.astype(BF)
            return carry

        lax.fori_loop(0, H // 256, one, 0)

    def goal_back(self):
        matmul_into(self.wide_512, self.goal_right[...], self.goal_out, turned=True)
        total = hidden_rows_back(
            lambda rows: self.wide_512[rows, :],
            self.goal_normed, self.goal_inverse, self.gain(GOAL_G, U), self.goal_pre,
        )
        put_vector(self.small, GOAL_G, total)
        spread_lanes(self.goal_pre, self.goal_pair, 0, 0)

    def weights(self):
        def one(j, carry):
            lanes = pl.ds(pl.multiple_of(j * 256, 256), 256)
            self.worker_left[H : 2 * H, lanes] = product(
                self.hot_turned[...], self.pre_pair[:, lanes]
            ).astype(BF)
            pair = self.sum_pair[:, lanes]
            self.worker_left[0:H, lanes] = product(self.turned[0:H], pair).astype(BF)
            self.worker_left[2 * H : 3 * H, lanes] = product(
                self.turned[H : 2 * H], pair
            ).astype(BF)
            return carry

        lax.fori_loop(0, 2 * U // 256, one, 0)


def worker_kernel(f):
    places = Places()
    peers = (places.to_c, places.to_y, places.to_x, places.to_z, places.to_w)
    greet(
        [(places.around(o), places.rep) for o in range(1, 8)] + [places.to_c, places.to_y]
    )
    reward = f.goal()
    f.slots()
    f.forward()
    f.targets(reward)
    f.summed[...] = jnp.zeros(f.summed.shape, F32)
    totals = (jnp.zeros((1, U), F32), jnp.zeros((1, U), F32))
    steps = (0, 3, 6, 9, 12, HOR)
    for k in range(5):
        copy = send_to(f.top, f.top_in.at[k], f.top_send.at[k], f.top_recv.at[k], peers[k])
        copy.start()
        totals = f.critic_back(steps[k], steps[k + 1], totals)
        copy.wait()
        f.top[...] = jnp.maximum(f.top[...], f.top_in[k])
    put_vector(f.small, CRI_G, totals[0])
    put_vector(f.small, CRI_O, totals[1])
    actor_gain, actor_out, chosen = f.actor_back()
    put_vector(f.small, ACT_G, actor_gain)
    put_table(f.small, ACT_T, actor_out, 24)
    weight = f.start_state[:, H : H + 1].astype(F32)
    squares = jnp.zeros((ROWS, 1), F32)
    for k in range(HOR):
        misfit = f.value[k] - f.returns[k]
        squares = squares + misfit * misfit
    loss = (0.5 * jnp.sum(weight * squares, 0, keepdims=True) - chosen) * (1.0 / (ROWS * HOR))
    for y in range(2):
        for c in range(2):
            f.small[c, y, LOSS : LOSS + 1, :] = jnp.broadcast_to(loss, (1, LANES))
    for which in range(2):
        f.sum_low[which] = f.summed[which].astype(BF)
    everything = pl.ds(0, ROWS)
    f.pair(f.sum_low[0].astype(F32), f.sum_low[1].astype(F32), f.sum_pair, everything)
    f.inputs_back(0, f.to_state)
    states = regroup_start(places, f.to_state, f.incoming, f.state_send, f.state_recv)
    f.inputs_back(2 * H, f.goal_right)
    f.goal_back()
    f.weights()
    for copy in states:
        copy.wait()
    f.returned[...] = f.incoming[...]


class Back(NamedTuple):
    meta: Any = taken(ROWS, LANES, dtype=F32)
    prev: Any = taken(ROWS, H)
    vectors: Any = taken(4, VECTOR_TILES, LANES, dtype=F32)
    gru_weight: Any = taken(2 * H, 3 * H)
    returned: Any = taken(ROWS, H)
    grad_partial: Any = taken(ROWS, H, dtype=F32)
    gru_normed: Any = taken(ROWS, 3 * H, dtype=F32)
    gru_inverse: Any = taken(ROWS, 1, dtype=F32)
    img_normed: Any = taken(ROWS, H, dtype=F32)
    img_inverse: Any = taken(ROWS, 1, dtype=F32)
    small_1: Any = taken(2, 2, SMALL_TILES, LANES, dtype=F32)
    small_2: Any = taken(2, 2, SMALL_TILES, LANES, dtype=F32)
    deter_grad: Any = given(ROWS, H, dtype=F32)
    gru_right: Any = given(ROWS, 3 * H)
    img_right: Any = given(ROWS, H)
    small: Any = given(2, 2, SMALL_TILES, LANES, dtype=F32)
    grad: Any = kept(ROWS, H, dtype=F32)
    wide: Any = kept(ROWS, 2 * H, dtype=F32)


def back_kernel(f):
    f.small[...] = f.small_1[...] + f.small_2[...]
    gain = vector_of(f.vectors, GRU_G, 6)
    meta = f.meta[...]
    lane = lax.broadcasted_iota(jnp.int32, (ROWS, LANES), 1)
    order = jnp.where(lane == 37, meta, 0.0).T[37:38, :]
    frame = lax.broadcasted_iota(jnp.int32, (ROWS, ROWS), 0).astype(F32)
    place = jnp.where(order == frame, 1.0, 0.0).astype(BF)

    def add(j, carry):
        lanes = pl.ds(pl.multiple_of(j * 256, 256), 256)
        f.grad[:, lanes] = f.grad_partial[:, lanes] + product(place, f.returned[:, lanes])
        return carry

    lax.fori_loop(0, H // 256, add, 0)

    def one(rows, total):
        normed = f.gru_normed[rows, :]
        parts = normed * gain
        inner = parts[:, H : 2 * H]
        reset = 1.0 / (1.0 + jnp.exp(-parts[:, :H]))
        candidate = jnp.tanh(reset * inner)
        update = 1.0 / (1.0 + jnp.exp(1.0 - parts[:, 2 * H :]))
        grad = f.grad[rows, :]
        prev = f.prev[rows, :].astype(F32)
        grad_inner = grad * update * (1.0 - candidate * candidate)
        grad_parts = jnp.concatenate(
            [
                grad_inner * inner * reset * (1.0 - reset),
                grad_inner * reset,
                grad * (candidate - prev) * update * (1.0 - update),
            ],
            1,
        )
        f.deter_grad[rows, :] = grad * (1.0 - update)
        total = total + jnp.sum(grad_parts * normed, 0, keepdims=True)
        back = normalize_back(grad_parts * gain, normed, f.gru_inverse[rows, :])
        f.gru_right[rows, :] = back.astype(BF)
        return total

    put_vector(f.small, GRU_G, by_rows(ROWS, 16, one, jnp.zeros((1, 3 * H), F32)))
    matmul_into(f.wide, f.gru_right[...], f.gru_weight, turned=True)
    f.deter_grad[...] += f.wide[:, H : 2 * H]
    total = hidden_rows_back(
        lambda rows: f.wide[rows, 0:H],
        f.img_normed, f.img_inverse, vector_of(f.vectors, IMG_G, 2), f.img_right,
    )
    put_vector(f.small, IMG_G, total)
    lane = lax.broadcasted_iota(jnp.int32, (ROWS, LANES), 1)
    action = jnp.sum(jnp.where(lane == 32, meta, 0.0), -1, keepdims=True)
    hot = jnp.where(action == lane.astype(F32), 1.0, 0.0).T[0:24].astype(BF)
    for r in range(4):
        for i in range(2):
            start = (2 * r + i) * LANES
            f.small[r % 2, r // 2, IMG_T + 24 * i : IMG_T + 24 * (i + 1), :] = product(
                hot, f.img_right[:, start : start + LANES]
            )


class Source(NamedTuple):
    rows: int
    parts: Any
    columns: int

    @property
    def depth(self):
        return sum(self.parts)


GRU, POST, PRIOR, POST_OUT, PRIOR_OUT, IMG, MAN_ENC, GOAL_OUT, GOAL_IN, WORKER = range(10)
SOURCES = (
    Source(512, (ROWS,), 3072),
    Source(640, (ROWS,), 1024),
    Source(256, (ROWS,), 1024),
    Source(256, (ROWS,), 1024),
    Source(256, (ROWS,), 1024),
    Source(256, (ROWS,), 1024),
    Source(256, (2 * ROWS,), 1024),
    Source(128, (ROWS, ROWS), 1024),
    Source(16, (ROWS, ROWS), 1024),
)
WORKER_SHARE = (768, 1024)
ALONG_X, ALONG_Z, ALONG_W, ALONG_Y = range(4)
Y_FIRST = (ALONG_Y, ALONG_X, ALONG_Z, ALONG_W)
X_FIRST = (ALONG_X, ALONG_Z, ALONG_Y, ALONG_W)
Z_FIRST = (ALONG_Z, ALONG_Y, ALONG_X, ALONG_W)
UNITS = (
    (POST, 128, 0, Y_FIRST),
    (WORKER, 128, 0, X_FIRST),
    (POST_OUT, 128, 0, Z_FIRST),
    (GRU, 384, 0, Y_FIRST),
    (GRU, 384, 128, X_FIRST),
    (GRU, 384, 256, Z_FIRST),
    (PRIOR_OUT, 128, 0, Y_FIRST),
    (IMG, 128, 0, X_FIRST),
    (PRIOR, 128, 0, Z_FIRST),
    (MAN_ENC, 128, 0, Y_FIRST),
    (GOAL_OUT, 128, 0, X_FIRST),
    (GOAL_IN, 128, 0, Z_FIRST),
)


def unit_rows(unit):
    return WORKER_SHARE[0] if unit[0] == WORKER else SOURCES[unit[0]].rows


def reduce_kernel(*refs):
    count, units = (len(SOURCES), len(UNITS))
    parts = sum(len(source.parts) for source in SOURCES)
    refs = iter(refs)

    def take(number):
        return [next(refs) for _ in range(number)]

    left_parts, right_parts = (take(parts), take(parts))
    worker, small = take(2)
    outs, (small_out,) = (take(units), take(1))
    left_2, right_2 = (take(count), take(count))
    worker_own, worker_sib = take(2)
    outbox = [take(4) for _ in range(units)]
    inbox = [take(4) for _ in range(units)]
    small_in = take(5)
    ex_send, ex_recv, wk_send, wk_recv, wk_local, st_send, st_recv, sm_send, sm_recv = take(9)
    places = Places()
    core = places.c
    bits = (places.x, places.z, places.w, places.y)
    peers = (places.to_x, places.to_z, places.to_w, places.to_y)
    greet((places.to_c,) + peers)
    exchange, own = ([], [])
    part = 0
    for s, source in enumerate(SOURCES):
        group, low = ([], 0)
        for depth in source.parts:
            left, right = (left_parts[part], right_parts[part])
            high = source.depth + low
            group.append(
                send_to(
                    right, right_2[s].at[pl.ds(high, depth)],
                    ex_send.at[part, 0], ex_recv.at[part, 0], places.to_c,
                )
            )
            for y in range(2):
                start = (2 * y + 1 - core) * source.rows
                group.append(
                    send_to(
                        left.at[pl.ds(pl.multiple_of(start, 16), source.rows)],
                        left_2[s].at[y, :, pl.ds(high, depth)],
                        ex_send.at[part, 1 + y], ex_recv.at[part, 1 + y], places.to_c,
                    )
                )
            own.append((s, left, right, low, depth))
            low += depth
            part += 1
        exchange.append(group)
    group = []
    for y in range(2):
        theirs = pl.ds(pl.multiple_of((2 * y + 1 - core) * WORKER_SHARE[0], 16), WORKER_SHARE[0])
        ours = pl.ds(pl.multiple_of((2 * y + core) * WORKER_SHARE[0], 16), WORKER_SHARE[0])
        group.append(
            send_to(worker.at[theirs], worker_sib.at[y], wk_send.at[y], wk_recv.at[y], places.to_c)
        )
        group.append(pltpu.make_async_copy(worker.at[ours], worker_own.at[y], wk_local.at[y]))
    exchange.append(group)
    for unit in UNITS:
        for copy in exchange[unit[0]] if unit[2] == 0 else ():
            copy.start()
    for s, left, right, low, depth in own:
        right_2[s][low : low + depth] = right[...]
        for y in range(2):
            start = pl.multiple_of((2 * y + core) * SOURCES[s].rows, 16)
            left_2[s][y, :, low : low + depth] = left[pl.ds(start, SOURCES[s].rows)]
    arrived = set()

    def term(u, y, device):
        s, stride, offset, _ = UNITS[u]
        lanes = pl.ds(pl.multiple_of(device * stride + offset, LANES), LANES)
        if s == WORKER:
            return worker_own[y, :, lanes].astype(F32) + worker_sib[y, :, lanes].astype(F32)
        return product(left_2[s][y], right_2[s][:, lanes])

    def block(u, k, j):
        order = UNITS[u][3]
        place = {}
        for i, along in enumerate(order):
            if i < k:
                place[along] = bits[along]
            elif i == k:
                place[along] = 1 - bits[along]
            else:
                place[along] = lax.rem(j // (1 << (3 - i)), 2)
        device = place[ALONG_W] * 4 + place[ALONG_Z] * 2 + place[ALONG_X]
        total = term(u, place[ALONG_Y], device)
        for i in range(k):
            index = 0
            for p in range(i + 1, 4):
                index = index * 2 + place[order[p]]
            total = total + inbox[u][i][index].astype(F32)
        return total

    started = {}

    def step(u, k):
        s = UNITS[u][0]
        if s not in arrived:
            arrived.add(s)
            for copy in exchange[s]:
                copy.wait()
        if k > 0:
            started[u, k - 1].wait_recv()

        def one(j, carry):
            outbox[u][k][j] = block(u, k, j).astype(BF)
            return carry

        if k == 3:
            one(0, 0)
        else:
            lax.fori_loop(0, 1 << (3 - k), one, 0)
        copy = send_to(
            outbox[u][k], inbox[u][k], st_send.at[u, k], st_recv.at[u, k], peers[UNITS[u][3][k]]
        )
        copy.start()
        started[u, k] = copy

    small_copies = []

    def small_step(k):
        if k > 0:
            small_copies[k - 1].wait()
        if k == 0:
            source, target, device = (small.at[1 - core], small_in[0], places.to_c)
        elif k == 1:
            small_in[0][...] = small_in[0][...] + small[core]
            source, target, device = (small_in[0].at[1 - places.y], small_in[1], places.to_y)
        else:
            if k == 2:
                small_out[...] = small_in[0][places.y] + small_in[1][...]
            else:
                small_out[...] = small_out[...] + small_in[k - 1][...]
            if k == 5:
                return
            source, target, device = (small_out, small_in[k], peers[k - 2])
        copy = send_to(source, target, sm_send.at[k], sm_recv.at[k], device)
        copy.start()
        small_copies.append(copy)

    small_step(0)
    for k in range(4):
        for u in range(units):
            step(u, k)
        small_step(k + 1)
    for u in range(units):
        started[u, 3].wait_recv()
        outs[u][...] = block(u, 4, 0)
    small_step(5)
    for copy in started.values():
        copy.wait_send()


def reduce_call(left, right, worker, small):
    vmem, dma = (pltpu.VMEM, pltpu.SemaphoreType.DMA)
    parts, units = (len(left), len(UNITS))
    scratch = [vmem((2, s.rows, 2 * s.depth), BF) for s in SOURCES]
    scratch += [vmem((2 * s.depth, s.columns), BF) for s in SOURCES]
    scratch += [vmem((2,) + WORKER_SHARE, BF)] * 2
    for _ in range(2):
        for unit in UNITS:
            scratch += [vmem((1 << (3 - k), unit_rows(unit), LANES), BF) for k in range(4)]
    scratch += [vmem((2, SMALL_TILES, LANES), F32)] + [vmem((SMALL_TILES, LANES), F32)] * 4
    scratch += [dma((parts, 3))] * 2 + [dma((2,))] * 3 + [dma((units, 4))] * 2 + [dma((5,))] * 2
    whole = pl.BlockSpec(memory_space=vmem)
    anywhere = pl.BlockSpec(memory_space=pl.ANY)
    out = pl.pallas_call(
        reduce_kernel,
        out_shape=[jax.ShapeDtypeStruct((unit_rows(unit), LANES), F32) for unit in UNITS]
        + [jax.ShapeDtypeStruct((SMALL_TILES, LANES), F32)],
        in_specs=[whole] * (2 * parts) + [anywhere, whole],
        out_specs=[whole] * (units + 1),
        scratch_shapes=scratch,
        compiler_params=pltpu.CompilerParams(
            collective_id=2, has_side_effects=True, vmem_limit_bytes=VMEM_BYTES
        ),
        name="reduce",
    )(*left, *right, worker, small)
    large = {}
    for (source, _, _, _), value in zip(UNITS, out):
        large.setdefault(source, []).append(value)
    return (large, out[units])


class Weights(NamedTuple):
    obs_gain: Any = None
    manager_in: Any = None
    manager_gain: Any = None
    manager_out: Any = None
    goal_in: Any = None
    goal_gain: Any = None
    goal_out: Any = None
    actor_in: Any = None
    actor_gain: Any = None
    actor_out: Any = None
    critic_in: Any = None
    critic_gain: Any = None
    critic_out: Any = None
    img_stoch: Any = None
    img_action: Any = None
    img_gain: Any = None
    gru_weight: Any = None
    gru_gain: Any = None
    post_in: Any = None
    post_gain: Any = None
    post_out: Any = None
    prior_in: Any = None
    prior_gain: Any = None
    prior_out: Any = None
    enc_in: Any = None
    enc_gain: Any = None
    enc_out: Any = None


class Data(NamedTuple):
    deter_states: Any
    embed: Any
    lengths: Any
    resets: Any
    terminal: Any
    rewards: Any
    prev_stoch: Any
    prev_action: Any
    regroup: Any
    goal_codes: Any
    samples: Any
    actions: Any


def vectors_in_order(w):
    return (
        w.obs_gain, w.manager_gain, w.manager_out, w.goal_gain, w.actor_gain, w.critic_gain,
        w.critic_out, w.img_gain, w.gru_gain, w.post_gain, w.prior_gain, w.enc_gain,
    )


def step_in_kernels(data, w):
    positions = lax.broadcasted_iota(jnp.int32, (SEQ_DEV, LEN), 1)
    is_valid = positions < data.lengths[:, None]
    next_valid = jnp.concatenate([is_valid[:, 1:], jnp.zeros((SEQ_DEV, 1), jnp.bool_)], 1)
    next_reset = jnp.concatenate([data.resets[:, 1:], jnp.ones((SEQ_DEV, 1), jnp.int32)], 1)
    columns = (
        data.prev_action, is_valid, next_valid & (next_reset == 0), 1 - data.terminal,
        data.rewards, data.regroup,
    )
    meta = jnp.concatenate(
        [data.prev_stoch.reshape(ROWS, ZG).astype(F32)]
        + [value.reshape(ROWS, 1).astype(F32) for value in columns]
        + [jnp.zeros((ROWS, LANES - ZG - 6), F32)],
        1,
    )
    slot_meta = jnp.concatenate(
        [
            data.goal_codes.astype(F32), jnp.zeros((ROWS, 32 - GC), F32),
            data.actions.astype(F32), jnp.zeros((ROWS, LANES - 32 - HOR), F32),
        ],
        1,
    )
    samples = data.samples.transpose(1, 0, 2).astype(F32)
    vectors = jnp.concatenate([v.astype(F32).reshape(-1, LANES) for v in vectors_in_order(w)], 0)
    vectors = jnp.pad(vectors, ((0, VECTOR_TILES - vectors.shape[0]), (0, 0)))
    tables = jnp.concatenate(
        [
            jnp.pad(w.actor_out.T, ((0, 32 - NA), (0, 0))),
            w.enc_out.T,
            jnp.pad(w.img_action[:, :LANES], ((0, 32 - NA), (0, 0))),
            jnp.pad(w.img_action[:, LANES:], ((0, 32 - NA), (0, 0))),
        ]
        + [w.goal_in[:, i * LANES : (i + 1) * LANES] for i in range(4)],
        0,
    )
    prev = data.deter_states.reshape(ROWS, H)
    f = run_kernel(
        frames_kernel, Frames(),
        (
            meta, prev, data.embed.reshape(ROWS, E), vectors, tables, w.img_stoch, w.gru_weight,
            w.manager_in, w.enc_in, w.goal_out, w.prior_in, w.post_in, w.prior_out, w.post_out,
            w.actor_in, w.critic_in,
        ),
        "frames", 0,
    )
    s = run_kernel(
        worker_kernel, Worker(),
        (
            slot_meta, samples, f.vectors, f.tables, f.start_state, f.goal_out_out,
            f.actor_in_out, f.critic_in_out,
        ),
        "worker", 1,
    )
    b = run_kernel(
        back_kernel, Back(),
        (
            meta, prev, f.vectors, f.gru_weight_out, s.returned, f.grad_deter, f.gru_normed,
            f.gru_inverse, f.img_normed, f.img_inverse, f.small, s.small,
        ),
        "back",
    )
    large, small = reduce_call(
        (
            f.gru_left, f.post_left, f.post_left, f.post_out_left, f.prior_out_left, f.img_left,
            f.me_left, s.goal_left, f.dec_left, s.code_turned, f.soft_turned,
        ),
        (
            b.gru_right, f.post_right, f.prior_right, f.post_out_right, f.prior_out_right,
            b.img_right, f.me_right, s.goal_right, f.recon_low, s.goal_pair, f.dec_pair,
        ),
        s.worker_left, b.small,
    )

    def vector(low, tiles):
        return small[low : low + tiles].reshape(-1)

    man_enc, worker = (large[MAN_ENC][0], large[WORKER][0])
    out = Weights(
        obs_gain=vector(OBS, 2), manager_gain=vector(MAN_G, 1), manager_out=vector(MAN_O, 1),
        goal_gain=vector(GOAL_G, 1), actor_gain=vector(ACT_G, 1), critic_gain=vector(CRI_G, 1),
        critic_out=vector(CRI_O, 1), img_gain=vector(IMG_G, 2), gru_gain=vector(GRU_G, 6),
        post_gain=vector(POST_G, 2), prior_gain=vector(PRIOR_G, 2), enc_gain=vector(ENC_G, 1),
        actor_out=small[ACT_T : ACT_T + NA].T, enc_out=small[ENC_T : ENC_T + GCODE].T,
        img_action=jnp.concatenate(
            [small[IMG_T : IMG_T + NA], small[IMG_T + 24 : IMG_T + 24 + NA]], 1
        ),
        manager_in=man_enc[:, :64], enc_in=man_enc[:, 64:],
        actor_in=worker[:, :64], critic_in=worker[:, 64:],
        goal_in=large[GOAL_IN][0][:, :64], goal_out=large[GOAL_OUT][0],
        img_stoch=large[IMG][0], gru_weight=jnp.concatenate(large[GRU], 1),
        post_in=large[POST][0], post_out=large[POST_OUT][0],
        prior_in=large[PRIOR][0], prior_out=large[PRIOR_OUT][0],
    )
    deter_grad = b.deter_grad.reshape(SEQ_DEV, LEN, H)
    return (small[LOSS, 0], deter_grad, f.embed_grad.reshape(SEQ_DEV, LEN, E)) + tuple(out)


DP, REP = ("dp", "rep")
IMG_ACTION = 14
LARGE = Weights(**dict.fromkeys(Weights._fields, False))._replace(
    manager_in=True,
    goal_in=True,
    goal_out=True,
    actor_in=True,
    critic_in=True,
    img_stoch=True,
    gru_weight=True,
    post_in=True,
    post_out=True,
    prior_in=True,
    prior_out=True,
    enc_in=True,
)


def hidden_forward(pre_act, scaling):
    normed, inverse = normalize(pre_act)
    scaled = normed * scaling
    return ((normed, inverse, scaled), jax.nn.elu(scaled).astype(jnp.bfloat16))


def hidden_backward(grad_hidden, cache, scaling):
    normed, inverse, scaled = cache
    grad_scaled = grad_hidden * jnp.where(scaled > 0, 1.0, jnp.exp(jnp.minimum(scaled, 0.0)))
    grad_gain = jnp.sum(grad_scaled * normed, tuple(range(scaled.ndim - 1)))
    return (normalize_back(grad_scaled * scaling, normed, inverse).astype(jnp.bfloat16), grad_gain)


def input_backward(grad_pre, input_low, weight):
    grad_weight = jnp.einsum("nk,nu->ku", input_low, grad_pre, preferred_element_type=jnp.float32)
    to_input = jnp.einsum("nu,ku->nk", grad_pre, weight, preferred_element_type=jnp.float32)
    return (grad_weight, to_input)


def head_backward(grad_head, hidden_low, head, cache, scaling):
    grad_weight = jnp.einsum("nu,nk->uk", hidden_low, grad_head, preferred_element_type=jnp.float32)
    grad_hidden = jnp.einsum("nk,uk->nu", grad_head, head, preferred_element_type=jnp.float32)
    grad_pre, grad_gain = hidden_backward(grad_hidden, cache, scaling)
    return (grad_weight, grad_pre, grad_gain)


def group_softmax(flat_logits, groups):
    log_part = jax.nn.log_softmax(flat_logits.reshape(flat_logits.shape[0], groups, -1), axis=-1)
    return (log_part, jnp.exp(log_part))


def chain_returns(values_now, rewards_now, linked, carried):

    def back_step(carry_pair, inputs):
        later_return, later_value = carry_pair
        current, reward_now, link_now, carry_now = inputs
        blended = (1.0 - return_mix) * later_value + return_mix * later_return
        result = jnp.where(link_now, reward_now + discount * carry_now * blended, current)
        return ((result, current), result)

    zero_start = jnp.zeros(values_now.shape[:1], jnp.float32)
    _, stacked = lax.scan(
        back_step,
        (zero_start, zero_start),
        (values_now.T, rewards_now.T, linked.T, carried.T),
        reverse=True,
    )
    return stacked.T


def worker_forward(start_state, goal_low, stoch_hot, first_layer, scaling):
    slot_part = product(start_state, first_layer[:H]) + product(goal_low, first_layer[H + Z :])
    varying = product(stoch_hot, first_layer[H : H + Z]).reshape(start_state.shape[0], HOR, U)
    return hidden_forward(slot_part[:, None, :] + varying, scaling)


def worker_backward(grad_pre, start_state, goal_low, stoch_hot, first_layer):
    slot_count = grad_pre.shape[0]
    grad_stoch = jnp.einsum(
        "nz,nu->zu",
        stoch_hot,
        grad_pre.reshape(slot_count * HOR, U),
        preferred_element_type=jnp.float32,
    )
    summed = jnp.sum(grad_pre, 1, dtype=jnp.float32).astype(jnp.bfloat16)
    grad_state_rows, to_state = input_backward(summed, start_state, first_layer[:H])
    grad_goal_rows, to_goal = input_backward(summed, goal_low, first_layer[H + Z :])
    return (jnp.concatenate([grad_state_rows, grad_stoch, grad_goal_rows], 0), to_state, to_goal)


def step_plain(data, shares):
    (deter_states, embed, lengths, resets, terminal, rewards, prev_stoch, prev_action, regroup, goal_codes, samples, actions) = data
    full = [
        lax.all_gather(share, REP, axis=1 if i == IMG_ACTION else 0, tiled=True)
        for i, share in enumerate(shares)
    ]
    (obs_gain, manager_in, manager_gain, manager_out, goal_in, goal_gain, goal_out, actor_in, actor_gain, actor_out, critic_in, critic_gain, critic_out, img_stoch, img_action, img_gain, gru_weight, gru_gain, post_in, post_gain, post_out, prior_in, prior_gain, prior_out, enc_in, enc_gain, enc_out) = full
    prev_low = deter_states.reshape(ROWS, H)
    prev_float = prev_low.astype(jnp.float32)
    embed_low = embed.reshape(ROWS, E)
    positions = lax.broadcasted_iota(jnp.int32, (SEQ_DEV, LEN), 1)
    is_valid = positions < lengths[:, None]
    next_valid = jnp.concatenate([is_valid[:, 1:], jnp.zeros((SEQ_DEV, 1), jnp.bool_)], 1)
    next_reset = jnp.concatenate([resets[:, 1:], jnp.ones((SEQ_DEV, 1), jnp.int32)], 1)
    linked = next_valid & (next_reset == 0)
    carried = 1.0 - terminal.astype(jnp.float32)
    valid_rows = is_valid.astype(jnp.float32).reshape(ROWS)
    frame_scale = valid_rows / ROWS
    stoch_prev_hot = (
        (prev_stoch[..., None] == lax.broadcasted_iota(jnp.int32, (1, 1, 1, ZK), 3))
        .astype(jnp.bfloat16)
        .reshape(ROWS, Z)
    )
    action_prev_hot = (
        prev_action.reshape(ROWS)[:, None] == lax.broadcasted_iota(jnp.int32, (1, NA), 1)
    ).astype(jnp.bfloat16)
    img_cache, img_hidden = hidden_forward(
        product(stoch_prev_hot, img_stoch) + product(action_prev_hot, img_action), img_gain
    )
    gru_input = jnp.concatenate([img_hidden, prev_low], 1)
    gru_normed, gru_inverse = normalize(product(gru_input, gru_weight))
    gru_parts = gru_normed * gru_gain
    reset_gate = jax.nn.sigmoid(gru_parts[:, :H])
    candidate_in = gru_parts[:, H : 2 * H]
    candidate = jnp.tanh(reset_gate * candidate_in)
    update_gate = jax.nn.sigmoid(gru_parts[:, 2 * H :] - 1.0)
    deter_state = update_gate * candidate + (1.0 - update_gate) * prev_float
    deter_low = deter_state.astype(jnp.bfloat16)
    obs_normed, obs_inverse = normalize(deter_state)
    feature = (obs_normed * obs_gain).astype(jnp.bfloat16)
    man_cache, man_hidden = hidden_forward(product(feature, manager_in), manager_gain)
    manager_value = product(man_hidden, manager_out).reshape(SEQ_DEV, LEN)
    manager_return = chain_returns(manager_value, rewards, linked, carried)
    manager_misfit = (manager_value - manager_return).reshape(ROWS)
    post_input = jnp.concatenate([deter_low, embed_low], 1)
    post_cache, post_hidden = hidden_forward(product(post_input, post_in), post_gain)
    post_log, post_prob = group_softmax(product(post_hidden, post_out), ZG)
    prior_cache, prior_hidden = hidden_forward(product(deter_low, prior_in), prior_gain)
    prior_log, prior_prob = group_softmax(product(prior_hidden, prior_out), ZG)
    log_gap = post_log - prior_log
    group_kl = jnp.sum(post_prob * log_gap, -1, keepdims=True)
    enc_cache, enc_hidden = hidden_forward(product(deter_low, enc_in), enc_gain)
    code_log, code_prob = group_softmax(product(enc_hidden, enc_out), GC)
    code_kl = jnp.sum(code_prob * (code_log + math.log(GK)), (1, 2))
    code_spread = jnp.sum(code_prob * code_log, -1, keepdims=True)
    soft_code = code_prob.reshape(ROWS, GCODE).astype(jnp.bfloat16)
    dec_cache, dec_hidden = hidden_forward(product(soft_code, goal_in), goal_gain)
    recon_err = product(dec_hidden, goal_out) - deter_state
    frame_terms = (
        jnp.sum(post_prob * log_gap, (1, 2)) + code_kl + 0.5 * jnp.mean(recon_err * recon_err, -1)
    )
    frame_loss = jnp.sum(valid_rows * (0.5 * manager_misfit * manager_misfit + frame_terms)) / ROWS
    send_order = regroup[0]
    start_state, slot_flag = (
        lax.all_to_all(deter_low[send_order], DP, split_axis=0, concat_axis=0, tiled=True),
        lax.all_to_all(
            valid_rows[send_order].astype(jnp.bfloat16),
            DP,
            split_axis=0,
            concat_axis=0,
            tiled=True,
        ),
    )
    slot_weight = slot_flag.astype(jnp.float32)
    code_hot = (
        (goal_codes[:, :, None] == lax.broadcasted_iota(jnp.int32, (1, 1, GK), 2))
        .astype(jnp.bfloat16)
        .reshape(ROWS, GCODE)
    )
    goal_cache, goal_hidden = hidden_forward(product(code_hot, goal_in), goal_gain)
    goal_vector = product(goal_hidden, goal_out)
    goal_low = goal_vector.astype(jnp.bfloat16)
    state_float = start_state.astype(jnp.float32)
    alignment = jnp.sum(goal_vector * state_float, -1)
    largest_square = (
        jnp.maximum(jnp.sum(goal_vector * goal_vector, -1), jnp.sum(state_float * state_float, -1))
        + small_floor
    )
    reward_slot = alignment / largest_square
    stoch_hot = (
        (samples[..., None] == lax.broadcasted_iota(jnp.int32, (1, 1, 1, ZK), 3))
        .astype(jnp.bfloat16)
        .reshape(ROWS * HOR, Z)
    )
    action_hot = (actions[..., None] == lax.broadcasted_iota(jnp.int32, (1, 1, NA), 2)).astype(
        jnp.float32
    )
    actor_cache, actor_hidden = worker_forward(
        start_state, goal_low, stoch_hot, actor_in, actor_gain
    )
    logits = jnp.einsum("rku,ua->rka", actor_hidden, actor_out, preferred_element_type=jnp.float32)
    log_chance = jax.nn.log_softmax(logits, axis=-1)
    chosen = jnp.sum(log_chance * action_hot, -1)
    critic_cache, critic_hidden = worker_forward(
        start_state, goal_low, stoch_hot, critic_in, critic_gain
    )
    worker_value = jnp.einsum(
        "rku,u->rk", critic_hidden, critic_out, preferred_element_type=jnp.float32
    )
    step_link = lax.broadcasted_iota(jnp.int32, (ROWS, HOR), 1) < HOR - 1
    worker_return = chain_returns(
        worker_value,
        jnp.broadcast_to(reward_slot[:, None], (ROWS, HOR)),
        step_link,
        jnp.ones((ROWS, HOR), jnp.float32),
    )
    advantage = worker_return - worker_value
    local_top = jnp.max(slot_weight[:, None] * jnp.abs(advantage))
    return_scale = lax.pmax(local_top, (DP, REP)) + small_floor
    step_total = ROWS * HOR
    value_misfit = worker_value - worker_return
    critic_part = 0.5 * jnp.sum(slot_weight[:, None] * value_misfit * value_misfit)
    actor_part = jnp.sum(slot_weight[:, None] * chosen * advantage) / return_scale
    local_loss = frame_loss + (critic_part - actor_part) / step_total
    grad_value = slot_weight[:, None] * value_misfit / step_total
    grad_chosen = -slot_weight[:, None] * advantage / return_scale / step_total
    grad_logits = (grad_chosen[..., None] * (action_hot - jnp.exp(log_chance))).astype(jnp.bfloat16)
    grad_actor_out = jnp.einsum(
        "rku,rka->ua", actor_hidden, grad_logits, preferred_element_type=jnp.float32
    )
    grad_actor_hidden = jnp.einsum(
        "rka,ua->rku", grad_logits, actor_out, preferred_element_type=jnp.float32
    )
    actor_pre, grad_actor_gain = hidden_backward(grad_actor_hidden, actor_cache, actor_gain)
    grad_critic_out = jnp.einsum("rku,rk->u", critic_hidden, grad_value, precision=highest)
    critic_pre, grad_critic_gain = hidden_backward(
        grad_value[..., None] * critic_out, critic_cache, critic_gain
    )
    grad_actor_in, actor_to_state, actor_to_goal = worker_backward(
        actor_pre, start_state, goal_low, stoch_hot, actor_in
    )
    grad_critic_in, critic_to_state, critic_to_goal = worker_backward(
        critic_pre, start_state, goal_low, stoch_hot, critic_in
    )
    grad_goal_low = (actor_to_goal + critic_to_goal).astype(jnp.bfloat16)
    worker_goal_out, goal_pre, worker_goal_gain = head_backward(
        grad_goal_low, goal_hidden, goal_out, goal_cache, goal_gain
    )
    worker_goal_in = jnp.einsum("ng,nu->gu", code_hot, goal_pre, preferred_element_type=jnp.float32)
    returned = lax.all_to_all(
        (actor_to_state + critic_to_state).astype(jnp.bfloat16),
        DP,
        split_axis=0,
        concat_axis=0,
        tiled=True,
    )
    grad_manager_value = frame_scale * manager_misfit
    grad_manager_out = jnp.dot(grad_manager_value, man_hidden, precision=highest)
    manager_pre, grad_manager_gain = hidden_backward(
        grad_manager_value[:, None] * manager_out, man_cache, manager_gain
    )
    grad_manager_in, grad_feature = input_backward(manager_pre, feature, manager_in)
    grad_obs_gain = jnp.sum(grad_feature * obs_normed, 0)
    obs_back = normalize_back(grad_feature * obs_gain, obs_normed, obs_inverse)
    weight_cube = frame_scale[:, None, None]
    post_grad_logits = (
        (weight_cube * post_prob * (log_gap - group_kl)).reshape(ROWS, Z).astype(jnp.bfloat16)
    )
    prior_grad_logits = (
        (weight_cube * (prior_prob - post_prob)).reshape(ROWS, Z).astype(jnp.bfloat16)
    )
    grad_post_out, post_pre, grad_post_gain = head_backward(
        post_grad_logits, post_hidden, post_out, post_cache, post_gain
    )
    grad_post_in, post_back = input_backward(post_pre, post_input, post_in)
    grad_prior_out, prior_pre, grad_prior_gain = head_backward(
        prior_grad_logits, prior_hidden, prior_out, prior_cache, prior_gain
    )
    grad_prior_in, prior_back = input_backward(prior_pre, deter_low, prior_in)
    recon_grad = frame_scale[:, None] * recon_err / H
    dec_goal_out, dec_pre, dec_goal_gain = head_backward(
        recon_grad.astype(jnp.bfloat16), dec_hidden, goal_out, dec_cache, goal_gain
    )
    dec_goal_in, grad_code = input_backward(dec_pre, soft_code, goal_in)
    grad_code = grad_code.reshape(ROWS, GC, GK)
    code_grad_logits = code_prob * (
        grad_code - jnp.sum(code_prob * grad_code, -1, keepdims=True)
    ) + weight_cube * code_prob * (code_log - code_spread)
    grad_enc_out, enc_pre, grad_enc_gain = head_backward(
        code_grad_logits.reshape(ROWS, GCODE).astype(jnp.bfloat16),
        enc_hidden,
        enc_out,
        enc_cache,
        enc_gain,
    )
    grad_enc_in, enc_back = input_backward(enc_pre, deter_low, enc_in)
    grad_goal_out = worker_goal_out + dec_goal_out
    grad_goal_in = worker_goal_in + dec_goal_in
    grad_goal_gain = worker_goal_gain + dec_goal_gain
    scattered = jnp.zeros((ROWS, H), jnp.float32).at[send_order].add(returned.astype(jnp.float32))
    grad_deter = obs_back + post_back[:, :H] + prior_back + enc_back + scattered - recon_grad
    grad_inner = grad_deter * update_gate * (1.0 - candidate * candidate)
    grad_parts = jnp.concatenate(
        [
            grad_inner * candidate_in * reset_gate * (1.0 - reset_gate),
            grad_inner * reset_gate,
            grad_deter * (candidate - prev_float) * update_gate * (1.0 - update_gate),
        ],
        1,
    )
    grad_gru_gain = jnp.sum(grad_parts * gru_normed, 0)
    gru_pre = normalize_back(grad_parts * gru_gain, gru_normed, gru_inverse).astype(jnp.bfloat16)
    grad_gru_weight, gru_back = input_backward(gru_pre, gru_input, gru_weight)
    img_pre, grad_img_gain = hidden_backward(gru_back[:, :H], img_cache, img_gain)
    grad_img_stoch = jnp.einsum(
        "nz,nh->zh", stoch_prev_hot, img_pre, preferred_element_type=jnp.float32
    )
    grad_img_action = jnp.einsum(
        "na,nh->ah", action_prev_hot, img_pre, preferred_element_type=jnp.float32
    )
    grad_prev = grad_deter * (1.0 - update_gate) + gru_back[:, H:]
    embed_grad = post_back[:, H:]
    count = lax.axis_size(REP)
    loss_share = lax.psum_scatter(
        jnp.full((count,), local_loss), REP, scatter_dimension=0, tiled=True
    )
    grads = Weights(
        obs_gain=grad_obs_gain,
        manager_in=grad_manager_in,
        manager_gain=grad_manager_gain,
        manager_out=grad_manager_out,
        goal_in=grad_goal_in,
        goal_gain=grad_goal_gain,
        goal_out=grad_goal_out,
        actor_in=grad_actor_in,
        actor_gain=grad_actor_gain,
        actor_out=grad_actor_out,
        critic_in=grad_critic_in,
        critic_gain=grad_critic_gain,
        critic_out=grad_critic_out,
        img_stoch=grad_img_stoch,
        img_action=grad_img_action,
        img_gain=grad_img_gain,
        gru_weight=grad_gru_weight,
        gru_gain=grad_gru_gain,
        post_in=grad_post_in,
        post_gain=grad_post_gain,
        post_out=grad_post_out,
        prior_in=grad_prior_in,
        prior_gain=grad_prior_gain,
        prior_out=grad_prior_out,
        enc_in=grad_enc_in,
        enc_gain=grad_enc_gain,
        enc_out=grad_enc_out,
    )
    shares = []
    for i, (grad, by_column) in enumerate(zip(grads, LARGE)):
        grad = lax.psum_scatter(
            grad, REP, scatter_dimension=1 if i == IMG_ACTION else 0, tiled=True
        )
        if by_column:
            shares.append(lax.psum_scatter(grad, DP, scatter_dimension=1, tiled=True))
        else:
            shares.append(lax.psum(grad, DP))
    return (
        lax.psum(loss_share, DP)[0],
        grad_prev.reshape(SEQ_DEV, LEN, H),
        embed_grad.reshape(SEQ_DEV, LEN, E),
    ) + tuple(shares)


def solution(mesh):
    split, over_rep = (P((DP, REP)), P(REP))
    in_kernels = mesh.shape[DP] == 8 and mesh.shape[REP] == 4

    def per_device(*arguments):
        data, shares = (Data(*arguments[:12]), Weights(*arguments[12:]))
        return (step_in_kernels if in_kernels else step_plain)(data, shares)

    in_specs, out_specs = ((split,) * 12, (P(), split, split))
    for i, by_column in enumerate(LARGE):
        spec = P(None, REP) if i == IMG_ACTION else over_rep
        in_specs += (spec,)
        out_specs += (P(REP, DP) if by_column else spec,)
    return jax.shard_map(
        per_device, mesh=mesh, in_specs=in_specs, out_specs=out_specs, check_vma=False
    )
```

time: 2270 us -> 438 us (0.19)
  waiting for transfers between devices: 1380 us -> 0 us
  Pallas kernels: 0 us -> 396 us
  local copies, waits for them, and re-layouts: 345 us -> 29.9 us
  blocking collectives: 174 us -> 0 us
  matrix products: 156 us -> 0 us
  other arithmetic: 155 us -> 9.9 us
  starting transfers between devices: 32.9 us -> 0 us
    reduce_scatter x22 -> x0, waiting for transfers between devices: 1080 us -> none  [the longest x1 183 us: per_device(): lax.psum_scatter(grad_gru_weight, 'rep', scatter_dimension=0, tiled=True)]
    pallas_call x0 -> x4, Pallas kernels: none -> 396 us  [the longest x3 210 us: run_kernel(): pl.pallas_call(kernel, out_shape=[jax.ShapeDtypeStruct(a.shape, a.dtype)...]
    unnamed x43 -> x0, waiting for transfers between devices: 292 us -> none
    dynamic_slice x128 -> x0, local copies, waits for them, and re-layouts: 160 us -> none  [chain_returns(): lax.scan(back_step, (zero_start, zero_start), (values_now.T, rewards_now....]
    dot_general x60 -> x0, matrix products: 152 us -> none  [the longest x21 44.1 us: product(): return jnp.dot(left, right, preferred_element_type=jnp.float32)]
    dynamic_update_slice x80 -> x0, local copies, waits for them, and re-layouts: 83.2 us -> none  [chain_returns(): lax.scan(back_step, (zero_start, zero_start), (values_now.T, rewards_now....]
    select_n x81 -> x0, other arithmetic: 82.9 us -> none  [the longest x80 82.9 us: back_step(): jnp.where(link_now, reward_now + discount * carry_now * blended, current)]
    all_gather x16 -> x0, blocking collectives: 82.9 us -> none  [the longest x1 5.68 us: per_device(): lax.all_gather(goal_in, 'rep', axis=0, tiled=True)]
  transfers between devices with their start and end apart: 41 -> 0, of which waited for: 23 -> 0; matrix products, arithmetic and copies ran while one was open for 26% -> 0% of each run, Pallas kernels for 0% -> 0%
where the time goes in v1:
time: 438 us; the launch traced here: 437 us
  Pallas kernels  396 us (90%)
  local copies, waits for them, and re-layouts  29.9 us (7%)
  other arithmetic  9.9 us (2%)
    pallas_call x3, Pallas kernels, run_kernel(): pl.pallas_call(kernel, out_shape=[jax.ShapeDtypeStruct(a.shape, a.dtype)...  210 us
    pallas_call x1, Pallas kernels, reduce_call(): pl.pallas_call(reduce_kernel, out_shape=[jax.ShapeDtypeStruct((unit_rows(...  187 us
    unnamed x39, local copies, waits for them, and re-layouts  12.1 us

profile of v1, /device:TPU:0, one launch (start us, length us, event | category | flops | bytes accessed | tf_op | source)
XLA Modules:
  0.0 436.8 jit_solution(18064526095156437686)
XLA Ops:
  1.5 0.7 slice.91
  3.6 0.7 iota_compare_fusion
  5.1 2.2 concatenate.28
  9.3 0.8 convert_element_type.105
  11.0 0.7 constant_dynamic-update-slice_fusion.6
  16.0 0.8 reshape.280
  16.8 0.8 concatenate.27.refs_0_
  17.7 1.0 convert_element_type.119
  18.6 1.3 copy.92
  19.9 122.9 %frames.1 = (bf16[2048,3072]{1,0:T(8,128)(2,1)}, bf16[512,1024]{1,0:T(8,128)(2,1)}, bf16[3072,512]{1,0:T(8,128)(2,1)}, bf16[3072,512]{1,0:T(8,128)(2,1)}, f32[4,...) custom-call(f32[128,128]{1,0:T(8,128)} %concatenate.27.refs_0_, ...), custom_call_target="tpu_custom_call" | custom-call | tf_op jit(solution)/shard_map/frames/pallas_call | solution.py:76
  142.9 71.3 %worker.1 = (bf16[3072,1024]{1,0:T(8,128)(2,1)}, bf16[128,1024]{1,0:T(8,128)(2,1)}, bf16[512,128]{1,0:T(8,128)(2,1)}, bf16[64,128]{1,0:T(8,128)(2,1)}, bf16[128,...) custom-call(f32[128,128]{1,0:T(8,128)} %maximum_maximum_fusion.refs_0_, ...), custom_call_target="tpu_custom_call" | custom-call | tf_op jit(solution)/shard_map/worker/pallas_call | solution.py:76
  214.2 15.3 %back.1 = (f32[128,1024]{1,0:T(8,128)}, bf16[128,3072]{1,0:T(8,128)(2,1)}, bf16[128,1024]{1,0:T(8,128)(2,1)}, f32[2,2,160,128]{3,2,1,0:T(8,128)}) custom-call(f32[128,128]{1,0:T(8,128)} %concatenate.27.refs_0_, bf16[128,1024]{1,0:T(8,128)(2,1)} %bitcast.55, f32[4,24,128]{2,1,0:T(8,128)} %get-tuple-element.89.refs_2_, ...), custom_call_target="tpu_custom_call" | custom-call | tf_op jit(solution)/shard_map/back/pallas_call | solution.py:76
  229.5 186.7 %reduce.1 = (f32[640,128]{1,0:T(8,128)}, f32[768,128]{1,0:T(8,128)}, f32[256,128]{1,0:T(8,128)}, f32[512,128]{1,0:T(8,128)}, f32[512,128]{1,0:T(8,128)}, /*index...) custom-call(bf16[2048,128]{1,0:T(8,128)(2,1)} %get-tuple-element.83., ...), custom_call_target="tpu_custom_call" | custom-call | tf_op jit(solution)/shard_map/reduce/pallas_call | solution.py:1536
  416.2 1.3 slice.98
  417.5 1.4 slice_bitcast_fusion.7
  418.9 1.3 slice_bitcast_fusion.2
  420.2 1.3 slice_bitcast_fusion.3
  421.5 1.4 slice_bitcast_fusion
  422.9 1.3 fusion.3
  424.9 1.1 fusion.2
  427.4 2.1 pad_maximum_fusion
  429.7 0.8 copy.95
  430.5 0.8 copy.94
  431.3 0.9 copy.112
  (61 shorter events, 16.9 us)
Async XLA Ops:
  14.5 5.4 %copy-start.7 = (bf16[224,128]{1,0:T(8,128)(2,1)}, bf16[224,128]{1,0:T(8,128)(2,1)S(1)}, u32[]{:S(2)}) copy-start(bf16[224,128]{1,0:T(8,128)(2,1)S(1)} %constant_dynamic-update-slice_fusion.refs_4_) | copy-start | bytes 172036
  416.2 13.3 %copy-start = (f32[768,128]{1,0:T(8,128)S(1)}, f32[768,128]{1,0:T(8,128)}, u32[]{:S(2)}) copy-start(f32[768,128]{1,0:T(8,128)} %get-tuple-element.127) | copy-start | bytes 1179652
  416.2 15.1 %copy-start.1 = (f32[128,1536]{1,0:T(8,128)S(1)}, f32[128,1536]{1,0:T(8,128)}, u32[]{:S(2)}) copy-start(f32[128,1536]{1,0:T(8,128)} %get-tuple-element.123) | copy-start | bytes 2359300
  425.9 6.3 %copy-start.9 = (f32[16,128]{1,0:T(8,128)S(1)}, f32[16,128]{1,0:T(8,128)}, u32[]{:S(2)}) copy-start(f32[16,128]{1,0:T(8,128)} %get-tuple-element.125) | copy-start | bytes 24580
  426.0 6.9 %copy-start.8 = (f32[128,128]{1,0:T(8,128)S(1)}, f32[128,128]{1,0:T(8,128)}, u32[]{:S(2)}) copy-start(f32[128,128]{1,0:T(8,128)} %get-tuple-element.257) | copy-start | bytes 196612
  426.7 6.8 %copy-start.6 = (f32[256,128]{1,0:T(8,128)S(1)}, f32[256,128]{1,0:T(8,128)}, u32[]{:S(2)}) copy-start(f32[256,128]{1,0:T(8,128)} %get-tuple-element.264) | copy-start | bytes 393220
  427.4 6.7 %copy-start.2 = (f32[640,128]{1,0:T(8,128)S(1)}, f32[640,128]{1,0:T(8,128)}, u32[]{:S(2)}) copy-start(f32[640,128]{1,0:T(8,128)} %get-tuple-element.269) | copy-start | bytes 983044
  427.4 7.4 %copy-start.5 = (f32[256,128]{1,0:T(8,128)S(1)}, f32[256,128]{1,0:T(8,128)}, u32[]{:S(2)}) copy-start(f32[256,128]{1,0:T(8,128)} %get-tuple-element.271) | copy-start | bytes 393220
  429.5 6.0 %copy-start.4 = (f32[256,128]{1,0:T(8,128)S(1)}, f32[256,128]{1,0:T(8,128)}, u32[]{:S(2)}) copy-start(f32[256,128]{1,0:T(8,128)} %get-tuple-element.272) | copy-start | bytes 393220
  429.5 6.7 %copy-start.3 = (f32[256,128]{1,0:T(8,128)S(1)}, f32[256,128]{1,0:T(8,128)}, u32[]{:S(2)}) copy-start(f32[256,128]{1,0:T(8,128)} %get-tuple-element.274) | copy-start | bytes 393220

commit v2 on v1

--- a/solution.py
+++ b/solution.py
@@ -65,29 +65,33 @@
 
 
 def run_kernel(body, layout, inputs, name, collective=None):
+    leaves, tree = jax.tree.flatten(layout, is_leaf=lambda a: isinstance(a, Arg))
+
     def kernel(*refs):
-        body(type(layout)(*refs))
+        body(jax.tree.unflatten(tree, refs))
 
     def place(arg):
         return pl.BlockSpec(memory_space=pltpu.VMEM if arg.here else pl.ANY)
 
-    outs = [a for a in layout if a.kind == GIVEN]
+    outs = [a for a in leaves if a.kind == GIVEN]
     more = {} if collective is None else dict(collective_id=collective, has_side_effects=True)
     results = pl.pallas_call(
         kernel,
         out_shape=[jax.ShapeDtypeStruct(a.shape, a.dtype) for a in outs],
-        in_specs=[place(a) for a in layout if a.kind == TAKEN],
+        in_specs=[place(a) for a in leaves if a.kind == TAKEN],
         out_specs=[place(a) for a in outs],
         scratch_shapes=[
             pltpu.VMEM(a.shape, a.dtype) if a.kind == KEPT else pltpu.SemaphoreType.DMA(a.shape)
-            for a in layout
+            for a in leaves
             if a.kind >= KEPT
         ],
         compiler_params=pltpu.CompilerParams(vmem_limit_bytes=VMEM_BYTES, **more),
         name=name,
     )(*inputs)
     results = iter(results)
-    return type(layout)(*[next(results) if a.kind == GIVEN else None for a in layout])
+    return jax.tree.unflatten(
+        tree, [next(results) if a.kind == GIVEN else None for a in leaves]
+    )
 
 
 def product(left, right):
@@ -152,7 +156,7 @@
     by_rows(ref.shape[0], size, one)
 
 
-def hidden_rows(ref, inverse_ref, gain, hidden_ref, size=32):
+def hidden_rows(ref, inverse_ref, gain, hidden_ref, size=128):
     def one(rows, carry):
         normed, inverse = normalize(ref[rows, :])
         ref[rows, :] = normed
@@ -163,13 +167,14 @@
     by_rows(ref.shape[0], size, one)
 
 
-def hidden_rows_back(grad_of, ref, inverse_ref, gain, pre_ref, size=32):
+def hidden_rows_back(grad_of, ref, inverse_ref, gain, pre_ref, size=128, hidden_ref=None):
     def one(rows, total):
         normed = ref[rows, :]
         scaled = normed * gain
-        grad_scaled = grad_of(rows) * jnp.where(
-            scaled > 0, 1.0, jnp.exp(jnp.minimum(scaled, 0.0))
-        )
+        power = jnp.exp(jnp.minimum(scaled, 0.0))
+        if hidden_ref is not None:
+            hidden_ref[rows, :] = jnp.where(scaled > 0, scaled, power - 1.0).astype(BF)
+        grad_scaled = grad_of(rows) * jnp.where(scaled > 0, 1.0, power)
         total = total + jnp.sum(grad_scaled * normed, 0, keepdims=True)
         back = normalize_back(grad_scaled * gain, normed, inverse_ref[rows, :])
         pre_ref[rows, :] = back.astype(pre_ref.dtype)
@@ -196,6 +201,11 @@
     lane = lax.broadcasted_iota(jnp.int32, (1, width), 1)
     same = here == jnp.bitwise_and(lane, classes - 1).astype(F32)
     return jnp.where(same & (lane < groups * classes), 1.0, 0.0)
+
+
+def columns_of(rows):
+    count = rows.shape[0]
+    return jnp.concatenate([rows, jnp.zeros((LANES - count, rows.shape[1]), F32)], 0).T
 
 
 def vector_of(packed, low, tiles):
@@ -244,11 +254,31 @@
 
 
 class Frames(NamedTuple):
-    meta: Any = taken(ROWS, LANES, dtype=F32)
+    lengths: Any = taken(SEQ_DEV, dtype=jnp.int32)
+    resets: Any = taken(SEQ_DEV, LEN, dtype=jnp.int32)
+    terminal: Any = taken(SEQ_DEV, LEN, dtype=jnp.int32)
+    rewards: Any = taken(SEQ_DEV, LEN, dtype=F32)
+    prev_stoch: Any = taken(SEQ_DEV, ZG, LEN, dtype=jnp.int32)
+    prev_action: Any = taken(SEQ_DEV, LEN, dtype=jnp.int32)
+    regroup: Any = taken(1, ROWS, dtype=jnp.int32)
     prev: Any = taken(ROWS, H)
     embed: Any = taken(ROWS, E)
-    vector_share: Any = taken(VECTOR_TILES, LANES, dtype=F32)
-    table_share: Any = taken(TABLES, LANES)
+    obs_gain: Any = taken(H // 4)
+    manager_gain: Any = taken(U // 4)
+    manager_head: Any = taken(U // 4)
+    goal_gain: Any = taken(U // 4)
+    actor_gain: Any = taken(U // 4)
+    critic_gain: Any = taken(U // 4)
+    critic_head: Any = taken(U // 4)
+    img_gain: Any = taken(H // 4)
+    gru_gain: Any = taken(3 * H // 4)
+    post_gain: Any = taken(H // 4)
+    prior_gain: Any = taken(H // 4)
+    enc_gain: Any = taken(U // 4)
+    actor_head: Any = taken(NA, U // 4)
+    enc_head: Any = taken(GCODE, U // 4)
+    img_action_share: Any = taken(NA, H // 4)
+    goal_in_share: Any = taken(GCODE // 4, U)
     img_stoch_share: Any = taken(Z // 4, H, here=False)
     gru_weight_share: Any = taken(H // 2, 3 * H, here=False)
     manager_in_share: Any = taken(H // 4, U, here=False)
@@ -266,6 +296,7 @@
     critic_in_out: Any = given(3 * H, U, here=False)
     vectors: Any = given(4, VECTOR_TILES, LANES, dtype=F32)
     tables: Any = given(4, TABLES, LANES)
+    meta_turned: Any = given(LANES, ROWS, dtype=F32)
     start_state: Any = given(ROWS, H + LANES)
     gru_left: Any = given(2 * H, ROWS)
     post_left: Any = given(H + E, ROWS)
@@ -303,8 +334,10 @@
     img_action: Any = kept(32, H)
     enc_out: Any = kept(GCODE, U)
     goal_in: Any = kept(GCODE, U)
+    vector_share: Any = kept(VECTOR_TILES, LANES, dtype=F32)
+    table_share: Any = kept(TABLES, LANES)
+    meta: Any = kept(ROWS, LANES, dtype=F32)
     hot: Any = kept(ROWS, Z)
-    meta_turned: Any = kept(LANES, ROWS, dtype=F32)
     img_hidden: Any = kept(ROWS, H)
     deter: Any = kept(ROWS, H, dtype=F32)
     deter_low: Any = kept(ROWS, H)
@@ -342,14 +375,57 @@
     state_send: Any = signal(8)
     state_recv: Any = signal(8)
 
+    def pack(self):
+        vectors = (
+            self.obs_gain, self.manager_gain, self.manager_head, self.goal_gain, self.actor_gain,
+            self.critic_gain, self.critic_head, self.img_gain, self.gru_gain, self.post_gain,
+            self.prior_gain, self.enc_gain,
+        )
+        low = 0
+        for vector in vectors:
+            for i in range(vector.shape[0] // LANES):
+                self.vector_share[low, :] = vector[pl.ds(i * LANES, LANES)].astype(F32)
+                low += 1
+        self.vector_share[low:, :] = jnp.zeros((VECTOR_TILES - low, LANES), F32)
+        self.table_share[...] = jnp.zeros(self.table_share.shape, BF)
+        self.table_share[TAB_ACT : TAB_ACT + NA, :] = self.actor_head[...]
+        self.table_share[TAB_ENC : TAB_ENC + GCODE, :] = self.enc_head[...]
+        for i in range(2):
+            low = TAB_IMG + 32 * i
+            lanes = slice(i * LANES, (i + 1) * LANES)
+            self.table_share[low : low + NA, :] = self.img_action_share[:, lanes]
+        for i in range(4):
+            low = TAB_GOAL + 16 * i
+            lanes = slice(i * LANES, (i + 1) * LANES)
+            self.table_share[low : low + 16, :] = self.goal_in_share[:, lanes]
+
     def start(self):
-        meta = self.meta[...]
-        hot = hot_rows(meta[:, 0:ZG], ZK, ZG, Z)
-        self.hot[...] = hot.astype(BF)
+        def row(ref):
+            value = ref[...].astype(F32)
+            return jnp.concatenate([value[0:1], value[1:2]], 1)
+
+        position = lax.broadcasted_iota(jnp.int32, (SEQ_DEV, LEN), 1)
+        length = self.lengths[...].reshape(SEQ_DEV, 1)
+        later = jnp.where((position + 1 < length) & (position + 1 < LEN), 1.0, 0.0)
+        kinds = (
+            row(self.prev_action),
+            row(jnp.where(position < length, 1.0, 0.0)),
+            row(later) * (1.0 - jnp.minimum(pltpu.roll(row(self.resets), ROWS - 1, 1), 1.0)),
+            1.0 - row(self.terminal),
+            row(self.rewards),
+            self.regroup[...].astype(F32),
+        )
+        self.meta_turned[...] = jnp.zeros(self.meta_turned.shape, F32)
+        for i, kind in enumerate(kinds):
+            self.meta_turned[32 + i : 33 + i, :] = kind
+        self.meta[...] = self.meta_turned[...].T
+        ids = jnp.concatenate([self.prev_stoch[0], self.prev_stoch[1]], 1).astype(F32)
+        self.hot[...] = hot_rows(columns_of(ids)[:, 0:ZG], ZK, ZG, Z).astype(BF)
+
+    def turns(self):
         turn_into(self.img_left, self.hot)
         turn_into(self.gru_left, self.prev, H)
         turn_into(self.post_left, self.embed, H)
-        self.meta_turned[...] = meta.T
         self.small[...] = jnp.zeros(self.small.shape, F32)
 
     def unpack(self):
@@ -835,6 +911,7 @@
     gather = Gather(places, units, f.piece_send, f.piece_recv, f.load_done)
     for u in range(len(units)):
         gather.load(u)
+    f.pack()
     greet(
         [(places.around(o), places.rep) for o in range(1, 8)]
         + [places.to_c, places.to_y, places.to_d]
@@ -851,7 +928,6 @@
         gather.over_y(u)
     f.vectors[places.rep] = f.vector_share[...]
     f.tables[places.rep] = f.table_share[...]
-    f.start()
     saves = []
 
     def save(k, source, target):
@@ -862,7 +938,9 @@
     def pump(t):
         gather.pump(t, AHEAD)
 
+    f.start()
     pump(0)
+    f.turns()
     pump(1)
     pump(2)
     for copy in packs:
@@ -918,15 +996,236 @@
     gather.drain()
 
 
+class Source(NamedTuple):
+    rows: int
+    parts: Any
+    columns: int
+
+    @property
+    def depth(self):
+        return sum(self.parts)
+
+
+SOURCE_POST = Source((H + E) // 4, (ROWS,), H)
+SOURCE_1024 = Source(H // 4, (ROWS,), H)
+SOURCE_MAN_ENC = Source(H // 4, (2 * ROWS,), 2 * U)
+SOURCE_GRU = Source(H // 2, (ROWS,), 3 * H)
+SOURCE_GOAL_OUT = Source(U // 4, (ROWS, ROWS), H)
+SOURCE_GOAL_IN = Source(GCODE // 4, (ROWS, ROWS), 2 * U)
+WORKER_SHARE = (768, 1024)
+ALONG_X, ALONG_Z, ALONG_W, ALONG_Y = range(4)
+Y_FIRST = (ALONG_Y, ALONG_X, ALONG_Z, ALONG_W)
+X_FIRST = (ALONG_X, ALONG_Y, ALONG_Z, ALONG_W)
+Z_FIRST = (ALONG_Z, ALONG_Y, ALONG_X, ALONG_W)
+
+
+class Exchange:
+    def __init__(self, places, source, left_2, right_2, send_sem, recv_sem, local_sem, first):
+        self.places, self.source = (places, source)
+        self.left_2, self.right_2 = (left_2, right_2)
+        self.sems, self.first = ((send_sem, recv_sem, local_sem), first)
+        self.copies = []
+
+    def move(self, part, j, mine, target, theirs, place):
+        send_sem, recv_sem, local_sem = (sem.at[self.first + part, j] for sem in self.sems)
+        remote = send_to(theirs, place, send_sem, recv_sem, self.places.to_c)
+        local = pltpu.make_async_copy(mine, target, local_sem)
+        remote.start()
+        local.start()
+        self.copies += [remote, local]
+
+    def lows(self, part):
+        low = sum(self.source.parts[:part])
+        depth = self.source.parts[part]
+        return (pl.ds(low, depth), pl.ds(self.source.depth + low, depth))
+
+    def start_left(self, part, left):
+        low, high = self.lows(part)
+        for y in range(2):
+            ours, theirs = (
+                pl.ds(pl.multiple_of((2 * y + core) * self.source.rows, 16), self.source.rows)
+                for core in (self.places.c, 1 - self.places.c)
+            )
+            self.move(
+                part, y, left.at[ours], self.left_2.at[y, :, low],
+                left.at[theirs], self.left_2.at[y, :, high],
+            )
+
+    def start_right(self, part, right):
+        low, high = self.lows(part)
+        self.move(part, 2, right, self.right_2.at[low], right, self.right_2.at[high])
+
+    def start(self, part, left, right):
+        self.start_right(part, right)
+        self.start_left(part, left)
+
+    def ready(self):
+        while self.copies:
+            self.copies.pop(0).wait()
+
+    def term(self, y, rows, lanes):
+        return product(self.left_2[y, rows, :], self.right_2[:, lanes])
+
+
+class Addition:
+    def __init__(self, places, own, sibling, send_sem, recv_sem, local_sem):
+        self.places, self.own, self.sibling = (places, own, sibling)
+        self.sems = (send_sem, recv_sem, local_sem)
+        self.copies = []
+
+    def start(self, whole):
+        rows = self.own.shape[1]
+        for y in range(2):
+            ours, theirs = (
+                pl.ds(pl.multiple_of((2 * y + core) * rows, 16), rows)
+                for core in (self.places.c, 1 - self.places.c)
+            )
+            send_sem, recv_sem, local_sem = (sem.at[y] for sem in self.sems)
+            remote = send_to(
+                whole.at[theirs], self.sibling.at[y], send_sem, recv_sem, self.places.to_c
+            )
+            local = pltpu.make_async_copy(whole.at[ours], self.own.at[y], local_sem)
+            remote.start()
+            local.start()
+            self.copies += [remote, local]
+
+    def ready(self):
+        while self.copies:
+            self.copies.pop(0).wait()
+
+    def term(self, y, rows, lanes):
+        return self.own[y, rows, lanes].astype(F32) + self.sibling[y, rows, lanes].astype(F32)
+
+
+class Halving:
+    def __init__(self, places, units, outbox, inbox, send_sem, recv_sem, outs, groups):
+        self.units, self.groups = (units, groups)
+        self.outbox, self.inbox, self.outs = (outbox, inbox, outs)
+        self.send_sem, self.recv_sem = (send_sem, recv_sem)
+        self.bits = (places.x, places.z, places.w, places.y)
+        self.peers = (places.to_x, places.to_z, places.to_w, places.to_y)
+        self.copies = {}
+
+    def block(self, u, k, j):
+        source, stride, offset, order, first, count = self.units[u]
+        place = {}
+        for i, along in enumerate(order):
+            if i < k:
+                place[along] = self.bits[along]
+            elif i == k:
+                place[along] = 1 - self.bits[along]
+            else:
+                place[along] = lax.rem(j // (1 << (3 - i)), 2)
+        device = place[ALONG_W] * 4 + place[ALONG_Z] * 2 + place[ALONG_X]
+        lanes = pl.ds(pl.multiple_of(device * stride + offset, LANES), LANES)
+        total = source.term(place[ALONG_Y], pl.ds(first, count), lanes)
+        for i in range(k):
+            index = 0
+            for p in range(i + 1, 4):
+                index = index * 2 + place[order[p]]
+            total = total + self.inbox[u][i][index].astype(F32)
+        return total
+
+    def step(self, u, k):
+        if k == 0:
+            self.units[u][0].ready()
+        else:
+            self.copies[u, k - 1].wait_recv()
+        if k == 4:
+            self.outs[u][...] = self.block(u, 4, 0)
+            return
+
+        def one(j, carry):
+            self.outbox[u][k][j] = self.block(u, k, j).astype(BF)
+            return carry
+
+        if k == 3:
+            one(0, 0)
+        else:
+            lax.fori_loop(0, 1 << (3 - k), one, 0)
+        copy = send_to(
+            self.outbox[u][k], self.inbox[u][k], self.send_sem.at[u, k], self.recv_sem.at[u, k],
+            self.peers[self.units[u][3][k]],
+        )
+        copy.start()
+        self.copies[u, k] = copy
+
+    def slot(self, t):
+        for k in range(5):
+            if 0 <= t - k < len(self.groups):
+                for u in self.groups[t - k]:
+                    self.step(u, k)
+
+    def drain(self):
+        for copy in self.copies.values():
+            copy.wait_send()
+
+
+def boxes(units):
+    return tuple(
+        tuple(kept(1 << (3 - k), unit[-1], LANES) for k in range(4)) for unit in units
+    )
+
+
+HEAD_POST, HEAD_PRIOR, HEAD_POST_OUT, HEAD_PRIOR_OUT, HEAD_MAN_ENC = range(5)
+HEAD_SOURCES = (SOURCE_POST, SOURCE_1024, SOURCE_1024, SOURCE_1024, SOURCE_MAN_ENC)
+HEAD_UNITS = (
+    (HEAD_POST, 128, 0, Y_FIRST, 0, 128),
+    (HEAD_PRIOR, 128, 0, X_FIRST, 0, 256),
+    (HEAD_POST_OUT, 128, 0, Z_FIRST, 0, 128),
+    (HEAD_POST, 128, 0, Y_FIRST, 128, 128),
+    (HEAD_POST, 128, 0, X_FIRST, 384, 256),
+    (HEAD_POST_OUT, 128, 0, Z_FIRST, 128, 128),
+    (HEAD_POST, 128, 0, Y_FIRST, 256, 128),
+    (HEAD_MAN_ENC, 128, 0, X_FIRST, 0, 256),
+    (HEAD_PRIOR_OUT, 128, 0, Z_FIRST, 0, 256),
+)
+HEAD_GROUPS = ((0, 1, 2), (3, 4, 5), (6, 7, 8))
+LAST_WORKER, LAST_GOAL_OUT, LAST_GOAL_IN, LAST_GRU, LAST_IMG = range(5)
+LAST_SOURCES = (None, SOURCE_GOAL_OUT, SOURCE_GOAL_IN, SOURCE_GRU, SOURCE_1024)
+LAST_UNITS = (
+    (LAST_WORKER, 128, 0, Y_FIRST, 0, 256),
+    (LAST_WORKER, 128, 0, X_FIRST, 256, 256),
+    (LAST_WORKER, 128, 0, Z_FIRST, 512, 256),
+    (LAST_GOAL_OUT, 128, 0, Z_FIRST, 0, 128),
+    (LAST_GOAL_IN, 128, 0, Z_FIRST, 0, 16),
+    (LAST_GRU, 384, 0, Y_FIRST, 0, 128),
+    (LAST_GRU, 384, 0, X_FIRST, 128, 256),
+    (LAST_GRU, 384, 0, Z_FIRST, 384, 128),
+    (LAST_GRU, 384, 128, Y_FIRST, 0, 128),
+    (LAST_IMG, 128, 0, X_FIRST, 0, 256),
+    (LAST_GRU, 384, 128, Z_FIRST, 384, 128),
+    (LAST_GRU, 384, 256, Y_FIRST, 0, 128),
+    (LAST_GRU, 384, 128, X_FIRST, 128, 256),
+    (LAST_GRU, 384, 256, Z_FIRST, 256, 256),
+    (LAST_GRU, 384, 256, X_FIRST, 128, 128),
+)
+LAST_EARLY = ((0, 1, 2), (3, 4))
+LAST_LATE = ((5, 6, 7), (8, 9, 10), (11, 12, 13), (14,))
+
+
+FORWARD_ROWS, BACK_ROWS = (128, 128)
+
+
 class Worker(NamedTuple):
-    meta: Any = taken(ROWS, LANES, dtype=F32)
-    samples: Any = taken(HOR, ROWS, ZG, dtype=F32)
+    goal_codes: Any = taken(GC, ROWS, dtype=jnp.int32)
+    actions: Any = taken(HOR, ROWS, dtype=jnp.int32)
+    samples: Any = taken(HOR, ZG, ROWS, dtype=jnp.int32)
     vectors: Any = taken(4, VECTOR_TILES, LANES, dtype=F32)
     tables: Any = taken(4, TABLES, LANES)
     start_state: Any = taken(ROWS, H + LANES)
     goal_out: Any = taken(U, H)
     actor_in: Any = taken(3 * H, U)
     critic_in: Any = taken(3 * H, U)
+    post_left: Any = taken(H + E, ROWS, here=False)
+    post_out_left: Any = taken(H, ROWS, here=False)
+    prior_out_left: Any = taken(H, ROWS, here=False)
+    me_left: Any = taken(H, 2 * ROWS, here=False)
+    post_right: Any = taken(ROWS, H, here=False)
+    prior_right: Any = taken(ROWS, H, here=False)
+    post_out_right: Any = taken(ROWS, Z, here=False)
+    prior_out_right: Any = taken(ROWS, Z, here=False)
+    me_right: Any = taken(2 * ROWS, 2 * U, here=False)
     worker_left: Any = given(3 * H, 2 * U)
     returned: Any = given(ROWS, H)
     goal_left: Any = given(U, ROWS)
@@ -934,8 +1233,10 @@
     goal_right: Any = given(ROWS, H)
     goal_pair: Any = given(ROWS, 2 * U)
     small: Any = given(2, 2, SMALL_TILES, LANES, dtype=F32)
+    sums: Any = tuple(given(unit[-1], LANES, dtype=F32) for unit in HEAD_UNITS)
     act_out: Any = kept(32, U)
     goal_in: Any = kept(GCODE, U)
+    action_columns: Any = kept(ROWS, LANES, dtype=F32)
     goal_normed: Any = kept(ROWS, U, dtype=F32)
     goal_inverse: Any = kept(ROWS, 1, dtype=F32)
     goal_hidden: Any = kept(ROWS, U)
@@ -943,29 +1244,40 @@
     goal_low: Any = kept(ROWS, H)
     turned: Any = kept(2 * H, ROWS)
     slot_part: Any = kept(2, ROWS, U, dtype=F32)
+    hot: Any = kept(2 * ROWS, Z)
+    pre: Any = kept(2 * ROWS, U, dtype=F32)
+    hidden: Any = kept(2 * ROWS, U)
     normed: Any = kept(2, HOR * ROWS, U, dtype=F32)
     inverse: Any = kept(2, HOR * ROWS, 1, dtype=F32)
-    hidden: Any = kept(2, HOR * ROWS, U)
     hot_turned: Any = kept(Z, HOR * ROWS)
     log_chance: Any = kept(HOR * ROWS, 32, dtype=F32)
-    chosen: Any = kept(HOR, ROWS, 1, dtype=F32)
-    value: Any = kept(HOR, ROWS, 1, dtype=F32)
-    returns: Any = kept(HOR, ROWS, 1, dtype=F32)
-    pre: Any = kept(HOR * ROWS, U, dtype=F32)
+    chosen: Any = kept(ROWS, LANES, dtype=F32)
+    value: Any = kept(ROWS, LANES, dtype=F32)
+    returns: Any = kept(ROWS, LANES, dtype=F32)
     pre_pair: Any = kept(HOR * ROWS, 2 * U)
     summed: Any = kept(2, ROWS, U, dtype=F32)
     sum_low: Any = kept(2, ROWS, U)
     sum_pair: Any = kept(ROWS, 2 * U)
+    low_512: Any = kept(ROWS, U)
+    grad_column: Any = kept(ROWS, 1, dtype=F32)
     to_state: Any = kept(ROWS, H)
     incoming: Any = kept(ROWS, H)
-    wide: Any = kept(ROWS, H, dtype=F32)
     wide_512: Any = kept(ROWS, U, dtype=F32)
     top: Any = kept(8, LANES, dtype=F32)
     top_in: Any = kept(5, 8, LANES, dtype=F32)
+    left_2: Any = tuple(kept(2, s.rows, 2 * s.depth) for s in HEAD_SOURCES)
+    right_2: Any = tuple(kept(2 * s.depth, s.columns) for s in HEAD_SOURCES)
+    outbox: Any = boxes(HEAD_UNITS)
+    inbox: Any = boxes(HEAD_UNITS)
     top_send: Any = signal(5)
     top_recv: Any = signal(5)
     state_send: Any = signal(8)
     state_recv: Any = signal(8)
+    pair_send: Any = signal(len(HEAD_SOURCES), 3)
+    pair_recv: Any = signal(len(HEAD_SOURCES), 3)
+    pair_local: Any = signal(len(HEAD_SOURCES), 3)
+    half_send: Any = signal(len(HEAD_UNITS), 4)
+    half_recv: Any = signal(len(HEAD_UNITS), 4)
 
     def gain(self, low, size):
         return vector_of(self.vectors, low, size // (4 * LANES))
@@ -980,7 +1292,8 @@
                 self.goal_in[16 * r : 16 * (r + 1), i * LANES : (i + 1) * LANES] = self.tables[
                     r, TAB_GOAL + 16 * i : TAB_GOAL + 16 * (i + 1), :
                 ]
-        hot = hot_rows(self.meta[:, 0:32], GK, GC, LANES)
+        self.action_columns[...] = columns_of(self.actions[...].astype(F32))
+        hot = hot_rows(columns_of(self.goal_codes[...].astype(F32)), GK, GC, LANES)
         self.code_turned[...] = hot.T[0:GCODE].astype(BF)
         matmul_into(self.goal_normed, hot[:, 0:GCODE].astype(BF), self.goal_in)
         hidden_rows(
@@ -1015,76 +1328,85 @@
 
             lax.fori_loop(0, U // 256, one, 0)
 
-    def forward(self):
+    def forward(self, first, last):
         gains = (self.gain(ACT_G, U), self.gain(CRI_G, U))
         head = self.gain(CRI_O, U)
         spread = class_spread(ZG, ZK, ZG, Z)
         lane = lax.broadcasted_iota(jnp.int32, (1, Z), 1)
         lane_class = jnp.bitwise_and(lane, ZK - 1).astype(F32)
-        group = lax.broadcasted_iota(jnp.int32, (Z, LANES), 1)
-        place = lax.broadcasted_iota(jnp.int32, (Z, LANES), 0)
-        inside = (place >= group * ZK) & (place < group * ZK + ZK) & (group < ZG)
+        group = lax.broadcasted_iota(jnp.int32, (Z, ZG), 1)
+        place = lax.broadcasted_iota(jnp.int32, (Z, ZG), 0)
+        inside = (place >= group * ZK) & (place < group * ZK + ZK)
         spread_turned = jnp.where(inside, 1.0, 0.0).astype(BF)
         place_class = jnp.bitwise_and(
             lax.broadcasted_iota(jnp.int32, (Z, 1), 0), ZK - 1
         ).astype(F32)
         act_lane = lax.broadcasted_iota(jnp.int32, (1, 32), 1)
-
-        def step(k, carry):
-            rows = pl.ds(pl.multiple_of(k * ROWS, ROWS), ROWS)
-            ids = self.samples[k]
-            hot = jnp.where(product(ids.astype(BF), spread) == lane_class, 1.0, 0.0).astype(BF)
-            ids_turned = jnp.concatenate(
-                [ids, jnp.zeros((ROWS, LANES - ZG), F32)], 1
-            ).T.astype(BF)
-            self.hot_turned[:, rows] = jnp.where(
-                product(spread_turned, ids_turned) == place_class, 1.0, 0.0
-            ).astype(BF)
+        step_lane = lax.broadcasted_iota(jnp.int32, (1, LANES), 1)
+
+        def pair(i, carry):
+            start = pl.multiple_of(i * 2 * ROWS, 2 * ROWS)
+            for half in range(2):
+                k = 2 * i + half
+                rows = pl.ds(pl.multiple_of(start + half * ROWS, ROWS), ROWS)
+                ids = self.samples[k].astype(F32)
+                self.hot[half * ROWS : (half + 1) * ROWS, :] = jnp.where(
+                    product(columns_of(ids)[:, 0:ZG].astype(BF), spread) == lane_class, 1.0, 0.0
+                ).astype(BF)
+                self.hot_turned[:, rows] = jnp.where(
+                    product(spread_turned, ids.astype(BF)) == place_class, 1.0, 0.0
+                ).astype(BF)
             for which, weight in enumerate((self.actor_in, self.critic_in)):
-                pre = product(hot, weight[H : 2 * H, :]) + self.slot_part[which]
-                normed, inverse = normalize(pre)
-                self.normed[which, rows, :] = normed
-                self.inverse[which, rows, :] = inverse
-                hidden = elu_of(normed * gains[which]).astype(BF)
-                self.hidden[which, rows, :] = hidden
-                if which == 0:
-                    logits = lax.dot_general(
-                        hidden, self.act_out[...], (((1,), (1,)), ((), ())),
-                        preferred_element_type=F32,
-                    )
-                    logits = jnp.where(act_lane < NA, logits, -1e30)
-                    shifted = logits - jnp.max(logits, -1, keepdims=True)
-                    total = jnp.sum(jnp.exp(shifted), -1, keepdims=True)
-                    log_chance = shifted - jnp.log(total)
-                    self.log_chance[rows, :] = log_chance
-                    self.chosen[k] = jnp.sum(
-                        jnp.where(self.action_here(k), log_chance, 0.0), -1, keepdims=True
-                    )
-                else:
-                    self.value[k] = jnp.sum(hidden.astype(F32) * head, -1, keepdims=True)
+                self.pre[...] = product(self.hot[...], weight[H : 2 * H, :])
+                for low in range(0, 2 * ROWS, FORWARD_ROWS):
+                    rows = pl.ds(pl.multiple_of(start + low, FORWARD_ROWS), FORWARD_ROWS)
+                    slot = pl.ds(low % ROWS, FORWARD_ROWS)
+                    pre = self.pre[low : low + FORWARD_ROWS, :] + self.slot_part[which, slot, :]
+                    normed, inverse = normalize(pre)
+                    self.normed[which, rows, :] = normed
+                    self.inverse[which, rows, :] = inverse
+                    hidden = elu_of(normed * gains[which]).astype(BF)
+                    if which == 0:
+                        self.hidden[low : low + FORWARD_ROWS, :] = hidden
+                    else:
+                        value = jnp.sum(hidden.astype(F32) * head, -1, keepdims=True)
+                        here = step_lane == 2 * i + low // ROWS
+                        self.value[slot, :] = jnp.where(here, value, self.value[slot, :])
+            logits = lax.dot_general(
+                self.hidden[...], self.act_out[...], (((1,), (1,)), ((), ())),
+                preferred_element_type=F32,
+            )
+            logits = jnp.where(act_lane < NA, logits, -1e30)
+            shifted = logits - jnp.max(logits, -1, keepdims=True)
+            total = jnp.sum(jnp.exp(shifted), -1, keepdims=True)
+            self.log_chance[pl.ds(start, 2 * ROWS), :] = shifted - jnp.log(total)
             return carry
 
-        lax.fori_loop(0, HOR, step, 0)
+        lax.fori_loop(first, last, pair, 0)
 
     def action_here(self, k):
-        meta = self.meta[...]
+        action = self.at_step(self.action_columns, k)
+        return action == lax.broadcasted_iota(jnp.int32, (1, 32), 1).astype(F32)
+
+    def at_step(self, ref, k):
         lane = lax.broadcasted_iota(jnp.int32, (ROWS, LANES), 1)
-        action = jnp.sum(jnp.where(lane == 32 + k, meta, 0.0), -1, keepdims=True)
-        return action == lax.broadcasted_iota(jnp.int32, (1, 32), 1).astype(F32)
+        return jnp.sum(jnp.where(lane == k, ref[...], 0.0), -1, keepdims=True)
 
     def targets(self, reward):
         weight = self.start_state[:, H : H + 1].astype(F32)
-        later = self.value[HOR - 1]
-        self.returns[HOR - 1] = later
+        lane = lax.broadcasted_iota(jnp.int32, (ROWS, LANES), 1)
+        later = self.value[:, HOR - 1 : HOR]
         result = later
-        top = jnp.zeros((ROWS, 1), F32)
+        returns = jnp.where(lane == HOR - 1, result, 0.0)
         for k in range(HOR - 2, -1, -1):
             blended = (1.0 - return_mix) * later + return_mix * result
             result = reward + discount * blended
-            self.returns[k] = result
-            later = self.value[k]
-            top = jnp.maximum(top, weight * jnp.abs(result - later))
-        self.top[...] = jnp.broadcast_to(jnp.max(top, 0, keepdims=True), (8, LANES))
+            returns = jnp.where(lane == k, result, returns)
+            later = self.value[:, k : k + 1]
+        self.returns[...] = returns
+        gaps = jnp.where(lane < HOR, jnp.abs(returns - self.value[...]), 0.0)
+        top = jnp.max(weight * gaps, 0, keepdims=True)
+        self.top[...] = jnp.broadcast_to(jnp.max(top, 1, keepdims=True), (8, LANES))
 
     def critic_back(self, first, last, total):
         gain, head = (self.gain(CRI_G, U), self.gain(CRI_O, U))
@@ -1092,19 +1414,23 @@
 
         def step(k, totals):
             rows = pl.ds(pl.multiple_of(k * ROWS, ROWS), ROWS)
-            grad = weight * (self.value[k] - self.returns[k]) * (1.0 / (ROWS * HOR))
-            self.wide_512[...] = grad * head
+            misfit = self.at_step(self.value, k) - self.at_step(self.returns, k)
+            grad = weight * misfit * (1.0 / (ROWS * HOR))
+            self.grad_column[...] = grad
+            gain_total = totals[0] + hidden_rows_back(
+                lambda r: self.grad_column[r, :] * head,
+                self.normed.at[1, rows], self.inverse.at[1, rows], gain, self.low_512, BACK_ROWS,
+                self.hidden,
+            )
             head_total = totals[1] + jnp.sum(
-                self.hidden[1, rows, :].astype(F32) * grad, 0, keepdims=True
+                self.hidden[0:ROWS, :].astype(F32) * grad, 0, keepdims=True
             )
-            gain_total = totals[0] + hidden_rows_back(
-                lambda r: self.wide_512[r, :],
-                self.normed.at[1, rows], self.inverse.at[1, rows], gain, self.pre.at[rows],
-                64,
-            )
-            low = self.pre[rows, :].astype(BF).astype(F32)
-            self.pre[rows, :] = low
-            self.summed[1] += low
+            for j in range(4):
+                tile = self.low_512[:, j * LANES : (j + 1) * LANES].astype(F32)
+                self.summed[1, :, j * LANES : (j + 1) * LANES] += tile
+                turned = pltpu.roll(tile, 64, 1)
+                self.pre_pair[rows, 2 * j * LANES : (2 * j + 1) * LANES] = turned.astype(BF)
+                self.pre_pair[rows, (2 * j + 1) * LANES : (2 * j + 2) * LANES] = tile.astype(BF)
             return (gain_total, head_total)
 
         return lax.fori_loop(first, last, step, total)
@@ -1113,46 +1439,47 @@
         lane = lax.broadcasted_iota(jnp.int32, (ROWS, LANES), 1)
         for j in range(4):
             lanes = slice(j * LANES, (j + 1) * LANES)
-            a, b = (first[:, lanes], second[:, lanes])
-            out_ref[rows, 2 * j * LANES : (2 * j + 1) * LANES] = jnp.where(
-                lane < 64, a, pltpu.roll(b, 64, 1)
-            ).astype(BF)
-            out_ref[rows, (2 * j + 1) * LANES : (2 * j + 2) * LANES] = jnp.where(
-                lane < 64, pltpu.roll(a, 64, 1), b
-            ).astype(BF)
-
-    def actor_back(self):
+            even = slice(2 * j * LANES, (2 * j + 1) * LANES)
+            odd = slice((2 * j + 1) * LANES, (2 * j + 2) * LANES)
+            a = first[:, lanes].astype(F32)
+            if second is None:
+                b_even, b_odd = (out_ref[rows, even].astype(F32), out_ref[rows, odd].astype(F32))
+            else:
+                b_odd = second[:, lanes].astype(F32)
+                b_even = pltpu.roll(b_odd, 64, 1)
+            out_ref[rows, even] = jnp.where(lane < 64, a, b_even).astype(BF)
+            out_ref[rows, odd] = jnp.where(lane < 64, pltpu.roll(a, 64, 1), b_odd).astype(BF)
+
+    def actor_back(self, first, last, totals):
         gain = self.gain(ACT_G, U)
         weight = self.start_state[:, H : H + 1].astype(F32)
         scale = self.top[0:1, 0:1] + small_floor
 
         def step(k, totals):
             rows = pl.ds(pl.multiple_of(k * ROWS, ROWS), ROWS)
-            advantage = self.returns[k] - self.value[k]
-            chosen_grad = -weight * advantage / scale * (1.0 / (ROWS * HOR))
-            hot = jnp.where(self.action_here(k), 1.0, 0.0)
-            grad = chosen_grad * (hot - jnp.exp(self.log_chance[rows, :]))
-            grad_low = grad.astype(BF)
+            advantage = self.at_step(self.returns, k) - self.at_step(self.value, k)
+            gained = weight * advantage / scale
+            here = self.action_here(k)
+            log_chance = self.log_chance[rows, :]
+            chance = jnp.exp(log_chance)
+            grad = (gained * (-1.0 / (ROWS * HOR))) * (jnp.where(here, 1.0, 0.0) - chance)
             grad_turned = jnp.concatenate(
                 [grad, jnp.zeros((ROWS, LANES - 32), F32)], 1
             ).T[0:32].astype(BF)
-            out_total = totals[1] + product(grad_turned, self.hidden[0, rows, :])
-            self.wide_512[...] = product(grad_low, self.act_out[...])
+            self.wide_512[...] = product(grad.astype(BF), self.act_out[...])
             gain_total = totals[0] + hidden_rows_back(
                 lambda r: self.wide_512[r, :],
-                self.normed.at[0, rows], self.inverse.at[0, rows], gain,
-                self.normed.at[0, rows], 64,
+                self.normed.at[0, rows], self.inverse.at[0, rows], gain, self.low_512, BACK_ROWS,
+                self.hidden,
             )
-            low = self.normed[0, rows, :].astype(BF).astype(F32)
-            self.summed[0] += low
-            self.pair(low, self.pre[rows, :], self.pre_pair, rows)
-            loss = totals[2] + jnp.sum(
-                weight * self.chosen[k] * advantage / scale, 0, keepdims=True
-            )
+            out_total = totals[1] + product(grad_turned, self.hidden[0:ROWS, :])
+            self.summed[0] += self.low_512[...].astype(F32)
+            self.pair(self.low_512, None, self.pre_pair, rows)
+            chosen = jnp.sum(jnp.where(here, log_chance, 0.0), -1, keepdims=True)
+            loss = totals[2] + jnp.sum(chosen * gained, 0, keepdims=True)
             return (gain_total, out_total, loss)
 
-        start = (jnp.zeros((1, U), F32), jnp.zeros((32, U), F32), jnp.zeros((1, 1), F32))
-        return lax.fori_loop(0, HOR, step, start)
+        return lax.fori_loop(first, last, step, totals)
 
     def inputs_back(self, low, out_ref):
         def one(j, carry):
@@ -1199,11 +1526,35 @@
     greet(
         [(places.around(o), places.rep) for o in range(1, 8)] + [places.to_c, places.to_y]
     )
+    heads = []
+    lefts = (f.post_left, f.post_left, f.post_out_left, f.prior_out_left, f.me_left)
+    rights = (f.post_right, f.prior_right, f.post_out_right, f.prior_out_right, f.me_right)
+    for i, source in enumerate(HEAD_SOURCES):
+        heads.append(
+            Exchange(
+                places, source, f.left_2[i], f.right_2[i], f.pair_send, f.pair_recv,
+                f.pair_local, i,
+            )
+        )
+    for i in (HEAD_POST, HEAD_PRIOR, HEAD_POST_OUT):
+        heads[i].start(0, lefts[i], rights[i])
+    halving = Halving(
+        places, [(heads[unit[0]],) + unit[1:] for unit in HEAD_UNITS], f.outbox, f.inbox,
+        f.half_send, f.half_recv, f.sums, HEAD_GROUPS,
+    )
     reward = f.goal()
+    halving.slot(0)
+    for i in (HEAD_MAN_ENC, HEAD_PRIOR_OUT):
+        heads[i].start(0, lefts[i], rights[i])
     f.slots()
-    f.forward()
+    f.value[...] = jnp.zeros(f.value.shape, F32)
+    f.summed[...] = jnp.zeros(f.summed.shape, F32)
+    f.forward(0, 3)
+    halving.slot(1)
+    f.forward(3, 6)
+    halving.slot(2)
+    f.forward(6, HOR // 2)
     f.targets(reward)
-    f.summed[...] = jnp.zeros(f.summed.shape, F32)
     totals = (jnp.zeros((1, U), F32), jnp.zeros((1, U), F32))
     steps = (0, 3, 6, 9, 12, HOR)
     for k in range(5):
@@ -1212,39 +1563,43 @@
         totals = f.critic_back(steps[k], steps[k + 1], totals)
         copy.wait()
         f.top[...] = jnp.maximum(f.top[...], f.top_in[k])
+        if k == 1:
+            halving.slot(3)
     put_vector(f.small, CRI_G, totals[0])
     put_vector(f.small, CRI_O, totals[1])
-    actor_gain, actor_out, chosen = f.actor_back()
+    halving.slot(4)
+    totals = (jnp.zeros((1, U), F32), jnp.zeros((32, U), F32), jnp.zeros((1, 1), F32))
+    totals = f.actor_back(0, HOR // 2, totals)
+    halving.slot(5)
+    actor_gain, actor_out, chosen = f.actor_back(HOR // 2, HOR, totals)
     put_vector(f.small, ACT_G, actor_gain)
     put_table(f.small, ACT_T, actor_out, 24)
+    for which in range(2):
+        f.sum_low[which] = f.summed[which].astype(BF)
+    f.inputs_back(0, f.to_state)
+    states = regroup_start(places, f.to_state, f.incoming, f.state_send, f.state_recv)
+    f.pair(f.sum_low.at[0], f.sum_low.at[1], f.sum_pair, slice(0, ROWS))
+    f.inputs_back(2 * H, f.goal_right)
+    f.goal_back()
+    halving.slot(6)
     weight = f.start_state[:, H : H + 1].astype(F32)
-    squares = jnp.zeros((ROWS, 1), F32)
-    for k in range(HOR):
-        misfit = f.value[k] - f.returns[k]
-        squares = squares + misfit * misfit
-    loss = (0.5 * jnp.sum(weight * squares, 0, keepdims=True) - chosen) * (1.0 / (ROWS * HOR))
+    misfit = f.value[...] - f.returns[...]
+    squares = jnp.sum(jnp.sum(weight * misfit * misfit, -1, keepdims=True), 0, keepdims=True)
+    loss = (0.5 * squares - chosen) * (1.0 / (ROWS * HOR))
     for y in range(2):
         for c in range(2):
             f.small[c, y, LOSS : LOSS + 1, :] = jnp.broadcast_to(loss, (1, LANES))
-    for which in range(2):
-        f.sum_low[which] = f.summed[which].astype(BF)
-    everything = pl.ds(0, ROWS)
-    f.pair(f.sum_low[0].astype(F32), f.sum_low[1].astype(F32), f.sum_pair, everything)
-    f.inputs_back(0, f.to_state)
-    states = regroup_start(places, f.to_state, f.incoming, f.state_send, f.state_recv)
-    f.inputs_back(2 * H, f.goal_right)
-    f.goal_back()
     f.weights()
     for copy in states:
         copy.wait()
     f.returned[...] = f.incoming[...]
-
-
-class Back(NamedTuple):
-    meta: Any = taken(ROWS, LANES, dtype=F32)
+    halving.drain()
+
+
+class Last(NamedTuple):
+    meta_turned: Any = taken(LANES, ROWS, dtype=F32)
     prev: Any = taken(ROWS, H)
     vectors: Any = taken(4, VECTOR_TILES, LANES, dtype=F32)
-    gru_weight: Any = taken(2 * H, 3 * H)
     returned: Any = taken(ROWS, H)
     grad_partial: Any = taken(ROWS, H, dtype=F32)
     gru_normed: Any = taken(ROWS, 3 * H, dtype=F32)
@@ -1253,302 +1608,270 @@
     img_inverse: Any = taken(ROWS, 1, dtype=F32)
     small_1: Any = taken(2, 2, SMALL_TILES, LANES, dtype=F32)
     small_2: Any = taken(2, 2, SMALL_TILES, LANES, dtype=F32)
+    gru_share: Any = taken(2 * H, 3 * H, here=False)
+    worker_left: Any = taken(3 * H, 2 * U, here=False)
+    goal_left: Any = taken(U, ROWS, here=False)
+    dec_left: Any = taken(U, ROWS, here=False)
+    code_turned: Any = taken(GCODE, ROWS, here=False)
+    soft_turned: Any = taken(GCODE, ROWS, here=False)
+    gru_left: Any = taken(2 * H, ROWS, here=False)
+    img_left: Any = taken(Z, ROWS, here=False)
+    goal_right: Any = taken(ROWS, H, here=False)
+    recon_low: Any = taken(ROWS, H, here=False)
+    goal_pair: Any = taken(ROWS, 2 * U, here=False)
+    dec_pair: Any = taken(ROWS, 2 * U, here=False)
     deter_grad: Any = given(ROWS, H, dtype=F32)
-    gru_right: Any = given(ROWS, 3 * H)
-    img_right: Any = given(ROWS, H)
-    small: Any = given(2, 2, SMALL_TILES, LANES, dtype=F32)
+    small_sum: Any = given(SMALL_TILES, LANES, dtype=F32)
+    sums: Any = tuple(given(unit[-1], LANES, dtype=F32) for unit in LAST_UNITS)
+    gru_weight: Any = kept(2 * H, 3 * H)
+    gru_right: Any = kept(ROWS, 3 * H)
+    img_right: Any = kept(ROWS, H)
     grad: Any = kept(ROWS, H, dtype=F32)
     wide: Any = kept(ROWS, 2 * H, dtype=F32)
-
-
-def back_kernel(f):
-    f.small[...] = f.small_1[...] + f.small_2[...]
-    gain = vector_of(f.vectors, GRU_G, 6)
-    meta = f.meta[...]
-    lane = lax.broadcasted_iota(jnp.int32, (ROWS, LANES), 1)
-    order = jnp.where(lane == 37, meta, 0.0).T[37:38, :]
-    frame = lax.broadcasted_iota(jnp.int32, (ROWS, ROWS), 0).astype(F32)
-    place = jnp.where(order == frame, 1.0, 0.0).astype(BF)
-
-    def add(j, carry):
-        lanes = pl.ds(pl.multiple_of(j * 256, 256), 256)
-        f.grad[:, lanes] = f.grad_partial[:, lanes] + product(place, f.returned[:, lanes])
-        return carry
-
-    lax.fori_loop(0, H // 256, add, 0)
-
-    def one(rows, total):
-        normed = f.gru_normed[rows, :]
-        parts = normed * gain
-        inner = parts[:, H : 2 * H]
-        reset = 1.0 / (1.0 + jnp.exp(-parts[:, :H]))
-        candidate = jnp.tanh(reset * inner)
-        update = 1.0 / (1.0 + jnp.exp(1.0 - parts[:, 2 * H :]))
-        grad = f.grad[rows, :]
-        prev = f.prev[rows, :].astype(F32)
-        grad_inner = grad * update * (1.0 - candidate * candidate)
-        grad_parts = jnp.concatenate(
-            [
-                grad_inner * inner * reset * (1.0 - reset),
-                grad_inner * reset,
-                grad * (candidate - prev) * update * (1.0 - update),
-            ],
-            1,
-        )
-        f.deter_grad[rows, :] = grad * (1.0 - update)
-        total = total + jnp.sum(grad_parts * normed, 0, keepdims=True)
-        back = normalize_back(grad_parts * gain, normed, f.gru_inverse[rows, :])
-        f.gru_right[rows, :] = back.astype(BF)
-        return total
-
-    put_vector(f.small, GRU_G, by_rows(ROWS, 16, one, jnp.zeros((1, 3 * H), F32)))
-    matmul_into(f.wide, f.gru_right[...], f.gru_weight, turned=True)
-    f.deter_grad[...] += f.wide[:, H : 2 * H]
-    total = hidden_rows_back(
-        lambda rows: f.wide[rows, 0:H],
-        f.img_normed, f.img_inverse, vector_of(f.vectors, IMG_G, 2), f.img_right,
-    )
-    put_vector(f.small, IMG_G, total)
-    lane = lax.broadcasted_iota(jnp.int32, (ROWS, LANES), 1)
-    action = jnp.sum(jnp.where(lane == 32, meta, 0.0), -1, keepdims=True)
-    hot = jnp.where(action == lane.astype(F32), 1.0, 0.0).T[0:24].astype(BF)
-    for r in range(4):
-        for i in range(2):
-            start = (2 * r + i) * LANES
-            f.small[r % 2, r // 2, IMG_T + 24 * i : IMG_T + 24 * (i + 1), :] = product(
-                hot, f.img_right[:, start : start + LANES]
+    small: Any = kept(2, 2, SMALL_TILES, LANES, dtype=F32)
+    small_pair: Any = kept(2, SMALL_TILES, LANES, dtype=F32)
+    small_in: Any = kept(4, SMALL_TILES, LANES, dtype=F32)
+    worker_own: Any = kept(2, *WORKER_SHARE)
+    worker_sibling: Any = kept(2, *WORKER_SHARE)
+    left_2: Any = tuple(kept(2, s.rows, 2 * s.depth) for s in LAST_SOURCES[1:])
+    right_2: Any = tuple(kept(2 * s.depth, s.columns) for s in LAST_SOURCES[1:])
+    outbox: Any = boxes(LAST_UNITS)
+    inbox: Any = boxes(LAST_UNITS)
+    load_done: Any = signal(1)
+    add_send: Any = signal(2)
+    add_recv: Any = signal(2)
+    add_local: Any = signal(2)
+    pair_send: Any = signal(6, 3)
+    pair_recv: Any = signal(6, 3)
+    pair_local: Any = signal(6, 3)
+    half_send: Any = signal(len(LAST_UNITS), 4)
+    half_recv: Any = signal(len(LAST_UNITS), 4)
+    small_send: Any = signal(5)
+    small_recv: Any = signal(5)
+
+    def state_back(self):
+        gain = vector_of(self.vectors, GRU_G, 6)
+        frame = lax.broadcasted_iota(jnp.int32, (ROWS, ROWS), 0).astype(F32)
+        place = jnp.where(self.meta_turned[37:38, :] == frame, 1.0, 0.0).astype(BF)
+
+        def add(j, carry):
+            lanes = pl.ds(pl.multiple_of(j * 256, 256), 256)
+            self.grad[:, lanes] = self.grad_partial[:, lanes] + product(
+                place, self.returned[:, lanes]
             )
-
-
-class Source(NamedTuple):
-    rows: int
-    parts: Any
-    columns: int
-
-    @property
-    def depth(self):
-        return sum(self.parts)
-
-
-GRU, POST, PRIOR, POST_OUT, PRIOR_OUT, IMG, MAN_ENC, GOAL_OUT, GOAL_IN, WORKER = range(10)
-SOURCES = (
-    Source(512, (ROWS,), 3072),
-    Source(640, (ROWS,), 1024),
-    Source(256, (ROWS,), 1024),
-    Source(256, (ROWS,), 1024),
-    Source(256, (ROWS,), 1024),
-    Source(256, (ROWS,), 1024),
-    Source(256, (2 * ROWS,), 1024),
-    Source(128, (ROWS, ROWS), 1024),
-    Source(16, (ROWS, ROWS), 1024),
-)
-WORKER_SHARE = (768, 1024)
-ALONG_X, ALONG_Z, ALONG_W, ALONG_Y = range(4)
-Y_FIRST = (ALONG_Y, ALONG_X, ALONG_Z, ALONG_W)
-X_FIRST = (ALONG_X, ALONG_Z, ALONG_Y, ALONG_W)
-Z_FIRST = (ALONG_Z, ALONG_Y, ALONG_X, ALONG_W)
-UNITS = (
-    (POST, 128, 0, Y_FIRST),
-    (WORKER, 128, 0, X_FIRST),
-    (POST_OUT, 128, 0, Z_FIRST),
-    (GRU, 384, 0, Y_FIRST),
-    (GRU, 384, 128, X_FIRST),
-    (GRU, 384, 256, Z_FIRST),
-    (PRIOR_OUT, 128, 0, Y_FIRST),
-    (IMG, 128, 0, X_FIRST),
-    (PRIOR, 128, 0, Z_FIRST),
-    (MAN_ENC, 128, 0, Y_FIRST),
-    (GOAL_OUT, 128, 0, X_FIRST),
-    (GOAL_IN, 128, 0, Z_FIRST),
-)
-
-
-def unit_rows(unit):
-    return WORKER_SHARE[0] if unit[0] == WORKER else SOURCES[unit[0]].rows
-
-
-def reduce_kernel(*refs):
-    count, units = (len(SOURCES), len(UNITS))
-    parts = sum(len(source.parts) for source in SOURCES)
-    refs = iter(refs)
-
-    def take(number):
-        return [next(refs) for _ in range(number)]
-
-    left_parts, right_parts = (take(parts), take(parts))
-    worker, small = take(2)
-    outs, (small_out,) = (take(units), take(1))
-    left_2, right_2 = (take(count), take(count))
-    worker_own, worker_sib = take(2)
-    outbox = [take(4) for _ in range(units)]
-    inbox = [take(4) for _ in range(units)]
-    small_in = take(5)
-    ex_send, ex_recv, wk_send, wk_recv, wk_local, st_send, st_recv, sm_send, sm_recv = take(9)
-    places = Places()
-    core = places.c
-    bits = (places.x, places.z, places.w, places.y)
-    peers = (places.to_x, places.to_z, places.to_w, places.to_y)
-    greet((places.to_c,) + peers)
-    exchange, own = ([], [])
-    part = 0
-    for s, source in enumerate(SOURCES):
-        group, low = ([], 0)
-        for depth in source.parts:
-            left, right = (left_parts[part], right_parts[part])
-            high = source.depth + low
-            group.append(
-                send_to(
-                    right, right_2[s].at[pl.ds(high, depth)],
-                    ex_send.at[part, 0], ex_recv.at[part, 0], places.to_c,
+            return carry
+
+        lax.fori_loop(0, H // 256, add, 0)
+
+        def one(rows, total):
+            normed = self.gru_normed[rows, :]
+            parts = normed * gain
+            inner = parts[:, H : 2 * H]
+            reset = 1.0 / (1.0 + jnp.exp(-parts[:, :H]))
+            candidate = jnp.tanh(reset * inner)
+            update = 1.0 / (1.0 + jnp.exp(1.0 - parts[:, 2 * H :]))
+            grad = self.grad[rows, :]
+            prev = self.prev[rows, :].astype(F32)
+            grad_inner = grad * update * (1.0 - candidate * candidate)
+            grad_parts = jnp.concatenate(
+                [
+                    grad_inner * inner * reset * (1.0 - reset),
+                    grad_inner * reset,
+                    grad * (candidate - prev) * update * (1.0 - update),
+                ],
+                1,
+            )
+            self.deter_grad[rows, :] = grad * (1.0 - update)
+            total = total + jnp.sum(grad_parts * normed, 0, keepdims=True)
+            back = normalize_back(grad_parts * gain, normed, self.gru_inverse[rows, :])
+            self.gru_right[rows, :] = back.astype(BF)
+            return total
+
+        put_vector(self.small, GRU_G, by_rows(ROWS, 16, one, jnp.zeros((1, 3 * H), F32)))
+
+    def input_back(self):
+        matmul_into(self.wide, self.gru_right[...], self.gru_weight, turned=True)
+        self.deter_grad[...] += self.wide[:, H : 2 * H]
+        total = hidden_rows_back(
+            lambda rows: self.wide[rows, 0:H],
+            self.img_normed, self.img_inverse, vector_of(self.vectors, IMG_G, 2), self.img_right,
+        )
+        put_vector(self.small, IMG_G, total)
+
+    def action_back(self):
+        place = lax.broadcasted_iota(jnp.int32, (24, ROWS), 0).astype(F32)
+        hot = jnp.where(self.meta_turned[32:33, :] == place, 1.0, 0.0).astype(BF)
+        for r in range(4):
+            for i in range(2):
+                start = (2 * r + i) * LANES
+                low = IMG_T + 24 * i
+                self.small[r % 2, r // 2, low : low + 24, :] = product(
+                    hot, self.img_right[:, start : start + LANES]
                 )
+
+
+class SmallSum:
+    def __init__(self, places, f):
+        self.places, self.f = (places, f)
+        self.copies = []
+
+    def step(self, k):
+        f, places = (self.f, self.places)
+        if k > 0:
+            self.copies[k - 1].wait()
+        if k == 0:
+            source, target, device = (f.small.at[1 - places.c], f.small_pair, places.to_c)
+        elif k == 1:
+            f.small_pair[...] = f.small_pair[...] + f.small[places.c]
+            source, target, device = (
+                f.small_pair.at[1 - places.y], f.small_in.at[0], places.to_y,
             )
-            for y in range(2):
-                start = (2 * y + 1 - core) * source.rows
-                group.append(
-                    send_to(
-                        left.at[pl.ds(pl.multiple_of(start, 16), source.rows)],
-                        left_2[s].at[y, :, pl.ds(high, depth)],
-                        ex_send.at[part, 1 + y], ex_recv.at[part, 1 + y], places.to_c,
-                    )
-                )
-            own.append((s, left, right, low, depth))
-            low += depth
-            part += 1
-        exchange.append(group)
-    group = []
-    for y in range(2):
-        theirs = pl.ds(pl.multiple_of((2 * y + 1 - core) * WORKER_SHARE[0], 16), WORKER_SHARE[0])
-        ours = pl.ds(pl.multiple_of((2 * y + core) * WORKER_SHARE[0], 16), WORKER_SHARE[0])
-        group.append(
-            send_to(worker.at[theirs], worker_sib.at[y], wk_send.at[y], wk_recv.at[y], places.to_c)
-        )
-        group.append(pltpu.make_async_copy(worker.at[ours], worker_own.at[y], wk_local.at[y]))
-    exchange.append(group)
-    for unit in UNITS:
-        for copy in exchange[unit[0]] if unit[2] == 0 else ():
-            copy.start()
-    for s, left, right, low, depth in own:
-        right_2[s][low : low + depth] = right[...]
-        for y in range(2):
-            start = pl.multiple_of((2 * y + core) * SOURCES[s].rows, 16)
-            left_2[s][y, :, low : low + depth] = left[pl.ds(start, SOURCES[s].rows)]
-    arrived = set()
-
-    def term(u, y, device):
-        s, stride, offset, _ = UNITS[u]
-        lanes = pl.ds(pl.multiple_of(device * stride + offset, LANES), LANES)
-        if s == WORKER:
-            return worker_own[y, :, lanes].astype(F32) + worker_sib[y, :, lanes].astype(F32)
-        return product(left_2[s][y], right_2[s][:, lanes])
-
-    def block(u, k, j):
-        order = UNITS[u][3]
-        place = {}
-        for i, along in enumerate(order):
-            if i < k:
-                place[along] = bits[along]
-            elif i == k:
-                place[along] = 1 - bits[along]
-            else:
-                place[along] = lax.rem(j // (1 << (3 - i)), 2)
-        device = place[ALONG_W] * 4 + place[ALONG_Z] * 2 + place[ALONG_X]
-        total = term(u, place[ALONG_Y], device)
-        for i in range(k):
-            index = 0
-            for p in range(i + 1, 4):
-                index = index * 2 + place[order[p]]
-            total = total + inbox[u][i][index].astype(F32)
-        return total
-
-    started = {}
-
-    def step(u, k):
-        s = UNITS[u][0]
-        if s not in arrived:
-            arrived.add(s)
-            for copy in exchange[s]:
-                copy.wait()
-        if k > 0:
-            started[u, k - 1].wait_recv()
-
-        def one(j, carry):
-            outbox[u][k][j] = block(u, k, j).astype(BF)
-            return carry
-
-        if k == 3:
-            one(0, 0)
-        else:
-            lax.fori_loop(0, 1 << (3 - k), one, 0)
-        copy = send_to(
-            outbox[u][k], inbox[u][k], st_send.at[u, k], st_recv.at[u, k], peers[UNITS[u][3][k]]
-        )
-        copy.start()
-        started[u, k] = copy
-
-    small_copies = []
-
-    def small_step(k):
-        if k > 0:
-            small_copies[k - 1].wait()
-        if k == 0:
-            source, target, device = (small.at[1 - core], small_in[0], places.to_c)
-        elif k == 1:
-            small_in[0][...] = small_in[0][...] + small[core]
-            source, target, device = (small_in[0].at[1 - places.y], small_in[1], places.to_y)
         else:
             if k == 2:
-                small_out[...] = small_in[0][places.y] + small_in[1][...]
+                f.small_sum[...] = f.small_pair[places.y] + f.small_in[0]
             else:
-                small_out[...] = small_out[...] + small_in[k - 1][...]
+                f.small_sum[...] = f.small_sum[...] + f.small_in[k - 2]
             if k == 5:
                 return
-            source, target, device = (small_out, small_in[k], peers[k - 2])
-        copy = send_to(source, target, sm_send.at[k], sm_recv.at[k], device)
+            device = (places.to_x, places.to_z, places.to_w)[k - 2]
+            source, target = (f.small_sum, f.small_in.at[k - 1])
+        copy = send_to(source, target, f.small_send.at[k], f.small_recv.at[k], device)
         copy.start()
-        small_copies.append(copy)
-
-    small_step(0)
-    for k in range(4):
-        for u in range(units):
-            step(u, k)
-        small_step(k + 1)
-    for u in range(units):
-        started[u, 3].wait_recv()
-        outs[u][...] = block(u, 4, 0)
-    small_step(5)
-    for copy in started.values():
-        copy.wait_send()
-
-
-def reduce_call(left, right, worker, small):
-    vmem, dma = (pltpu.VMEM, pltpu.SemaphoreType.DMA)
-    parts, units = (len(left), len(UNITS))
-    scratch = [vmem((2, s.rows, 2 * s.depth), BF) for s in SOURCES]
-    scratch += [vmem((2 * s.depth, s.columns), BF) for s in SOURCES]
-    scratch += [vmem((2,) + WORKER_SHARE, BF)] * 2
-    for _ in range(2):
-        for unit in UNITS:
-            scratch += [vmem((1 << (3 - k), unit_rows(unit), LANES), BF) for k in range(4)]
-    scratch += [vmem((2, SMALL_TILES, LANES), F32)] + [vmem((SMALL_TILES, LANES), F32)] * 4
-    scratch += [dma((parts, 3))] * 2 + [dma((2,))] * 3 + [dma((units, 4))] * 2 + [dma((5,))] * 2
-    whole = pl.BlockSpec(memory_space=vmem)
-    anywhere = pl.BlockSpec(memory_space=pl.ANY)
-    out = pl.pallas_call(
-        reduce_kernel,
-        out_shape=[jax.ShapeDtypeStruct((unit_rows(unit), LANES), F32) for unit in UNITS]
-        + [jax.ShapeDtypeStruct((SMALL_TILES, LANES), F32)],
-        in_specs=[whole] * (2 * parts) + [anywhere, whole],
-        out_specs=[whole] * (units + 1),
-        scratch_shapes=scratch,
-        compiler_params=pltpu.CompilerParams(
-            collective_id=2, has_side_effects=True, vmem_limit_bytes=VMEM_BYTES
-        ),
-        name="reduce",
-    )(*left, *right, worker, small)
-    large = {}
-    for (source, _, _, _), value in zip(UNITS, out):
-        large.setdefault(source, []).append(value)
-    return (large, out[units])
+        self.copies.append(copy)
+
+
+def last_kernel(f):
+    places = Places()
+    load = pltpu.make_async_copy(f.gru_share, f.gru_weight, f.load_done.at[0])
+    load.start()
+    greet((places.to_c, places.to_y, places.to_x, places.to_z, places.to_w))
+    worker = Addition(
+        places, f.worker_own, f.worker_sibling, f.add_send, f.add_recv, f.add_local
+    )
+    worker.start(f.worker_left)
+    sources, part = ([worker], 0)
+    for i, source in enumerate(LAST_SOURCES[1:]):
+        sources.append(
+            Exchange(
+                places, source, f.left_2[i], f.right_2[i], f.pair_send, f.pair_recv,
+                f.pair_local, part,
+            )
+        )
+        part += len(source.parts)
+    sources[LAST_GOAL_OUT].start(0, f.goal_left, f.goal_right)
+    sources[LAST_GOAL_OUT].start(1, f.dec_left, f.recon_low)
+    sources[LAST_GOAL_IN].start(0, f.code_turned, f.goal_pair)
+    sources[LAST_GOAL_IN].start(1, f.soft_turned, f.dec_pair)
+    sources[LAST_GRU].start_left(0, f.gru_left)
+    sources[LAST_IMG].start_left(0, f.img_left)
+    halving = Halving(
+        places, [(sources[unit[0]],) + unit[1:] for unit in LAST_UNITS], f.outbox, f.inbox,
+        f.half_send, f.half_recv, f.sums, LAST_EARLY + LAST_LATE,
+    )
+    f.small[...] = f.small_1[...] + f.small_2[...]
+    f.state_back()
+    sources[LAST_GRU].start_right(0, f.gru_right)
+    halving.slot(0)
+    load.wait()
+    f.input_back()
+    sources[LAST_IMG].start_right(0, f.img_right)
+    halving.slot(1)
+    f.action_back()
+    small = SmallSum(places, f)
+    small.step(0)
+    groups = len(halving.groups)
+    for t in range(2, groups + 4):
+        halving.slot(t)
+        if t < 7:
+            small.step(t - 1)
+    halving.drain()
+
+
+class Unpack(NamedTuple):
+    heads: Any = tuple(taken(unit[-1], LANES, dtype=F32) for unit in HEAD_UNITS)
+    last: Any = tuple(taken(unit[-1], LANES, dtype=F32) for unit in LAST_UNITS)
+    small: Any = taken(SMALL_TILES, LANES, dtype=F32)
+    deter: Any = taken(ROWS, H, dtype=F32)
+    embed: Any = taken(ROWS, E, dtype=F32)
+    loss: Any = given(1, LANES, dtype=F32)
+    deter_grad: Any = given(ROWS, H, dtype=F32)
+    embed_grad: Any = given(ROWS, E, dtype=F32)
+    obs_gain: Any = given(H // 4, dtype=F32)
+    manager_in: Any = given(U // 8, H // 4, dtype=F32)
+    manager_gain: Any = given(U // 4, dtype=F32)
+    manager_out: Any = given(U // 4, dtype=F32)
+    goal_in: Any = given(GCODE // 4, U // 8, dtype=F32)
+    goal_gain: Any = given(U // 4, dtype=F32)
+    goal_out: Any = given(U // 4, H // 8, dtype=F32)
+    actor_in: Any = given(U // 8, 3 * H // 4, dtype=F32)
+    actor_gain: Any = given(U // 4, dtype=F32)
+    actor_out: Any = given(NA, U // 4, dtype=F32)
+    critic_in: Any = given(U // 8, 3 * H // 4, dtype=F32)
+    critic_gain: Any = given(U // 4, dtype=F32)
+    critic_out: Any = given(U // 4, dtype=F32)
+    img_stoch: Any = given(Z // 4, H // 8, dtype=F32)
+    img_action: Any = given(NA, H // 4, dtype=F32)
+    img_gain: Any = given(H // 4, dtype=F32)
+    gru_weight: Any = given(H // 2, 3 * H // 8, dtype=F32)
+    gru_gain: Any = given(3 * H // 4, dtype=F32)
+    post_in: Any = given((H + E) // 4, H // 8, dtype=F32)
+    post_gain: Any = given(H // 4, dtype=F32)
+    post_out: Any = given(H // 4, Z // 8, dtype=F32)
+    prior_in: Any = given(H // 4, H // 8, dtype=F32)
+    prior_gain: Any = given(H // 4, dtype=F32)
+    prior_out: Any = given(H // 4, Z // 8, dtype=F32)
+    enc_in: Any = given(U // 8, H // 4, dtype=F32)
+    enc_gain: Any = given(U // 4, dtype=F32)
+    enc_out: Any = given(GCODE, U // 4, dtype=F32)
+
+
+def unpack_kernel(f):
+    f.loss[...] = f.small[LOSS : LOSS + 1, :]
+    f.deter_grad[...] = f.deter[...]
+    f.embed_grad[...] = f.embed[...]
+    for low, vector in (
+        (OBS, f.obs_gain), (MAN_G, f.manager_gain), (MAN_O, f.manager_out),
+        (GOAL_G, f.goal_gain), (ACT_G, f.actor_gain), (CRI_G, f.critic_gain),
+        (CRI_O, f.critic_out), (IMG_G, f.img_gain), (GRU_G, f.gru_gain), (POST_G, f.post_gain),
+        (PRIOR_G, f.prior_gain), (ENC_G, f.enc_gain),
+    ):
+        for i in range(vector.shape[0] // LANES):
+            vector[pl.ds(i * LANES, LANES)] = f.small[low + i, :]
+    f.actor_out[...] = f.small[ACT_T : ACT_T + NA, :]
+    f.enc_out[...] = f.small[ENC_T : ENC_T + GCODE, :]
+    for i in range(2):
+        f.img_action[:, i * LANES : (i + 1) * LANES] = f.small[
+            IMG_T + 24 * i : IMG_T + 24 * i + NA, :
+        ]
+
+    def halves(value, rows, first, second):
+        for low in range(0, value.shape[0], LANES):
+            turned = value[low : low + LANES, :].T
+            places = slice(rows.start + low, rows.start + low + LANES)
+            first[:, places] = turned[0:64]
+            second[:, places] = turned[64:LANES]
+
+    whole = {
+        HEAD_POST: f.post_in, HEAD_PRIOR: f.prior_in, HEAD_POST_OUT: f.post_out,
+        HEAD_PRIOR_OUT: f.prior_out,
+    }
+    for unit, value in zip(HEAD_UNITS, f.heads):
+        rows = slice(unit[4], unit[4] + unit[5])
+        if unit[0] == HEAD_MAN_ENC:
+            halves(value, rows, f.manager_in, f.enc_in)
+        else:
+            whole[unit[0]][rows, :] = value[...]
+    whole = {LAST_GOAL_OUT: f.goal_out, LAST_IMG: f.img_stoch}
+    for unit, value in zip(LAST_UNITS, f.last):
+        rows = slice(unit[4], unit[4] + unit[5])
+        if unit[0] == LAST_WORKER:
+            halves(value, rows, f.actor_in, f.critic_in)
+        elif unit[0] == LAST_GOAL_IN:
+            f.goal_in[...] = value[:, 0:64]
+        elif unit[0] == LAST_GRU:
+            f.gru_weight[rows, unit[2] : unit[2] + LANES] = value[...]
+        else:
+            whole[unit[0]][rows, :] = value[...]
 
 
 class Weights(NamedTuple):
@@ -1596,108 +1919,57 @@
     actions: Any
 
 
-def vectors_in_order(w):
-    return (
-        w.obs_gain, w.manager_gain, w.manager_out, w.goal_gain, w.actor_gain, w.critic_gain,
-        w.critic_out, w.img_gain, w.gru_gain, w.post_gain, w.prior_gain, w.enc_gain,
-    )
-
-
 def step_in_kernels(data, w):
-    positions = lax.broadcasted_iota(jnp.int32, (SEQ_DEV, LEN), 1)
-    is_valid = positions < data.lengths[:, None]
-    next_valid = jnp.concatenate([is_valid[:, 1:], jnp.zeros((SEQ_DEV, 1), jnp.bool_)], 1)
-    next_reset = jnp.concatenate([data.resets[:, 1:], jnp.ones((SEQ_DEV, 1), jnp.int32)], 1)
-    columns = (
-        data.prev_action, is_valid, next_valid & (next_reset == 0), 1 - data.terminal,
-        data.rewards, data.regroup,
-    )
-    meta = jnp.concatenate(
-        [data.prev_stoch.reshape(ROWS, ZG).astype(F32)]
-        + [value.reshape(ROWS, 1).astype(F32) for value in columns]
-        + [jnp.zeros((ROWS, LANES - ZG - 6), F32)],
-        1,
-    )
-    slot_meta = jnp.concatenate(
-        [
-            data.goal_codes.astype(F32), jnp.zeros((ROWS, 32 - GC), F32),
-            data.actions.astype(F32), jnp.zeros((ROWS, LANES - 32 - HOR), F32),
-        ],
-        1,
-    )
-    samples = data.samples.transpose(1, 0, 2).astype(F32)
-    vectors = jnp.concatenate([v.astype(F32).reshape(-1, LANES) for v in vectors_in_order(w)], 0)
-    vectors = jnp.pad(vectors, ((0, VECTOR_TILES - vectors.shape[0]), (0, 0)))
-    tables = jnp.concatenate(
-        [
-            jnp.pad(w.actor_out.T, ((0, 32 - NA), (0, 0))),
-            w.enc_out.T,
-            jnp.pad(w.img_action[:, :LANES], ((0, 32 - NA), (0, 0))),
-            jnp.pad(w.img_action[:, LANES:], ((0, 32 - NA), (0, 0))),
-        ]
-        + [w.goal_in[:, i * LANES : (i + 1) * LANES] for i in range(4)],
-        0,
-    )
     prev = data.deter_states.reshape(ROWS, H)
     f = run_kernel(
         frames_kernel, Frames(),
         (
-            meta, prev, data.embed.reshape(ROWS, E), vectors, tables, w.img_stoch, w.gru_weight,
-            w.manager_in, w.enc_in, w.goal_out, w.prior_in, w.post_in, w.prior_out, w.post_out,
-            w.actor_in, w.critic_in,
+            data.lengths, data.resets, data.terminal, data.rewards,
+            data.prev_stoch.transpose(0, 2, 1), data.prev_action, data.regroup, prev,
+            data.embed.reshape(ROWS, E), w.obs_gain, w.manager_gain, w.manager_out, w.goal_gain,
+            w.actor_gain, w.critic_gain, w.critic_out, w.img_gain, w.gru_gain, w.post_gain,
+            w.prior_gain, w.enc_gain, w.actor_out.T, w.enc_out.T, w.img_action, w.goal_in,
+            w.img_stoch, w.gru_weight, w.manager_in, w.enc_in, w.goal_out, w.prior_in, w.post_in,
+            w.prior_out, w.post_out, w.actor_in, w.critic_in,
         ),
         "frames", 0,
     )
     s = run_kernel(
         worker_kernel, Worker(),
         (
-            slot_meta, samples, f.vectors, f.tables, f.start_state, f.goal_out_out,
-            f.actor_in_out, f.critic_in_out,
+            data.goal_codes.T, data.actions.T, data.samples.transpose(1, 2, 0), f.vectors,
+            f.tables, f.start_state, f.goal_out_out, f.actor_in_out, f.critic_in_out, f.post_left,
+            f.post_out_left, f.prior_out_left, f.me_left, f.post_right, f.prior_right,
+            f.post_out_right, f.prior_out_right, f.me_right,
         ),
         "worker", 1,
     )
     b = run_kernel(
-        back_kernel, Back(),
+        last_kernel, Last(),
         (
-            meta, prev, f.vectors, f.gru_weight_out, s.returned, f.grad_deter, f.gru_normed,
-            f.gru_inverse, f.img_normed, f.img_inverse, f.small, s.small,
+            f.meta_turned, prev, f.vectors, s.returned, f.grad_deter, f.gru_normed, f.gru_inverse,
+            f.img_normed, f.img_inverse, f.small, s.small, f.gru_weight_out, s.worker_left,
+            s.goal_left, f.dec_left, s.code_turned, f.soft_turned, f.gru_left, f.img_left,
+            s.goal_right, f.recon_low, s.goal_pair, f.dec_pair,
         ),
-        "back",
-    )
-    large, small = reduce_call(
-        (
-            f.gru_left, f.post_left, f.post_left, f.post_out_left, f.prior_out_left, f.img_left,
-            f.me_left, s.goal_left, f.dec_left, s.code_turned, f.soft_turned,
-        ),
-        (
-            b.gru_right, f.post_right, f.prior_right, f.post_out_right, f.prior_out_right,
-            b.img_right, f.me_right, s.goal_right, f.recon_low, s.goal_pair, f.dec_pair,
-        ),
-        s.worker_left, b.small,
-    )
-
-    def vector(low, tiles):
-        return small[low : low + tiles].reshape(-1)
-
-    man_enc, worker = (large[MAN_ENC][0], large[WORKER][0])
-    out = Weights(
-        obs_gain=vector(OBS, 2), manager_gain=vector(MAN_G, 1), manager_out=vector(MAN_O, 1),
-        goal_gain=vector(GOAL_G, 1), actor_gain=vector(ACT_G, 1), critic_gain=vector(CRI_G, 1),
-        critic_out=vector(CRI_O, 1), img_gain=vector(IMG_G, 2), gru_gain=vector(GRU_G, 6),
-        post_gain=vector(POST_G, 2), prior_gain=vector(PRIOR_G, 2), enc_gain=vector(ENC_G, 1),
-        actor_out=small[ACT_T : ACT_T + NA].T, enc_out=small[ENC_T : ENC_T + GCODE].T,
-        img_action=jnp.concatenate(
-            [small[IMG_T : IMG_T + NA], small[IMG_T + 24 : IMG_T + 24 + NA]], 1
-        ),
-        manager_in=man_enc[:, :64], enc_in=man_enc[:, 64:],
-        actor_in=worker[:, :64], critic_in=worker[:, 64:],
-        goal_in=large[GOAL_IN][0][:, :64], goal_out=large[GOAL_OUT][0],
-        img_stoch=large[IMG][0], gru_weight=jnp.concatenate(large[GRU], 1),
-        post_in=large[POST][0], post_out=large[POST_OUT][0],
-        prior_in=large[PRIOR][0], prior_out=large[PRIOR_OUT][0],
-    )
-    deter_grad = b.deter_grad.reshape(SEQ_DEV, LEN, H)
-    return (small[LOSS, 0], deter_grad, f.embed_grad.reshape(SEQ_DEV, LEN, E)) + tuple(out)
+        "last", 2,
+    )
+    u = run_kernel(
+        unpack_kernel, Unpack(),
+        tuple(s.sums) + tuple(b.sums) + (b.small_sum, b.deter_grad, f.embed_grad),
+        "unpack",
+    )
+    first = len(Unpack._fields) - len(Weights._fields)
+    grads = Weights(*tuple(u)[first:])
+    grads = grads._replace(
+        manager_in=grads.manager_in.T, actor_in=grads.actor_in.T, critic_in=grads.critic_in.T,
+        enc_in=grads.enc_in.T, actor_out=grads.actor_out.T, enc_out=grads.enc_out.T,
+    )
+    return (
+        u.loss[0, 0],
+        u.deter_grad.reshape(SEQ_DEV, LEN, H),
+        u.embed_grad.reshape(SEQ_DEV, LEN, E),
+    ) + tuple(grads)
 
 
 DP, REP = ("dp", "rep")

time: 438 us -> 322 us (0.74)
  Pallas kernels: 396 us -> 321 us
  local copies, waits for them, and re-layouts: 29.9 us -> 0 us
  other arithmetic: 9.9 us -> 0 us
    pallas_call x1 -> x0, Pallas kernels: 187 us -> none  [reduce_call(): pl.pallas_call(reduce_kernel, out_shape=[jax.ShapeDtypeStruct((unit_rows(...]
    pallas_call x3 -> x4, Pallas kernels: 210 us -> 321 us  [run_kernel(): pl.pallas_call(kernel, out_shape=[jax.ShapeDtypeStruct(a.shape, a.dtype)...]
    unnamed x39 -> x0, local copies, waits for them, and re-layouts: 12.1 us -> none
    slice x7 -> x0, local copies, waits for them, and re-layouts: 5.41 us -> none  [the longest x1 1.34 us: step_in_kernels(): small[IMG_T:IMG_T + NA]]
    convert_element_type x8 -> x0, other arithmetic: 5.15 us -> none  [the longest x4 2.03 us: step_in_kernels(): value.reshape(ROWS, 1).astype(F32)]
    reshape x4 -> x0, local copies, waits for them, and re-layouts: 4.86 us -> none  [the longest x3 4.04 us: vector(): return small[low:low + tiles].reshape(-1)]
where the time goes in v2:
time: 322 us
  Pallas kernels  321 us (100%)
    pallas_call x4, Pallas kernels, run_kernel(): pl.pallas_call(kernel, out_shape=[jax.ShapeDtypeStruct(a.shape, a.dtype)...  321 us

profile of v2, /device:TPU:0, one launch (start us, length us, event | category | flops | bytes accessed | tf_op | source)
XLA Modules:
  0.0 322.3 jit_solution(9089335917454651317)
XLA Ops:
  0.7 119.4 %frames.1 = (bf16[2048,3072]{1,0:T(8,128)(2,1)}, bf16[512,1024]{1,0:T(8,128)(2,1)}, bf16[3072,512]{1,0:T(8,128)(2,1)}, bf16[3072,512]{1,0:T(8,128)(2,1)}, f32[4,...) custom-call(s32[2]{0:T(128)} %refs_0_.1, ...), custom_call_target="tpu_custom_call" | custom-call | tf_op jit(solution)/shard_map/frames/pallas_call | solution.py:78
  120.1 92.8 %worker.1 = (bf16[3072,1024]{1,0:T(8,128)(2,1)}, bf16[128,1024]{1,0:T(8,128)(2,1)}, bf16[512,128]{1,0:T(8,128)(2,1)}, bf16[64,128]{1,0:T(8,128)(2,1)}, bf16[128,...) custom-call(s32[8,128]{1,0:T(8,128)} %bitcast.26, ...), custom_call_target="tpu_custom_call" | custom-call | tf_op jit(solution)/shard_map/worker/pallas_call | solution.py:78
  212.9 105.0 %last.1 = (f32[128,1024]{1,0:T(8,128)}, f32[160,128]{1,0:T(8,128)}, f32[256,128]{1,0:T(8,128)}, f32[256,128]{1,0:T(8,128)}, f32[256,128]{1,0:T(8,128)}, /*index=...) custom-call(f32[128,128]{1,0:T(8,128)} %get-tuple-element.147.refs_0, ...), custom_call_target="tpu_custom_call" | custom-call | tf_op jit(solution)/shard_map/last/pallas_call | solution.py:78
  317.9 4.2 %unpack.1 = (f32[1,128]{1,0:T(1,128)}, f32[128,1024]{1,0:T(8,128)}, f32[128,1536]{1,0:T(8,128)}, f32[256]{0:T(256)}, f32[64,256]{1,0:T(8,128)}, /*index=5*/f32[1...) custom-call(f32[128,128]{1,0:T(8,128)} %get-tuple-element.138.refs_0, ...), custom_call_target="tpu_custom_call" | custom-call | tf_op jit(solution)/shard_map/unpack/pallas_call | solution.py:78
